TPU v7x, 32 devices: a whole 2x2x4 slice. The times are simulated.
32 devices in a mesh: dp: 4 (over z), ctx: 8 (over y, x, core).
Axes of the slice: x: 2, y: 2, z: 4, core: 2. Of those that a mesh axis runs over, the one named last changes fastest.
Arguments:
- q_proj: bfloat16 [4, 1024, 4096], P('dp', 'ctx'), may hold values from -6 to 6
- k_proj: bfloat16 [4, 1024, 4096], P('dp', 'ctx'), may hold values from -6 to 6
- v_proj: bfloat16 [4, 1024, 4096], P('dp', 'ctx'), may hold values from -6 to 6
- out_grad: bfloat16 [4, 1024, 4096], P('dp', 'ctx'), may hold values from -6 to 6
- residue: float32 [16, 4096], replicated, may hold values from -1.5 to 1.5
- pole_decay: float32 [16, 4096], replicated, may hold values from 0.00390625 to 1024
- group_doc: int32 [4, 8], P('dp'), may hold values from 0 to 1, never falling along the last dimension, each value on 1 to 5 neighbouring positions
Outputs:
- mixed: bfloat16 [4, 1024, 4096], P('dp', 'ctx')
- q_grad: bfloat16 [4, 1024, 4096], P('dp', 'ctx')
- k_grad: bfloat16 [4, 1024, 4096], P('dp', 'ctx')
- v_grad: bfloat16 [4, 1024, 4096], P('dp', 'ctx')
- residue_grad: float32 [16, 4096], replicated
- pole_grad: float32 [16, 4096], replicated
Inputs may be any that keep to these rules, and one draw needn't show every extreme that they name: group_doc[r, j] numbers the packed sequence that holds block j of row r (tokens j * 128 to (j + 1) * 128 - 1); it never falls along a row, every number appears, each sequence covers 1 to 5 consecutive blocks.
All inputs are finite; a program needn't handle non-finite values.
Results may differ from a plain program's by a relative error of at most 0.001.
Values sent between devices are 32-bit elements; how exact they have to be, the bound alone decides.
No kernel may reach another device: no remote copies, remote signals or barrier semaphores. Data moves between devices by JAX's collectives and lax.ppermute only.
A program may use at most 128 MiB of HBM per device.

v0:
```python
from functools import partial
import math

import jax
import jax.numpy as jnp
from jax import lax
from jax.experimental import pallas as pl
from jax.experimental.pallas import tpu as pltpu
from jax.sharding import PartitionSpec as P

F32 = jnp.float32
LANES = 128
SUBS = 8
GROUP = LANES * SUBS
CHUNK = 8
VMEM_BYTES = 48 * 1024 * 1024


def to_rows(left_ref, right_ref, rows_ref):
    tokens = left_ref.shape[0]
    for pair in range(tokens // 16):
        window = pl.ds(pair * 16, 16)
        for tile in range(SUBS):
            lanes = pl.ds(tile * LANES, LANES)
            product = left_ref[window, lanes].astype(F32) * right_ref[window, lanes].astype(F32)
            for part in range(2):
                start = (pair * 2 + part) * 64 + tile * 8
                rows_ref[pl.ds(start, 8), :] = product[part * 8 : part * 8 + 8]


def token_row(rows_ref, chunk, token):
    return rows_ref[pl.ds(chunk * 64 + token, 8, stride=8), :]


def stats_kernel(
    row_len, k_ref, v_ref, q_ref, g_ref, pole_ref, c_ref, b_ref, st_ref,
    u_rows, d_rows, lam_s, jump_s, slope_s, state_s, lag_s, res_s, mixl_s, head_s, headl_s, headm_s, pow_s, corr_s,
):
    modes = pole_ref.shape[0]
    chunks = k_ref.shape[0] // CHUNK
    to_rows(k_ref, v_ref, u_rows)
    to_rows(g_ref, q_ref, d_rows)
    zero = jnp.zeros((SUBS, LANES), F32)
    for m in range(modes):
        rate = pole_ref[m] / row_len
        lam_s[m] = jnp.exp(-rate)
        jump_s[m] = jnp.exp(-CHUNK * rate)
        slope_s[m] = CHUNK * jnp.exp(-(CHUNK - 1) * rate)
        for ref in (state_s, lag_s, res_s, mixl_s, head_s, headl_s, headm_s):
            ref[m] = zero
        pow_s[m] = zero + 1.0
    for lag in range(CHUNK):
        corr_s[lag] = zero

    def step(chunk, _):
        u = [token_row(u_rows, chunk, t) for t in range(CHUNK)]
        d = [token_row(d_rows, chunk, t) for t in range(CHUNK)]
        for lag in range(CHUNK):
            total = corr_s[lag]
            for t in range(CHUNK - lag):
                total = total + d[t + lag] * u[t]
            corr_s[lag] = total
        offset = (chunk * CHUNK).astype(F32)
        for m in range(modes):
            lam = lam_s[m]
            end, endl = u[0], None
            for t in range(1, CHUNK):
                endl = end if endl is None else endl * lam + end
                end = end * lam + u[t]
            head, headl = d[CHUNK - 1], None
            for t in range(CHUNK - 2, -1, -1):
                headl = head if headl is None else headl * lam + head
                head = head * lam + d[t]
            c_ref[chunk, m] = end
            b_ref[chunk, m] = head
            state, lag_state = state_s[m], lag_s[m]
            res_s[m] = res_s[m] + head * state
            mixl_s[m] = mixl_s[m] + (headl * state + head * lag_state)
            jump = jump_s[m]
            lag_s[m] = lag_state * jump + (state * slope_s[m] + endl)
            state_s[m] = state * jump + end
            power = pow_s[m]
            far = power * head
            head_s[m] = head_s[m] + far
            headl_s[m] = headl_s[m] + power * headl
            headm_s[m] = headm_s[m] + offset * far
            pow_s[m] = power * jump
        return 0

    lax.fori_loop(0, chunks, step, 0)
    for m in range(modes):
        lam = lam_s[m]
        st_ref[0, m] = state_s[m]
        st_ref[1, m] = lam * lag_s[m]
        st_ref[2, m] = head_s[m]
        st_ref[3, m] = lam * headl_s[m] + headm_s[m]
        near, nearl = corr_s[CHUNK - 1], None
        for lag in range(CHUNK - 2, -1, -1):
            nearl = near if nearl is None else nearl * lam + near
            near = near * lam + corr_s[lag]
        res = res_s[m]
        st_ref[4, m] = near + lam * res
        st_ref[5, m] = lam * (nearl + (res + lam * mixl_s[m]))


def output_kernel(
    row_len, core_ref, k_ref, v_ref, q_ref, g_ref, pole_ref, residue_ref, c_ref, b_ref, kept_ref, got_ref,
    mixed_ref, qg_ref, kg_ref, vg_ref,
    u_rows, d_rows, z_rows, w_rows, lam_s, jump_s, lead_s, state_s, back_s, tap_s,
):
    modes = pole_ref.shape[0]
    half = modes // 2
    chunks = k_ref.shape[0] // CHUNK
    first = core_ref[0] == 0
    to_rows(k_ref, v_ref, u_rows)
    to_rows(g_ref, q_ref, d_rows)
    taps = [jnp.zeros((SUBS, LANES), F32) for _ in range(CHUNK)]
    for m in range(modes):
        rate = pole_ref[m] / row_len
        lam = jnp.exp(-rate)
        lam_s[m] = lam
        jump_s[m] = jnp.exp(-CHUNK * rate)
        power = residue_ref[m] * jnp.sqrt(2.0 * rate)
        lead_s[m] = power * lam
        for lag in range(CHUNK):
            taps[lag] = taps[lag] + power
            power = power * lam
        mine = first if m < half else jnp.logical_not(first)
        state_s[m] = jnp.where(mine, kept_ref[0, m % half], got_ref[0, m % half])
        back_s[m] = jnp.where(mine, kept_ref[1, m % half], got_ref[1, m % half])
    for lag in range(CHUNK):
        tap_s[lag] = taps[lag]

    def ahead(chunk, _):
        u = [token_row(u_rows, chunk, t) for t in range(CHUNK)]
        z = [None] * CHUNK
        for lag in range(CHUNK):
            tap = tap_s[lag]
            for t in range(lag, CHUNK):
                term = tap * u[t - lag]
                z[t] = term if z[t] is None else z[t] + term
        for m in range(modes):
            lam = lam_s[m]
            state = state_s[m]
            term = state * lead_s[m]
            for t in range(CHUNK):
                z[t] = z[t] + term
                if t + 1 < CHUNK:
                    term = term * lam
            state_s[m] = state * jump_s[m] + c_ref[chunk, m]
        for t in range(CHUNK):
            z_rows[pl.ds(chunk * 64 + t, 8, stride=8), :] = z[t]
        return 0

    def behind(index, _):
        chunk = chunks - 1 - index
        d = [token_row(d_rows, chunk, t) for t in range(CHUNK)]
        w = [None] * CHUNK
        for lag in range(CHUNK):
            tap = tap_s[lag]
            for t in range(CHUNK - lag):
                term = tap * d[t + lag]
                w[t] = term if w[t] is None else w[t] + term
        for m in range(modes):
            lam = lam_s[m]
            back = back_s[m]
            term = back * lead_s[m]
            for t in range(CHUNK - 1, -1, -1):
                w[t] = w[t] + term
                if t > 0:
                    term = term * lam
            back_s[m] = back * jump_s[m] + b_ref[chunk, m]
        for t in range(CHUNK):
            w_rows[pl.ds(chunk * 64 + t, 8, stride=8), :] = w[t]
        return 0

    lax.fori_loop(0, chunks, ahead, 0)
    lax.fori_loop(0, chunks, behind, 0)
    for pair in range(chunks // 2):
        window = pl.ds(pair * 16, 16)
        for tile in range(SUBS):
            lanes = pl.ds(tile * LANES, LANES)
            z = jnp.concatenate([z_rows[pl.ds((pair * 2 + part) * 64 + tile * 8, 8), :] for part in range(2)], axis=0)
            w = jnp.concatenate([w_rows[pl.ds((pair * 2 + part) * 64 + tile * 8, 8), :] for part in range(2)], axis=0)
            mixed_ref[window, lanes] = (q_ref[window, lanes].astype(F32) * z).astype(jnp.bfloat16)
            qg_ref[window, lanes] = (g_ref[window, lanes].astype(F32) * z).astype(jnp.bfloat16)
            kg_ref[window, lanes] = (w * v_ref[window, lanes].astype(F32)).astype(jnp.bfloat16)
            vg_ref[window, lanes] = (w * k_ref[window, lanes].astype(F32)).astype(jnp.bfloat16)


def merge_kernel(row_len, block, info_ref, kept_ref, got_ref, pole_ref, chip_ref):
    first = info_ref[0] == 0
    joined = (info_ref[2] == info_ref[3]).astype(F32)
    rate = pole_ref[...] / row_len
    lam = jnp.exp(-rate)
    hop = joined * jnp.exp(-block * rate)
    link = joined * lam
    left = [jnp.where(first, kept_ref[i], got_ref[i]) for i in range(6)]
    right = [jnp.where(first, got_ref[i], kept_ref[i]) for i in range(6)]
    chip_ref[0] = right[0] + hop * left[0]
    chip_ref[1] = right[1] + hop * (left[1] + block * left[0])
    chip_ref[2] = left[2] + hop * right[2]
    chip_ref[3] = left[3] + hop * (right[3] + block * right[2])
    chip_ref[4] = left[4] + right[4] + link * (right[2] * left[0])
    chip_ref[5] = left[5] + right[5] + link * ((right[3] + right[2]) * left[0] + right[2] * left[1])


def scan_kernel(row_len, block, chips, info_ref, doc_ref, pole_ref, *refs):
    ins, outs, total_ref = refs[:chips], refs[chips : 2 * chips], refs[2 * chips]
    ordered, ends = refs[2 * chips + 1], refs[2 * chips + 2]
    chip = info_ref[1]
    for away in range(chips):
        ordered[chip ^ away] = ins[away][...]
    rate = pole_ref[...] / row_len
    lam = jnp.exp(-rate)
    span = 2.0 * block
    hop = jnp.exp(-span * rate)
    zero = jnp.zeros_like(rate)
    state, lag_state, res, grad_lag = zero, zero, zero, zero
    for j in range(chips):
        ends[j, 0] = state
        res = res + (ordered[j, 4] + lam * (ordered[j, 2] * state))
        grad_lag = grad_lag + (
            ordered[j, 5]
            + lam * ((ordered[j, 3] + ordered[j, 2]) * state + ordered[j, 2] * lag_state)
        )
        if j + 1 < chips:
            through = (doc_ref[0, 2 * j] == doc_ref[0, 2 * j + 1]).astype(F32) * hop
            keep = (doc_ref[0, 2 * j + 1] == doc_ref[0, 2 * j + 2]).astype(F32)
            lag_state = keep * (ordered[j, 1] + through * (lag_state + span * state))
            state = keep * (ordered[j, 0] + through * state)
    back = zero
    for j in range(chips - 1, -1, -1):
        ends[j, 1] = back
        if j > 0:
            through = (doc_ref[0, 2 * j] == doc_ref[0, 2 * j + 1]).astype(F32) * hop
            keep = (doc_ref[0, 2 * j - 1] == doc_ref[0, 2 * j]).astype(F32)
            back = keep * (ordered[j, 2] + through * back)
    for away in range(chips):
        outs[away][...] = ends[chip ^ away]
    total_ref[0] = res
    total_ref[1] = grad_lag


def expand_kernel(row_len, block, chips, info_ref, pole_ref, kept_ref, got_ref, *refs):
    ins, mine_ref, send_ref, whole = refs[:chips], refs[chips], refs[chips + 1], refs[chips + 2]
    first = info_ref[0] == 0
    chip = info_ref[1]
    joined = (info_ref[2] == info_ref[3]).astype(F32)
    part = ins[0].shape[1]
    for away in range(chips):
        start = pl.multiple_of((chip ^ away) * part, part)
        whole[:, pl.ds(start, part), :] = ins[away][...]
    hop = joined * jnp.exp(-block * (pole_ref[...] / row_len))
    end_left = jnp.where(first, kept_ref[0], got_ref[0])
    head_right = jnp.where(first, got_ref[2], kept_ref[2])
    state, back = whole[0], whole[1]
    state_right = joined * end_left + hop * state
    back_left = joined * head_right + hop * back
    mine_ref[0] = jnp.where(first, state, state_right)
    mine_ref[1] = jnp.where(first, back_left, back)
    send_ref[0] = jnp.where(first, state_right, state)
    send_ref[1] = jnp.where(first, back, back_left)


def gather_kernel(chips, info_ref, *refs):
    ins, out_ref = refs[:chips], refs[chips]
    chip = info_ref[1]
    part = ins[0].shape[1]
    for away in range(chips):
        start = pl.multiple_of((chip ^ away) * part, part)
        out_ref[:, pl.ds(start, part), :] = ins[away][...]


def final_kernel(row_len, scale, info_ref, pole_ref, residue_ref, kept_ref, got_ref, res_ref, grad_ref):
    first = info_ref[0] == 0
    half = kept_ref.shape[1]
    for part in range(2):
        mine = first if part == 0 else jnp.logical_not(first)
        rows = pl.ds(part * half, half)
        grad_res = jnp.where(mine, kept_ref[0], got_ref[0])
        grad_lag = jnp.where(mine, kept_ref[1], got_ref[1])
        rate = pole_ref[rows, :] / row_len
        root = jnp.sqrt(2.0 * rate)
        res_ref[rows, :] = root * grad_res * scale
        grad_ref[rows, :] = residue_ref[rows, :] * root * (0.5 * grad_res - rate * grad_lag) * scale


def whole_spec():
    return pl.BlockSpec(memory_space=pltpu.VMEM)


def scalar_spec():
    return pl.BlockSpec(memory_space=pltpu.SMEM)


def params():
    return pltpu.CompilerParams(vmem_limit_bytes=VMEM_BYTES)


def body(q_proj, k_proj, v_proj, out_grad, residue, pole_decay, group_doc):
    block, channels = q_proj.shape[1], q_proj.shape[2]
    modes = residue.shape[0]
    n_ctx, n_dp = lax.axis_size("ctx"), lax.axis_size("dp")
    row_len = block * n_ctx
    total_tokens = row_len * n_dp
    chips = n_ctx // 2
    groups = channels // GROUP
    chunks = block // CHUNK
    tall = channels // LANES
    rows = modes * tall
    half = rows // 2
    part = half // chips

    me = lax.axis_index("ctx").astype(jnp.int32)
    core, chip = me % 2, me // 2
    docs = lax.dynamic_slice(group_doc, (0, chip * 2), (1, 2))
    info = jnp.stack([core, chip, docs[0, 0], docs[0, 1]]).astype(jnp.int32)
    pole = pole_decay.reshape(modes, tall, LANES)
    resid = residue.reshape(modes, tall, LANES)
    pole_rows, resid_rows = pole.reshape(rows, LANES), resid.reshape(rows, LANES)

    k_in, v_in, q_in, g_in = (x.reshape(block, channels) for x in (k_proj, v_proj, q_proj, out_grad))
    wide = pl.BlockSpec((block, GROUP), lambda i: (0, i))
    slim = pl.BlockSpec((modes, SUBS, LANES), lambda i: (0, i, 0))
    chunked = pl.BlockSpec((chunks, modes, SUBS, LANES), lambda i: (0, 0, i, 0))
    row_scratch = pltpu.VMEM((block * SUBS, LANES), F32)
    mode_scratch = pltpu.VMEM((modes, SUBS, LANES), F32)
    tap_scratch = pltpu.VMEM((CHUNK, SUBS, LANES), F32)

    ends, heads, stats = pl.pallas_call(
        partial(stats_kernel, float(row_len)),
        grid=(groups,),
        in_specs=[wide] * 4 + [slim],
        out_specs=[chunked, chunked, pl.BlockSpec((6, modes, SUBS, LANES), lambda i: (0, 0, i, 0))],
        out_shape=[
            jax.ShapeDtypeStruct((chunks, modes, tall, LANES), F32),
            jax.ShapeDtypeStruct((chunks, modes, tall, LANES), F32),
            jax.ShapeDtypeStruct((6, modes, tall, LANES), F32),
        ],
        scratch_shapes=[row_scratch] * 2 + [mode_scratch] * 11 + [tap_scratch],
        compiler_params=params(),
        name="block_stats",
    )(k_in, v_in, q_in, g_in, pole)

    stats = stats.reshape(6, rows, LANES)

    def swap_core(x):
        return lax.ppermute(x, "ctx", [(i, i ^ 1) for i in range(n_ctx)])

    def swap_chip(x, away):
        return lax.ppermute(x, "ctx", [(i, i ^ (2 * away)) for i in range(n_ctx)])

    kept = lax.dynamic_slice(stats, (0, core * half, 0), (6, half, LANES))
    got = swap_core(lax.dynamic_slice(stats, (0, (1 - core) * half, 0), (6, half, LANES)))
    pole_half = lax.dynamic_slice(pole_rows, (core * half, 0), (half, LANES))
    merged = pl.pallas_call(
        partial(merge_kernel, float(row_len), float(block)),
        in_specs=[scalar_spec()] + [whole_spec()] * 3,
        out_specs=whole_spec(),
        out_shape=jax.ShapeDtypeStruct((6, half, LANES), F32),
        compiler_params=params(),
        name="chip_stats",
    )(info, kept, got, pole_half)

    def cut(away):
        return lax.dynamic_slice(merged, (0, (chip ^ away) * part, 0), (6, part, LANES))

    pieces = [cut(0)] + [swap_chip(cut(away), away) for away in range(1, chips)]
    pole_part = lax.dynamic_slice(pole_half, (chip * part, 0), (part, LANES))
    scanned = pl.pallas_call(
        partial(scan_kernel, float(row_len), float(block), chips),
        in_specs=[scalar_spec(), scalar_spec()] + [whole_spec()] * (1 + chips),
        out_specs=[whole_spec()] * (chips + 1),
        out_shape=[jax.ShapeDtypeStruct((2, part, LANES), F32)] * (chips + 1),
        scratch_shapes=[pltpu.VMEM((chips, 6, part, LANES), F32), pltpu.VMEM((chips, 2, part, LANES), F32)],
        compiler_params=params(),
        name="row_scan",
    )(info, group_doc, pole_part, *pieces)

    edges = [scanned[0]] + [swap_chip(scanned[away], away) for away in range(1, chips)]
    mine, send = pl.pallas_call(
        partial(expand_kernel, float(row_len), float(block), chips),
        in_specs=[scalar_spec()] + [whole_spec()] * (3 + chips),
        out_specs=[whole_spec()] * 2,
        out_shape=[jax.ShapeDtypeStruct((2, half, LANES), F32)] * 2,
        scratch_shapes=[pltpu.VMEM((2, half, LANES), F32)],
        compiler_params=params(),
        name="block_edges",
    )(info, pole_half, kept, got, *edges)
    theirs = swap_core(send)

    total = scanned[chips]
    reach = 1
    while reach < n_dp:
        total = total + lax.ppermute(total, "dp", [(i, i ^ reach) for i in range(n_dp)])
        reach *= 2
    sums = [total] + [swap_chip(total, away) for away in range(1, chips)]
    gathered = pl.pallas_call(
        partial(gather_kernel, chips),
        in_specs=[scalar_spec()] + [whole_spec()] * chips,
        out_specs=whole_spec(),
        out_shape=jax.ShapeDtypeStruct((2, half, LANES), F32),
        compiler_params=params(),
        name="gather_sums",
    )(info, *sums)
    other = swap_core(gathered)

    halves = modes // 2
    edge_spec = pl.BlockSpec((2, halves, SUBS, LANES), lambda i: (0, 0, i, 0))
    outs = pl.pallas_call(
        partial(output_kernel, float(row_len)),
        grid=(groups,),
        in_specs=[scalar_spec()] + [wide] * 4 + [slim] * 2 + [chunked] * 2 + [edge_spec] * 2,
        out_specs=[wide] * 4,
        out_shape=[jax.ShapeDtypeStruct((block, channels), jnp.bfloat16)] * 4,
        scratch_shapes=[row_scratch] * 4 + [mode_scratch] * 5 + [tap_scratch],
        compiler_params=params(),
        cost_estimate=pl.CostEstimate(flops=60_000_000_000, bytes_accessed=20_000_000, transcendentals=0),
        name="outputs",
    )(
        info, k_in, v_in, q_in, g_in, pole, resid, ends, heads,
        mine.reshape(2, halves, tall, LANES), theirs.reshape(2, halves, tall, LANES),
    )

    residue_grad, pole_grad = pl.pallas_call(
        partial(final_kernel, float(row_len), 1.0 / math.sqrt(total_tokens)),
        in_specs=[scalar_spec()] + [whole_spec()] * 4,
        out_specs=[whole_spec()] * 2,
        out_shape=[jax.ShapeDtypeStruct((rows, LANES), F32)] * 2,
        compiler_params=params(),
        name="parameter_grads",
    )(info, pole_rows, resid_rows, gathered, other)
    return (
        *(x[None] for x in outs),
        residue_grad.reshape(modes, channels),
        pole_grad.reshape(modes, channels),
    )


def solution(mesh):
    tokens = P("dp", "ctx", None)
    return jax.shard_map(
        body,
        mesh=mesh,
        in_specs=(tokens, tokens, tokens, tokens, P(), P(), P("dp", None)),
        out_specs=(tokens, tokens, tokens, tokens, P(), P()),
        check_vma=False,
    )
```

profile of v0, /device:TPU:1, one launch (start us, length us, event | category | flops | bytes accessed | tf_op | source)
XLA Modules:
  0.0 86.6 jit_solution(17081556065089743107)
XLA Ops:
  3.0 1.2 %copy-done.2 = bf16[1,128,4096]{2,1,0:T(8,128)(2,1)S(1)} copy-done((bf16[1,128,4096]{2,1,0:T(8,128)(2,1)S(1)}, bf16[1,128,4096]{2,1,0:T(8,128)(2,1)}, u32[]{:S(2)}) %copy-start.2) | copy-done | bytes 1048600
  4.2 1.2 %copy-done.4 = bf16[1,128,4096]{2,1,0:T(8,128)(2,1)S(1)} copy-done((bf16[1,128,4096]{2,1,0:T(8,128)(2,1)S(1)}, bf16[1,128,4096]{2,1,0:T(8,128)(2,1)}, u32[]{:S(2)}) %copy-start.4) | copy-done | bytes 1048600
  5.4 1.2 %copy-done.6 = bf16[1,128,4096]{2,1,0:T(8,128)(2,1)S(1)} copy-done((bf16[1,128,4096]{2,1,0:T(8,128)(2,1)S(1)}, bf16[1,128,4096]{2,1,0:T(8,128)(2,1)}, u32[]{:S(2)}) %copy-start.6) | copy-done | bytes 1048600
  6.6 14.1 %block_stats.1 = (f32[16,16,32,128]{3,2,1,0:T(8,128)}, f32[16,16,32,128]{3,2,1,0:T(8,128)}, f32[6,16,32,128]{3,2,1,0:T(8,128)S(1)}) custom-call(bf16[128,4096]{1,0:T(8,128)(2,1)S(1)} %bitcast.20, bf16[128,4096]{1,0:T(8,128)(2,1)S(1)} %bitcast.22, bf16[128,4096]{1,0:T(8,128)(2,1)S(1)} %bitcast.24, bf16[128,4096]{1,0:T(8,128)(2,1)S(1)} %bitcast.26, ...), custom_call_target="tpu_custom_call" | custom-call | tf_op jit(solution)/shard_map/block_stats/pallas_call | solution.py:331
  21.7 1.4 %pad_add_fusion.info_ref.core_ref = s32[4]{0:T(128)S(1)} fusion(s32[1]{0:T(128)} %bitcast.3, s32[1]{0:T(128)} %bitcast.2, s32[1]{0:T(128)} %bitcast.1, s32[1]{0:T(128)} %bitcast), kind=kLoop, calls=%fused_computation.9 | loop fusion | flops 12 | bytes 32 | tf_op jit(solution)/shard_map/stack | solution.py:318
  24.8 2.6 %collective-permute-start.1 = (f32[6,64,128]{2,1,0:T(8,128)}, f32[6,64,128]{2,1,0:T(8,128)}, u32[]{:S(2)}, u32[]{:S(2)}) collective-permute-start(f32[6,64,128]{2,1,0:T(8,128)} %get-tuple-element.42), channel_id=1, source_target_pairs={{0,2},{1,3},{2,0},{3,1},{4,6},{5,7},{6,4},{7,5},{8,10},{9,11},{10,... | collective-permute-start | bytes 589832 | tf_op jit(solution)/shard_map/ppermute | solution.py:352
  27.4 1.2 %collective-permute-start.2 = (f32[6,64,128]{2,1,0:T(8,128)}, f32[6,64,128]{2,1,0:T(8,128)}, u32[]{:S(2)}, u32[]{:S(2)}) collective-permute-start(f32[6,64,128]{2,1,0:T(8,128)} %get-tuple-element.41), channel_id=1, source_target_pairs={{0,4},{1,5},{2,6},{3,7},{4,0},{5,1},{6,2},{7,3},{8,12},{9,13},{10,... | collective-permute-start | bytes 589832 | tf_op jit(solution)/shard_map/ppermute | solution.py:352
  28.7 4.2 %collective-permute-done.1.refs_1_ = f32[6,64,128]{2,1,0:T(8,128)} collective-permute-done((f32[6,64,128]{2,1,0:T(8,128)}, f32[6,64,128]{2,1,0:T(8,128)}, u32[]{:S(2)}, u32[]{:S(2)}) %collective-permute-start.1) | collective-permute-done | bytes 196640 | tf_op jit(solution)/shard_map/ppermute | solution.py:352
  32.9 4.1 %collective-permute-done.2.refs_2_ = f32[6,64,128]{2,1,0:T(8,128)} collective-permute-done((f32[6,64,128]{2,1,0:T(8,128)}, f32[6,64,128]{2,1,0:T(8,128)}, u32[]{:S(2)}, u32[]{:S(2)}) %collective-permute-start.2) | collective-permute-done | bytes 196640 | tf_op jit(solution)/shard_map/ppermute | solution.py:352
  38.2 1.3 %row_scan.1 = (f32[2,64,128]{2,1,0:T(8,128)S(1)}, f32[2,64,128]{2,1,0:T(8,128)S(1)}, f32[2,64,128]{2,1,0:T(8,128)S(1)}, f32[2,64,128]{2,1,0:T(8,128)S(1)}, f32[2,64,128]{2,1,0:T(8,128)S(1)}) custom-call(s32[4]{0:T(128)S(1)} %pad_add_fusion.info_ref.core_ref, s32[1,8]{1,0:T(1,128)S(1)} %copy-done.8, f32[64,128]{1,0:T(8,128)S(1)} %constant_dynamic-slice_fusion.4.pole_ref, ...), custom_call_target="tpu_custom_call" | custom-call | tf_op jit(solution)/shard_map/row_scan/pallas_call | solution.py:371
  39.5 1.2 %collective-permute-start.4 = (f32[2,64,128]{2,1,0:T(8,128)S(1)}, f32[2,64,128]{2,1,0:T(8,128)S(1)}, u32[]{:S(2)}, u32[]{:S(2)}) collective-permute-start(f32[2,64,128]{2,1,0:T(8,128)S(1)} %get-tuple-element.26), channel_id=1, source_target_pairs={{0,2},{1,3},{2,0},{3,1},{4,6},{5,7},{6,4},{7,5},{8,10},{9,11},{10,... | collective-permute-start | bytes 196616 | tf_op jit(solution)/shard_map/ppermute | solution.py:352
  42.7 1.5 %collective-permute-done.5.refs_2_ = f32[2,64,128]{2,1,0:T(8,128)S(1)} collective-permute-done((f32[2,64,128]{2,1,0:T(8,128)S(1)}, f32[2,64,128]{2,1,0:T(8,128)S(1)}, u32[]{:S(2)}, u32[]{:S(2)}) %collective-permute-start.5) | collective-permute-done | bytes 65568 | tf_op jit(solution)/shard_map/ppermute | solution.py:352
  44.1 1.4 %collective-permute-done.6.refs_3_ = f32[2,64,128]{2,1,0:T(8,128)S(1)} collective-permute-done((f32[2,64,128]{2,1,0:T(8,128)S(1)}, f32[2,64,128]{2,1,0:T(8,128)S(1)}, u32[]{:S(2)}, u32[]{:S(2)}) %collective-permute-start.6) | collective-permute-done | bytes 65568 | tf_op jit(solution)/shard_map/ppermute | solution.py:352
  45.5 1.4 %block_edges.1 = (f32[2,256,128]{2,1,0:T(8,128)S(1)}, f32[2,256,128]{2,1,0:T(8,128)}) custom-call(s32[4]{0:T(128)S(1)} %pad_add_fusion.info_ref.core_ref, f32[256,128]{1,0:T(8,128)S(1)} %constant_dynamic-slice_fusion.7.pole_ref, f32[6,256,128]{2,1,0:T(8,128)S(1)} %get-tuple-element.39.kept_ref, f32[6,256,128]{2,1,0:T(8,128)S(1)} %collective-permute-done.got_ref, ...), custom_call_target="tpu_custom_call" | custom-call | tf_op jit(solution)/shard_map/block_edges/pallas_call | solution.py:382
  46.9 2.3 %collective-permute-start.7 = (f32[2,256,128]{2,1,0:T(8,128)}, f32[2,256,128]{2,1,0:T(8,128)S(1)}, u32[]{:S(2)}, u32[]{:S(2)}) collective-permute-start(f32[2,256,128]{2,1,0:T(8,128)} %get-tuple-element.30), channel_id=1, source_target_pairs={{0,1},{1,0},{2,3},{3,2},{4,5},{5,4},{6,7},{7,6},{8,9},{9,8},{10,11... | collective-permute-start | bytes 786440 | tf_op jit(solution)/shard_map/ppermute | solution.py:349
  49.3 1.3 %collective-permute-start.8 = (f32[2,64,128]{2,1,0:T(8,128)S(1)}, f32[2,64,128]{2,1,0:T(8,128)S(1)}, u32[]{:S(2)}, u32[]{:S(2)}) collective-permute-start(f32[2,64,128]{2,1,0:T(8,128)S(1)} %get-tuple-element.35), channel_id=1, source_target_pairs={{0,8},{8,0},{16,24},{24,16},{1,9},{9,1},{17,25},{25,17},{2,10},{10... | collective-permute-start | bytes 196616 | tf_op jit(solution)/shard_map/ppermute | solution.py:396
  50.5 2.4 %collective-permute-done.8 = f32[2,64,128]{2,1,0:T(8,128)S(1)} collective-permute-done((f32[2,64,128]{2,1,0:T(8,128)S(1)}, f32[2,64,128]{2,1,0:T(8,128)S(1)}, u32[]{:S(2)}, u32[]{:S(2)}) %collective-permute-start.8) | collective-permute-done | bytes 65568 | tf_op jit(solution)/shard_map/ppermute | solution.py:396
  53.0 2.4 %collective-permute-start.9 = (f32[2,64,128]{2,1,0:T(8,128)S(1)}, f32[2,64,128]{2,1,0:T(8,128)S(1)}, u32[]{:S(2)}, u32[]{:S(2)}) collective-permute-start(f32[2,64,128]{2,1,0:T(8,128)S(1)} %add.44), channel_id=1, source_target_pairs={{0,16},{8,24},{16,0},{24,8},{1,17},{9,25},{17,1},{25,9},{2,18},{10... | collective-permute-start | bytes 196616 | tf_op jit(solution)/shard_map/ppermute | solution.py:396
  55.4 1.7 %collective-permute-done.9 = f32[2,64,128]{2,1,0:T(8,128)S(1)} collective-permute-done((f32[2,64,128]{2,1,0:T(8,128)S(1)}, f32[2,64,128]{2,1,0:T(8,128)S(1)}, u32[]{:S(2)}, u32[]{:S(2)}) %collective-permute-start.9) | collective-permute-done | bytes 65568 | tf_op jit(solution)/shard_map/ppermute | solution.py:396
  57.1 1.3 %collective-permute-start.10 = (f32[2,64,128]{2,1,0:T(8,128)S(1)}, f32[2,64,128]{2,1,0:T(8,128)S(1)}, u32[]{:S(2)}, u32[]{:S(2)}) collective-permute-start(f32[2,64,128]{2,1,0:T(8,128)S(1)} %add.45.refs_0_), channel_id=1, source_target_pairs={{0,2},{1,3},{2,0},{3,1},{4,6},{5,7},{6,4},{7,5},{8,10},{9,11},{10,... | collective-permute-start | bytes 196616 | tf_op jit(solution)/shard_map/ppermute | solution.py:352
  63.2 4.9 %collective-permute-start.13 = (f32[2,256,128]{2,1,0:T(8,128)S(1)}, f32[2,256,128]{2,1,0:T(8,128)S(1)}, u32[]{:S(2)}, u32[]{:S(2)}) collective-permute-start(f32[2,256,128]{2,1,0:T(8,128)S(1)} %gather_sums.1.kept_ref), channel_id=1, source_target_pairs={{0,1},{1,0},{2,3},{3,2},{4,5},{5,4},{6,7},{7,6},{8,9},{9,8},{10,11... | collective-permute-start | bytes 786440 | tf_op jit(solution)/shard_map/ppermute | solution.py:349
  68.1 1.2 %copy-done.3 = bf16[1,128,4096]{2,1,0:T(8,128)(2,1)S(1)} copy-done((bf16[1,128,4096]{2,1,0:T(8,128)(2,1)S(1)}, bf16[1,128,4096]{2,1,0:T(8,128)(2,1)}, u32[]{:S(2)}) %copy-start.3) | copy-done | bytes 1048600
  70.5 1.2 %copy-done.7 = bf16[1,128,4096]{2,1,0:T(8,128)(2,1)S(1)} copy-done((bf16[1,128,4096]{2,1,0:T(8,128)(2,1)S(1)}, bf16[1,128,4096]{2,1,0:T(8,128)(2,1)}, u32[]{:S(2)}) %copy-start.7) | copy-done | bytes 1048600
  72.7 11.7 %outputs.1 = (bf16[128,4096]{1,0:T(8,128)(2,1)}, bf16[128,4096]{1,0:T(8,128)(2,1)}, bf16[128,4096]{1,0:T(8,128)(2,1)}, bf16[128,4096]{1,0:T(8,128)(2,1)}) custom-call(s32[4]{0:T(128)S(1)} %pad_add_fusion.info_ref.core_ref, bf16[128,4096]{1,0:T(8,128)(2,1)S(1)} %bitcast.21, bf16[128,4096]{1,0:T(8,128)(2,1)S(1)} %bitcast.23, bf16[128,4096]{1,0:T(8,128)(2,1)S(1)} %bitcast.25, ...), custom_call_target="tpu_custom_call" | custom-call | flops 60000002048 | bytes 20000000 | tf_op jit(solution)/shard_map/outputs/pallas_call | solution.py:411
  (50 shorter events, 17.3 us)
Async XLA Ops:
  0.6 20.3 %copy-start.11 = (f32[16,4096]{1,0:T(8,128)S(1)}, f32[16,4096]{1,0:T(8,128)}, u32[]{:S(2)}) copy-start(f32[16,4096]{1,0:T(8,128)} %param.12) | copy-start | bytes 786436
  1.7 19.3 %copy-start.8 = (s32[1,8]{1,0:T(1,128)S(1)}, s32[1,8]{1,0:T(1,128)}, u32[]{:S(2)}) copy-start(s32[1,8]{1,0:T(1,128)} %doc_ref.1) | copy-start | bytes 100
  1.7 1.2 %copy-start = (bf16[1,128,4096]{2,1,0:T(8,128)(2,1)S(1)}, bf16[1,128,4096]{2,1,0:T(8,128)(2,1)}, u32[]{:S(2)}) copy-start(bf16[1,128,4096]{2,1,0:T(8,128)(2,1)} %param.8) | copy-start | bytes 3145732
  3.0 1.2 %copy-start.2 = (bf16[1,128,4096]{2,1,0:T(8,128)(2,1)S(1)}, bf16[1,128,4096]{2,1,0:T(8,128)(2,1)}, u32[]{:S(2)}) copy-start(bf16[1,128,4096]{2,1,0:T(8,128)(2,1)} %param.9) | copy-start | bytes 3145732
  4.2 1.2 %copy-start.4 = (bf16[1,128,4096]{2,1,0:T(8,128)(2,1)S(1)}, bf16[1,128,4096]{2,1,0:T(8,128)(2,1)}, u32[]{:S(2)}) copy-start(bf16[1,128,4096]{2,1,0:T(8,128)(2,1)} %param.7) | copy-start | bytes 3145732
  5.4 1.2 %copy-start.6 = (bf16[1,128,4096]{2,1,0:T(8,128)(2,1)S(1)}, bf16[1,128,4096]{2,1,0:T(8,128)(2,1)}, u32[]{:S(2)}) copy-start(bf16[1,128,4096]{2,1,0:T(8,128)(2,1)} %param.10) | copy-start | bytes 3145732
  20.8 2.4 %collective-permute-start = (f32[6,256,128]{2,1,0:T(8,128)S(1)}, f32[6,256,128]{2,1,0:T(8,128)S(1)}, u32[]{:S(2)}, u32[]{:S(2)}) collective-permute-start(f32[6,256,128]{2,1,0:T(8,128)S(1)} %get-tuple-element.38), channel_id=1, source_target_pairs={{0,1},{1,0},{2,3},{3,2},{4,5},{5,4},{6,7},{7,6},{8,9},{9,8},{10,11... | collective-permute-start | bytes 2359304 | tf_op jit(solution)/shard_map/ppermute | solution.py:349
  23.2 44.9 %copy-start.1 = (bf16[1,128,4096]{2,1,0:T(8,128)(2,1)S(1)}, bf16[1,128,4096]{2,1,0:T(8,128)(2,1)}, u32[]{:S(2)}) copy-start(bf16[1,128,4096]{2,1,0:T(8,128)(2,1)} %param.8) | copy-start | bytes 3145732
  24.8 8.1 %collective-permute-start.1 = (f32[6,64,128]{2,1,0:T(8,128)}, f32[6,64,128]{2,1,0:T(8,128)}, u32[]{:S(2)}, u32[]{:S(2)}) collective-permute-start(f32[6,64,128]{2,1,0:T(8,128)} %get-tuple-element.42), channel_id=1, source_target_pairs={{0,2},{1,3},{2,0},{3,1},{4,6},{5,7},{6,4},{7,5},{8,10},{9,11},{10,... | collective-permute-start | bytes 589832 | tf_op jit(solution)/shard_map/ppermute | solution.py:352
  27.4 9.6 %collective-permute-start.2 = (f32[6,64,128]{2,1,0:T(8,128)}, f32[6,64,128]{2,1,0:T(8,128)}, u32[]{:S(2)}, u32[]{:S(2)}) collective-permute-start(f32[6,64,128]{2,1,0:T(8,128)} %get-tuple-element.41), channel_id=1, source_target_pairs={{0,4},{1,5},{2,6},{3,7},{4,0},{5,1},{6,2},{7,3},{8,12},{9,13},{10,... | collective-permute-start | bytes 589832 | tf_op jit(solution)/shard_map/ppermute | solution.py:352
  28.7 9.5 %collective-permute-start.3 = (f32[6,64,128]{2,1,0:T(8,128)}, f32[6,64,128]{2,1,0:T(8,128)}, u32[]{:S(2)}, u32[]{:S(2)}) collective-permute-start(f32[6,64,128]{2,1,0:T(8,128)} %get-tuple-element.40), channel_id=1, source_target_pairs={{0,6},{1,7},{2,4},{3,5},{4,2},{5,3},{6,0},{7,1},{8,14},{9,15},{10,... | collective-permute-start | bytes 589832 | tf_op jit(solution)/shard_map/ppermute | solution.py:352
  39.5 3.2 %collective-permute-start.4 = (f32[2,64,128]{2,1,0:T(8,128)S(1)}, f32[2,64,128]{2,1,0:T(8,128)S(1)}, u32[]{:S(2)}, u32[]{:S(2)}) collective-permute-start(f32[2,64,128]{2,1,0:T(8,128)S(1)} %get-tuple-element.26), channel_id=1, source_target_pairs={{0,2},{1,3},{2,0},{3,1},{4,6},{5,7},{6,4},{7,5},{8,10},{9,11},{10,... | collective-permute-start | bytes 196616 | tf_op jit(solution)/shard_map/ppermute | solution.py:352
  40.7 3.4 %collective-permute-start.5 = (f32[2,64,128]{2,1,0:T(8,128)S(1)}, f32[2,64,128]{2,1,0:T(8,128)S(1)}, u32[]{:S(2)}, u32[]{:S(2)}) collective-permute-start(f32[2,64,128]{2,1,0:T(8,128)S(1)} %get-tuple-element.27), channel_id=1, source_target_pairs={{0,4},{1,5},{2,6},{3,7},{4,0},{5,1},{6,2},{7,3},{8,12},{9,13},{10,... | collective-permute-start | bytes 196616 | tf_op jit(solution)/shard_map/ppermute | solution.py:352
  41.0 4.6 %collective-permute-start.6 = (f32[2,64,128]{2,1,0:T(8,128)S(1)}, f32[2,64,128]{2,1,0:T(8,128)S(1)}, u32[]{:S(2)}, u32[]{:S(2)}) collective-permute-start(f32[2,64,128]{2,1,0:T(8,128)S(1)} %get-tuple-element.28), channel_id=1, source_target_pairs={{0,6},{1,7},{2,4},{3,5},{4,2},{5,3},{6,0},{7,1},{8,14},{9,15},{10,... | collective-permute-start | bytes 196616 | tf_op jit(solution)/shard_map/ppermute | solution.py:352
  46.9 11.7 %copy-start.9 = (f32[2,256,128]{2,1,0:T(8,128)}, f32[2,256,128]{2,1,0:T(8,128)S(1)}, u32[]{:S(2)}) copy-start(f32[2,256,128]{2,1,0:T(8,128)S(1)} %get-tuple-element.29) | copy-start | bytes 786436
  46.9 21.1 %collective-permute-start.7 = (f32[2,256,128]{2,1,0:T(8,128)}, f32[2,256,128]{2,1,0:T(8,128)S(1)}, u32[]{:S(2)}, u32[]{:S(2)}) collective-permute-start(f32[2,256,128]{2,1,0:T(8,128)} %get-tuple-element.30), channel_id=1, source_target_pairs={{0,1},{1,0},{2,3},{3,2},{4,5},{5,4},{6,7},{7,6},{8,9},{9,8},{10,11... | collective-permute-start | bytes 786440 | tf_op jit(solution)/shard_map/ppermute | solution.py:349
  49.3 3.7 %collective-permute-start.8 = (f32[2,64,128]{2,1,0:T(8,128)S(1)}, f32[2,64,128]{2,1,0:T(8,128)S(1)}, u32[]{:S(2)}, u32[]{:S(2)}) collective-permute-start(f32[2,64,128]{2,1,0:T(8,128)S(1)} %get-tuple-element.35), channel_id=1, source_target_pairs={{0,8},{8,0},{16,24},{24,16},{1,9},{9,1},{17,25},{25,17},{2,10},{10... | collective-permute-start | bytes 196616 | tf_op jit(solution)/shard_map/ppermute | solution.py:396
  53.0 4.1 %collective-permute-start.9 = (f32[2,64,128]{2,1,0:T(8,128)S(1)}, f32[2,64,128]{2,1,0:T(8,128)S(1)}, u32[]{:S(2)}, u32[]{:S(2)}) collective-permute-start(f32[2,64,128]{2,1,0:T(8,128)S(1)} %add.44), channel_id=1, source_target_pairs={{0,16},{8,24},{16,0},{24,8},{1,17},{9,25},{17,1},{25,9},{2,18},{10... | collective-permute-start | bytes 196616 | tf_op jit(solution)/shard_map/ppermute | solution.py:396
  57.1 4.7 %collective-permute-start.10 = (f32[2,64,128]{2,1,0:T(8,128)S(1)}, f32[2,64,128]{2,1,0:T(8,128)S(1)}, u32[]{:S(2)}, u32[]{:S(2)}) collective-permute-start(f32[2,64,128]{2,1,0:T(8,128)S(1)} %add.45.refs_0_), channel_id=1, source_target_pairs={{0,2},{1,3},{2,0},{3,1},{4,6},{5,7},{6,4},{7,5},{8,10},{9,11},{10,... | collective-permute-start | bytes 196616 | tf_op jit(solution)/shard_map/ppermute | solution.py:352
  58.4 3.5 %collective-permute-start.11 = (f32[2,64,128]{2,1,0:T(8,128)S(1)}, f32[2,64,128]{2,1,0:T(8,128)S(1)}, u32[]{:S(2)}, u32[]{:S(2)}) collective-permute-start(f32[2,64,128]{2,1,0:T(8,128)S(1)} %add.45.refs_0_), channel_id=1, source_target_pairs={{0,4},{1,5},{2,6},{3,7},{4,0},{5,1},{6,2},{7,3},{8,12},{9,13},{10,... | collective-permute-start | bytes 196616 | tf_op jit(solution)/shard_map/ppermute | solution.py:352
  58.6 4.0 %collective-permute-start.12 = (f32[2,64,128]{2,1,0:T(8,128)S(1)}, f32[2,64,128]{2,1,0:T(8,128)S(1)}, u32[]{:S(2)}, u32[]{:S(2)}) collective-permute-start(f32[2,64,128]{2,1,0:T(8,128)S(1)} %add.45.refs_0_), channel_id=1, source_target_pairs={{0,6},{1,7},{2,4},{3,5},{4,2},{5,3},{6,0},{7,1},{8,14},{9,15},{10,... | collective-permute-start | bytes 196616 | tf_op jit(solution)/shard_map/ppermute | solution.py:352
  63.2 21.2 %collective-permute-start.13 = (f32[2,256,128]{2,1,0:T(8,128)S(1)}, f32[2,256,128]{2,1,0:T(8,128)S(1)}, u32[]{:S(2)}, u32[]{:S(2)}) collective-permute-start(f32[2,256,128]{2,1,0:T(8,128)S(1)} %gather_sums.1.kept_ref), channel_id=1, source_target_pairs={{0,1},{1,0},{2,3},{3,2},{4,5},{5,4},{6,7},{7,6},{8,9},{9,8},{10,11... | collective-permute-start | bytes 786440 | tf_op jit(solution)/shard_map/ppermute | solution.py:349
  68.1 1.2 %copy-start.3 = (bf16[1,128,4096]{2,1,0:T(8,128)(2,1)S(1)}, bf16[1,128,4096]{2,1,0:T(8,128)(2,1)}, u32[]{:S(2)}) copy-start(bf16[1,128,4096]{2,1,0:T(8,128)(2,1)} %param.9) | copy-start | bytes 3145732
  70.5 1.2 %copy-start.7 = (bf16[1,128,4096]{2,1,0:T(8,128)(2,1)S(1)}, bf16[1,128,4096]{2,1,0:T(8,128)(2,1)}, u32[]{:S(2)}) copy-start(bf16[1,128,4096]{2,1,0:T(8,128)(2,1)} %param.10) | copy-start | bytes 3145732
  (2 other events, 2.2 us)
where the time goes:
time: 87.2 us; the launch traced here: 86.6 us
  Pallas kernels  30.5 us (35%)
  starting transfers between devices  20.3 us (23%)
  waiting for transfers between devices  17.9 us (21%)
  local copies, waits for them, and re-layouts  15.7 us (18%)
  other arithmetic  1.38 us (2%)
    pallas_call x1, Pallas kernels, body(): pl.pallas_call(partial(stats_kernel, float(row_len)), grid=(groups,), in_...  14.1 us
    ppermute x9, waiting for transfers between devices, swap_chip(): return lax.ppermute(x, 'ctx', [(i, i ^ 2 * away) for i in range(n_ctx)])  13.6 us
    pallas_call x1, Pallas kernels, body(): pl.pallas_call(partial(output_kernel, float(row_len)), grid=(groups,), in...  11.7 us
    unnamed x26, local copies, waits for them, and re-layouts  11.6 us
    ppermute x9, starting transfers between devices, swap_chip(): return lax.ppermute(x, 'ctx', [(i, i ^ 2 * away) for i in range(n_ctx)])  9.3 us
    ppermute x3, starting transfers between devices, swap_core(): return lax.ppermute(x, 'ctx', [(i, i ^ 1) for i in range(n_ctx)])  7.32 us
    ppermute x2, waiting for transfers between devices, body(): lax.ppermute(total, 'dp', [(i, i ^ reach) for i in range(n_dp)])  4.13 us
    ppermute x2, starting transfers between devices, body(): lax.ppermute(total, 'dp', [(i, i ^ reach) for i in range(n_dp)])  3.67 us
  transfers between devices with their start and end apart: 14, of which 10 were waited for; matrix products, arithmetic and copies ran while one was open for 5% of the time, Pallas kernels for 14%

commit v1 on v0

v1 whole, which is shorter than its diff:
```python
from functools import partial
import math

import jax
import jax.numpy as jnp
from jax import lax
from jax.experimental import pallas as pl
from jax.experimental.pallas import tpu as pltpu
from jax.sharding import PartitionSpec as P

F32 = jnp.float32
LANES = 128
SUBS = 8
GROUP = LANES * SUBS
CHUNK = 8
BIG = 60


def to_rows(left_ref, right_ref, rows_ref):
    tokens = left_ref.shape[0]
    for pair in range(tokens // 16):
        window = pl.ds(pair * 16, 16)
        for tile in range(SUBS):
            lanes = pl.ds(tile * LANES, LANES)
            product = left_ref[window, lanes].astype(F32) * right_ref[window, lanes].astype(F32)
            for part in range(2):
                start = (pair * 2 + part) * 64 + tile * 8
                rows_ref[pl.ds(start, 8), :] = product[part * 8 : part * 8 + 8]


def token_row(rows_ref, chunk, token):
    return rows_ref[pl.ds(chunk * 64 + token, 8, stride=8), :]


def mode_rows(natural_ref, rows_ref):
    for eight in range(natural_ref.shape[0] // 8):
        for tile in range(SUBS):
            rows_ref[pl.ds(eight * 64 + tile * 8, 8), :] = natural_ref[
                pl.ds(eight * 8, 8), pl.ds(tile * LANES, LANES)
            ]


def mode_row(rows_ref, mode):
    return rows_ref[pl.ds((mode // 8) * 64 + mode % 8, 8, stride=8), :]


def stats_kernel(
    row_len, k_ref, v_ref, q_ref, g_ref, pole_ref, c_ref, b_ref, rate_ref, kept_ref, send_ref,
    u_rows, d_rows, p_rows, lam_s, jump_s, slope_s, state_s, lag_s, res_s, mixl_s, head_s, headl_s, headm_s, pow_s,
    corr_s,
):
    modes = pole_ref.shape[0]
    chunks = k_ref.shape[0] // CHUNK
    first = lax.axis_index("ctx") % 2 == 0
    to_rows(k_ref, v_ref, u_rows)
    to_rows(g_ref, q_ref, d_rows)
    mode_rows(pole_ref, p_rows)
    zero = jnp.zeros((SUBS, LANES), F32)
    for m in range(modes):
        rate = mode_row(p_rows, m) / row_len
        rate_ref[m] = rate
        lam = jnp.exp(-rate)
        square = lam * lam
        fourth = square * square
        lam_s[m] = lam
        jump_s[m] = fourth * fourth
        slope_s[m] = CHUNK * (fourth * (square * lam))
        for ref in (state_s, lag_s, res_s, mixl_s, head_s, headl_s, headm_s):
            ref[m] = zero
        pow_s[m] = zero + 1.0
    for lag in range(CHUNK):
        corr_s[lag] = zero

    def step(chunk, _):
        u = [token_row(u_rows, chunk, t) for t in range(CHUNK)]
        d = [token_row(d_rows, chunk, t) for t in range(CHUNK)]
        for lag in range(CHUNK):
            total = corr_s[lag]
            for t in range(CHUNK - lag):
                total = total + d[t + lag] * u[t]
            corr_s[lag] = total
        offset = (chunk * CHUNK).astype(F32)
        for m in range(modes):
            lam = lam_s[m]
            end, endl = u[0], None
            for t in range(1, CHUNK):
                endl = end if endl is None else endl * lam + end
                end = end * lam + u[t]
            head, headl = d[CHUNK - 1], None
            for t in range(CHUNK - 2, -1, -1):
                headl = head if headl is None else headl * lam + head
                head = head * lam + d[t]
            c_ref[chunk, m] = end
            b_ref[chunk, m] = head
            state, lag_state = state_s[m], lag_s[m]
            res_s[m] = res_s[m] + head * state
            mixl_s[m] = mixl_s[m] + (headl * state + head * lag_state)
            jump = jump_s[m]
            lag_s[m] = lag_state * jump + (state * slope_s[m] + endl)
            state_s[m] = state * jump + end
            power = pow_s[m]
            far = power * head
            head_s[m] = head_s[m] + far
            headl_s[m] = headl_s[m] + power * headl
            headm_s[m] = headm_s[m] + offset * far
            pow_s[m] = power * jump
        return 0

    lax.fori_loop(0, chunks, step, 0)
    def stats_of(m):
        lam = lam_s[m]
        near, nearl = corr_s[CHUNK - 1], None
        for lag in range(CHUNK - 2, -1, -1):
            nearl = near if nearl is None else nearl * lam + near
            near = near * lam + corr_s[lag]
        res = res_s[m]
        return (
            state_s[m],
            lam * lag_s[m],
            head_s[m],
            lam * headl_s[m] + headm_s[m],
            near + lam * res,
            lam * (nearl + (res + lam * mixl_s[m])),
        )

    half = modes // 2
    for m in range(half):
        kept_ref[6, m] = jnp.where(first, rate_ref[m], rate_ref[m + half])
        for i, (low, high) in enumerate(zip(stats_of(m), stats_of(m + half))):
            kept_ref[i, m] = jnp.where(first, low, high)
            send_ref[i, m] = jnp.where(first, high, low)


def local_kernel(
    k_ref, v_ref, q_ref, g_ref, rate_ref, residue_ref, c_ref, b_ref, after_ref,
    z_ref, w_ref, zeros_ref, u_rows, d_rows, r_rows, lam_s, jump_s, lead_s, state_s, back_s, tap_s,
):
    modes = rate_ref.shape[0]
    chunks = k_ref.shape[0] // CHUNK
    zeros_ref[...] = jnp.zeros((1, LANES), F32)
    to_rows(k_ref, v_ref, u_rows)
    to_rows(g_ref, q_ref, d_rows)
    mode_rows(residue_ref, r_rows)
    zero = jnp.zeros((SUBS, LANES), F32)
    taps = [zero for _ in range(CHUNK)]
    for m in range(modes):
        rate = rate_ref[m]
        lam = jnp.exp(-rate)
        square = lam * lam
        fourth = square * square
        lam_s[m] = lam
        jump_s[m] = fourth * fourth
        power = mode_row(r_rows, m) * jnp.sqrt(2.0 * rate)
        lead_s[m] = power * lam
        for lag in range(CHUNK):
            taps[lag] = taps[lag] + power
            power = power * lam
        state_s[m] = zero
        back_s[m] = zero
    for lag in range(CHUNK):
        tap_s[lag] = taps[lag]

    def ahead(chunk, _):
        u = [token_row(u_rows, chunk, t) for t in range(CHUNK)]
        z = [None] * CHUNK
        for lag in range(CHUNK):
            tap = tap_s[lag]
            for t in range(lag, CHUNK):
                term = tap * u[t - lag]
                z[t] = term if z[t] is None else z[t] + term
        for m in range(modes):
            lam = lam_s[m]
            state = state_s[m]
            term = state * lead_s[m]
            for t in range(CHUNK):
                z[t] = z[t] + term
                if t + 1 < CHUNK:
                    term = term * lam
            state_s[m] = state * jump_s[m] + c_ref[chunk, m]
        for t in range(CHUNK):
            z_ref[0, chunk * CHUNK + t] = z[t]
        return 0

    def behind(index, _):
        chunk = chunks - 1 - index
        d = [token_row(d_rows, chunk, t) for t in range(CHUNK)]
        w = [None] * CHUNK
        for lag in range(CHUNK):
            tap = tap_s[lag]
            for t in range(CHUNK - lag):
                term = tap * d[t + lag]
                w[t] = term if w[t] is None else w[t] + term
        for m in range(modes):
            lam = lam_s[m]
            back = back_s[m]
            term = back * lead_s[m]
            for t in range(CHUNK - 1, -1, -1):
                w[t] = w[t] + term
                if t > 0:
                    term = term * lam
            back_s[m] = back * jump_s[m] + b_ref[chunk, m]
        for t in range(CHUNK):
            w_ref[0, chunk * CHUNK + t] = w[t]
        return 0

    lax.fori_loop(0, chunks, ahead, 0)
    lax.fori_loop(0, chunks, behind, 0)


def output_kernel(
    earlier, k_ref, v_ref, q_ref, g_ref, rate_ref, residue_ref, zl_ref, wl_ref, kept_ref, got_ref, after_ref, *refs
):
    mixed_ref, qg_ref, kg_ref, vg_ref, zeros_ref = refs[earlier : earlier + 5]
    z_rows, w_rows, r_rows, lam_s, ahead_s, behind_s = refs[earlier + 5 :]
    modes = rate_ref.shape[0]
    half = modes // 2
    chunks = k_ref.shape[0] // CHUNK
    first = lax.axis_index("ctx") % 2 == 0
    zeros_ref[...] = jnp.zeros((1, LANES), F32)
    mode_rows(residue_ref, r_rows)
    for m in range(modes):
        rate = rate_ref[m]
        lam = jnp.exp(-rate)
        lam_s[m] = lam
        lead = mode_row(r_rows, m) * jnp.sqrt(2.0 * rate) * lam
        mine = first if m < half else jnp.logical_not(first)
        ahead_s[m] = lead * jnp.where(mine, kept_ref[0, m % half], got_ref[0, m % half])
        behind_s[m] = lead * jnp.where(mine, kept_ref[1, m % half], got_ref[1, m % half])

    def step(chunk, _):
        mirror = chunks - 1 - chunk
        z = [zl_ref[0, chunk * CHUNK + t] for t in range(CHUNK)]
        w = [wl_ref[0, mirror * CHUNK + t] for t in range(CHUNK)]
        for m in range(modes):
            lam = lam_s[m]
            ahead, behind = ahead_s[m], behind_s[m]
            for t in range(CHUNK):
                z[t] = z[t] + ahead
                ahead = ahead * lam
                w[CHUNK - 1 - t] = w[CHUNK - 1 - t] + behind
                behind = behind * lam
            ahead_s[m] = ahead
            behind_s[m] = behind
        for t in range(CHUNK):
            z_rows[pl.ds(chunk * 64 + t, 8, stride=8), :] = z[t]
            w_rows[pl.ds(mirror * 64 + t, 8, stride=8), :] = w[t]
        return 0

    lax.fori_loop(0, chunks, step, 0)
    for pair in range(chunks // 2):
        window = pl.ds(pair * 16, 16)
        for tile in range(SUBS):
            lanes = pl.ds(tile * LANES, LANES)
            z = jnp.concatenate([z_rows[pl.ds((pair * 2 + part) * 64 + tile * 8, 8), :] for part in range(2)], axis=0)
            w = jnp.concatenate([w_rows[pl.ds((pair * 2 + part) * 64 + tile * 8, 8), :] for part in range(2)], axis=0)
            mixed_ref[window, lanes] = (q_ref[window, lanes].astype(F32) * z).astype(jnp.bfloat16)
            qg_ref[window, lanes] = (g_ref[window, lanes].astype(F32) * z).astype(jnp.bfloat16)
            kg_ref[window, lanes] = (w * v_ref[window, lanes].astype(F32)).astype(jnp.bfloat16)
            vg_ref[window, lanes] = (w * k_ref[window, lanes].astype(F32)).astype(jnp.bfloat16)


def chip_of():
    me = lax.axis_index("ctx")
    return me % 2, me // 2


def joined_in(doc_ref, chip):
    return (doc_ref[0, 2 * chip] == doc_ref[0, 2 * chip + 1]).astype(F32)


def merge_kernel(block, chips, doc_ref, kept_ref, got_ref, *refs):
    outs, part_ref, chip_ref = refs[:chips], refs[chips], refs[chips + 1]
    core, chip = chip_of()
    first = core == 0
    half = kept_ref.shape[1]
    part = half // chips
    joined = joined_in(doc_ref, chip)
    rate = kept_ref[6]
    part_ref[...] = kept_ref[6, pl.ds(pl.multiple_of(chip * part, part), part), :]
    hop = joined * jnp.exp(-block * rate)
    link = joined * jnp.exp(-rate)
    left = [jnp.where(first, kept_ref[i], got_ref[i]) for i in range(6)]
    right = [jnp.where(first, got_ref[i], kept_ref[i]) for i in range(6)]
    chip_ref[0] = right[0] + hop * left[0]
    chip_ref[1] = right[1] + hop * (left[1] + block * left[0])
    chip_ref[2] = left[2] + hop * right[2]
    chip_ref[3] = left[3] + hop * (right[3] + block * right[2])
    chip_ref[4] = left[4] + right[4] + link * (right[2] * left[0])
    chip_ref[5] = left[5] + right[5] + link * ((right[3] + right[2]) * left[0] + right[2] * left[1])
    for away in range(chips):
        start = pl.multiple_of((chip ^ away) * part, part)
        outs[away][...] = chip_ref[:, pl.ds(start, part), :]


def scan_kernel(block, chips, doc_ref, rate_ref, after_ref, *refs):
    ins, outs, total_ref = refs[:chips], refs[chips : 2 * chips], refs[2 * chips]
    ordered, ends = refs[2 * chips + 1], refs[2 * chips + 2]
    core, chip = chip_of()
    for away in range(chips):
        ordered[chip ^ away] = ins[away][...]
    rate = rate_ref[...]
    lam = jnp.exp(-rate)
    span = 2.0 * block
    hop = jnp.exp(-span * rate)
    zero = jnp.zeros_like(rate)
    state, lag_state, res, grad_lag = zero, zero, zero, zero
    for j in range(chips):
        ends[j, 0] = state
        res = res + (ordered[j, 4] + lam * (ordered[j, 2] * state))
        grad_lag = grad_lag + (
            ordered[j, 5]
            + lam * ((ordered[j, 3] + ordered[j, 2]) * state + ordered[j, 2] * lag_state)
        )
        if j + 1 < chips:
            through = joined_in(doc_ref, j) * hop
            keep = (doc_ref[0, 2 * j + 1] == doc_ref[0, 2 * j + 2]).astype(F32)
            lag_state = keep * (ordered[j, 1] + through * (lag_state + span * state))
            state = keep * (ordered[j, 0] + through * state)
    back = zero
    for j in range(chips - 1, -1, -1):
        ends[j, 1] = back
        if j > 0:
            through = joined_in(doc_ref, j) * hop
            keep = (doc_ref[0, 2 * j - 1] == doc_ref[0, 2 * j]).astype(F32)
            back = keep * (ordered[j, 2] + through * back)
    for away in range(chips):
        outs[away][...] = ends[chip ^ away]
    total_ref[0] = res
    total_ref[1] = grad_lag


def expand_kernel(block, chips, doc_ref, kept_ref, got_ref, after_ref, *refs):
    ins, mine_ref, send_ref, whole = refs[:chips], refs[chips], refs[chips + 1], refs[chips + 2]
    core, chip = chip_of()
    first = core == 0
    joined = joined_in(doc_ref, chip)
    part = ins[0].shape[1]
    for away in range(chips):
        start = pl.multiple_of((chip ^ away) * part, part)
        whole[:, pl.ds(start, part), :] = ins[away][...]
    hop = joined * jnp.exp(-block * kept_ref[6])
    end_left = jnp.where(first, kept_ref[0], got_ref[0])
    head_right = jnp.where(first, got_ref[2], kept_ref[2])
    state, back = whole[0], whole[1]
    state_right = joined * end_left + hop * state
    back_left = joined * head_right + hop * back
    mine_ref[0] = jnp.where(first, state, state_right)
    mine_ref[1] = jnp.where(first, back_left, back)
    send_ref[0] = jnp.where(first, state_right, state)
    send_ref[1] = jnp.where(first, back, back_left)


def gather_kernel(chips, zeros_ref, *refs):
    ins, out_ref = refs[:chips], refs[chips]
    core, chip = chip_of()
    part = ins[0].shape[1]
    for away in range(chips):
        start = pl.multiple_of((chip ^ away) * part, part)
        out_ref[:, pl.ds(start, part), :] = ins[away][...]


def final_kernel(scale, rate_ref, residue_ref, kept_ref, got_ref, res_ref, grad_ref, sums, res_rows, grad_rows):
    core, chip = chip_of()
    half = kept_ref.shape[1]
    sums[:, pl.ds(pl.multiple_of(core * half, half), half), :] = kept_ref[...]
    sums[:, pl.ds(pl.multiple_of((1 - core) * half, half), half), :] = got_ref[...]
    modes, channels = residue_ref.shape
    tall = channels // LANES
    for group in range(channels // GROUP):
        for m in range(modes):
            window = pl.ds(m * tall + group * SUBS, SUBS)
            rate = rate_ref[window, :]
            root = jnp.sqrt(2.0 * rate) * scale
            grad_res, grad_lag = sums[0, window, :], sums[1, window, :]
            target = pl.ds((m // 8) * 64 + m % 8, 8, stride=8)
            res_rows[target, :] = root * grad_res
            grad_rows[target, :] = root * (0.5 * grad_res - rate * grad_lag)
        for eight in range(modes // 8):
            for tile in range(SUBS):
                place = (pl.ds(eight * 8, 8), pl.ds(group * GROUP + tile * LANES, LANES))
                rows = pl.ds(eight * 64 + tile * 8, 8)
                res_ref[place] = res_rows[rows, :]
                grad_ref[place] = residue_ref[place] * grad_rows[rows, :]


def whole(array):
    rank = len(array.shape)
    return pl.BlockSpec(array.shape, lambda i: (0,) * rank)


def small_call(kernel, name, ins, outs, scratch):
    return pl.pallas_call(
        kernel,
        grid=(1,),
        in_specs=[scalar_spec() if x.dtype == jnp.int32 else whole(x) for x in ins],
        out_specs=[whole(x) for x in outs],
        out_shape=outs,
        scratch_shapes=scratch,
        compiler_params=params(),
        name=name,
    )(*ins)


def f32(*shape):
    return jax.ShapeDtypeStruct(shape, F32)


def scalar_spec():
    return pl.BlockSpec(memory_space=pltpu.SMEM)


def params(mib=16):
    return pltpu.CompilerParams(vmem_limit_bytes=mib * 1024 * 1024)


def body(q_proj, k_proj, v_proj, out_grad, residue, pole_decay, group_doc):
    block, channels = q_proj.shape[1], q_proj.shape[2]
    modes = residue.shape[0]
    n_ctx, n_dp = lax.axis_size("ctx"), lax.axis_size("dp")
    row_len = block * n_ctx
    total_tokens = row_len * n_dp
    chips = n_ctx // 2
    groups = channels // GROUP
    chunks = block // CHUNK
    tall = channels // LANES
    rows = modes * tall
    half = rows // 2
    part = half // chips
    halves = modes // 2

    k_in, v_in, q_in, g_in = (x.reshape(block, channels) for x in (k_proj, v_proj, q_proj, out_grad))
    row_scratch = pltpu.VMEM((block * SUBS, LANES), F32)
    mode_scratch = pltpu.VMEM((modes, SUBS, LANES), F32)
    flat_scratch = pltpu.VMEM((modes * SUBS, LANES), F32)
    tap_scratch = pltpu.VMEM((CHUNK, SUBS, LANES), F32)

    def specs(at):
        return (
            pl.BlockSpec((block, GROUP), lambda i: (0, at(i))),
            pl.BlockSpec((modes, SUBS, LANES), lambda i: (0, at(i), 0)),
            pl.BlockSpec((modes, GROUP), lambda i: (0, at(i))),
            pl.BlockSpec((chunks, modes, SUBS, LANES), lambda i: (0, 0, at(i), 0)),
            lambda count: pl.BlockSpec((count, halves, SUBS, LANES), lambda i: (0, 0, at(i), 0)),
        )

    wide, slim, natural, chunked, halved = specs(lambda i: i)
    ends, heads, rate, kept, send = pl.pallas_call(
        partial(stats_kernel, float(row_len)),
        grid=(groups,),
        in_specs=[wide] * 4 + [natural],
        out_specs=[chunked, chunked, slim, halved(7), halved(6)],
        out_shape=[
            jax.ShapeDtypeStruct((chunks, modes, tall, LANES), F32),
            jax.ShapeDtypeStruct((chunks, modes, tall, LANES), F32),
            jax.ShapeDtypeStruct((modes, tall, LANES), F32),
            jax.ShapeDtypeStruct((7, halves, tall, LANES), F32),
            jax.ShapeDtypeStruct((6, halves, tall, LANES), F32),
        ],
        scratch_shapes=[row_scratch] * 2 + [flat_scratch] + [mode_scratch] * 11 + [tap_scratch],
        compiler_params=params(BIG),
        name="block_stats",
    )(k_in, v_in, q_in, g_in, pole_decay)

    rate_rows = rate.reshape(rows, LANES)
    kept = kept.reshape(7, half, LANES)
    send = send.reshape(6, half, LANES)

    def swap_core(x):
        return lax.ppermute(x, "ctx", [(i, i ^ 1) for i in range(n_ctx)])

    def swap_chips(xs):
        return [xs[0]] + [
            lax.ppermute(xs[away], "ctx", [(i, i ^ (2 * away)) for i in range(n_ctx)]) for away in range(1, chips)
        ]

    got = swap_core(send)
    *pieces, rate_part = small_call(
        partial(merge_kernel, float(block), chips),
        "chip_stats",
        [group_doc, kept, got],
        [f32(6, part, LANES)] * chips + [f32(part, LANES)],
        [pltpu.VMEM((6, half, LANES), F32)],
    )
    columns = pl.BlockSpec((1, block, SUBS, LANES), lambda i: (i, 0, 0, 0))
    z_local, w_local, zeros = pl.pallas_call(
        local_kernel,
        grid=(groups,),
        in_specs=[wide] * 4 + [slim, natural] + [chunked] * 2 + [pl.BlockSpec(memory_space=pl.ANY)],
        out_specs=[columns] * 2 + [pl.BlockSpec((1, LANES), lambda i: (0, 0))],
        out_shape=[f32(groups, block, SUBS, LANES)] * 2 + [f32(1, LANES)],
        scratch_shapes=[row_scratch] * 2 + [flat_scratch] + [mode_scratch] * 5 + [tap_scratch],
        compiler_params=params(BIG),
        cost_estimate=pl.CostEstimate(flops=10_000_000_000, bytes_accessed=20_000_000, transcendentals=0),
        name="local_outputs",
    )(k_in, v_in, q_in, g_in, rate, residue, ends, heads, rate_part)
    scanned = small_call(
        partial(scan_kernel, float(block), chips),
        "row_scan",
        [group_doc, rate_part, zeros, *swap_chips(pieces)],
        [f32(2, part, LANES)] * (chips + 1),
        [pltpu.VMEM((chips, 6, part, LANES), F32), pltpu.VMEM((chips, 2, part, LANES), F32)],
    )
    total, reach, outs, done = scanned[chips], 1, [], 0
    arrived = swap_chips(scanned[:chips])
    if n_dp > 2:
        total = total + lax.ppermute(total, "dp", [(i, i ^ reach) for i in range(n_dp)])
        reach *= 2
    mine, give = small_call(
        partial(expand_kernel, float(block), chips),
        "block_edges",
        [group_doc, kept, got, total, *arrived],
        [f32(2, half, LANES)] * 2,
        [pltpu.VMEM((2, half, LANES), F32)],
    )
    theirs = swap_core(give)
    edges = [x.reshape(2, halves, tall, LANES) for x in (mine, theirs)]

    def outputs(first, count, after, outs):
        wide, slim, natural, chunked, halved = specs(lambda i: i + first)
        columns = pl.BlockSpec((1, block, SUBS, LANES), lambda i: (i + first, 0, 0, 0))
        result = pl.pallas_call(
            partial(output_kernel, len(outs)),
            grid=(count,),
            in_specs=[wide] * 4 + [slim, natural] + [columns] * 2 + [halved(2)] * 2
            + [pl.BlockSpec(memory_space=pl.ANY)] * (1 + len(outs)),
            out_specs=[wide] * 4 + [pl.BlockSpec((1, LANES), lambda i: (0, 0))],
            out_shape=[jax.ShapeDtypeStruct((block, channels), jnp.bfloat16)] * 4 + [f32(1, LANES)],
            input_output_aliases={11 + i: i for i in range(len(outs))},
            scratch_shapes=[row_scratch] * 2 + [flat_scratch] + [mode_scratch] * 3,
            compiler_params=params(BIG),
            cost_estimate=pl.CostEstimate(
                flops=2_000_000_000 * count, bytes_accessed=5_000_000 * count, transcendentals=0
            ),
            name="outputs",
        )(k_in, v_in, q_in, g_in, rate, residue, z_local, w_local, *edges, after, *outs)
        return result[:4], result[4]

    while reach < n_dp:
        other = lax.ppermute(total, "dp", [(i, i ^ reach) for i in range(n_dp)])
        reach *= 2
        if reach >= n_dp and groups > 1:
            done = groups // 2
            outs, zeros = outputs(0, done, total, outs)
            other = other + zeros
        total = total + other
    sums = swap_chips([total] * chips)
    outs, zeros = outputs(done, groups - done, total, outs)
    (gathered,) = small_call(
        partial(gather_kernel, chips), "gather_sums", [zeros, *sums], [f32(2, half, LANES)], []
    )
    residue_grad, pole_grad = small_call(
        partial(final_kernel, 1.0 / math.sqrt(total_tokens)),
        "parameter_grads",
        [rate_rows, residue, gathered, swap_core(gathered)],
        [f32(modes, channels)] * 2,
        [pltpu.VMEM((2, rows, LANES), F32)] + [flat_scratch] * 2,
    )
    return (*(x[None] for x in outs), residue_grad, pole_grad)


def solution(mesh):
    tokens = P("dp", "ctx", None)
    return jax.shard_map(
        body,
        mesh=mesh,
        in_specs=(tokens, tokens, tokens, tokens, P(), P(), P("dp", None)),
        out_specs=(tokens, tokens, tokens, tokens, P(), P()),
        check_vma=False,
    )
```

time: 87.2 us -> 73 us (0.84)
  waiting for transfers between devices: 17.9 us -> 7.47 us
  local copies, waits for them, and re-layouts: 15.7 us -> 5.32 us
  Pallas kernels: 30.5 us -> 40.7 us
  starting transfers between devices: 20.3 us -> 17.2 us
    ppermute x9 -> x10, waiting for transfers between devices: 13.6 us -> 3.21 us  [the longest x9 3.2 us: swap_chips(): lax.ppermute(xs[away], 'ctx', [(i, i ^ 2 * away) for i in range(n_ctx)])]
    pallas_call x6 -> x8, Pallas kernels: 16.5 us -> 25.7 us  [the longest x1 11.3 us: body(): pl.pallas_call(local_kernel, grid=(groups,), in_specs=[wide] * 4 + [slim,...]
    unnamed x26 -> x28, local copies, waits for them, and re-layouts: 11.6 us -> 5.32 us
    ppermute x3, waiting for transfers between devices: 0.08 us -> 3.6 us  [swap_core(): return lax.ppermute(x, 'ctx', [(i, i ^ 1) for i in range(n_ctx)])]
    ppermute x2 -> x1, waiting for transfers between devices: 4.13 us -> 0.66 us  [body(): lax.ppermute(total, 'dp', [(i, i ^ reach) for i in range(n_dp)])]
    ppermute x3, starting transfers between devices: 7.32 us -> 4.41 us  [swap_core(): return lax.ppermute(x, 'ctx', [(i, i ^ 1) for i in range(n_ctx)])]
    ppermute x2 -> x1, starting transfers between devices: 3.67 us -> 1.3 us  [body(): lax.ppermute(total, 'dp', [(i, i ^ reach) for i in range(n_dp)])]
    ppermute x9 -> x10, starting transfers between devices: 9.3 us -> 11.5 us  [the longest x9 9.21 us: swap_chips(): lax.ppermute(xs[away], 'ctx', [(i, i ^ 2 * away) for i in range(n_ctx)])]
  transfers between devices with their start and end apart: 14 -> 14, of which waited for: 10 -> 5; matrix products, arithmetic and copies ran while one was open for 5% -> 0% of each run, Pallas kernels for 14% -> 31%
where the time goes in v1:
time: 73 us; the launch traced here: 72.3 us
  Pallas kernels  40.7 us (56%)
  starting transfers between devices  17.2 us (24%)
  waiting for transfers between devices  7.47 us (10%)
  local copies, waits for them, and re-layouts  5.32 us (7%)
  other arithmetic  0.86 us (1%)
  between operations  0.81 us (1%)
    pallas_call x1, Pallas kernels, body(): pl.pallas_call(partial(stats_kernel, float(row_len)), grid=(groups,), in_...  15 us
    pallas_call x1, Pallas kernels, body(): pl.pallas_call(local_kernel, grid=(groups,), in_specs=[wide] * 4 + [slim,...  11.3 us
    pallas_call x2, Pallas kernels, outputs(): pl.pallas_call(partial(output_kernel, len(outs)), grid=(count,), in_specs...  11 us
    ppermute x9, starting transfers between devices, swap_chips(): lax.ppermute(xs[away], 'ctx', [(i, i ^ 2 * away) for i in range(n_ctx)])  9.21 us
    unnamed x28, local copies, waits for them, and re-layouts  5.32 us
    ppermute x3, starting transfers between devices, swap_core(): return lax.ppermute(x, 'ctx', [(i, i ^ 1) for i in range(n_ctx)])  4.41 us
    ppermute x3, waiting for transfers between devices, swap_core(): return lax.ppermute(x, 'ctx', [(i, i ^ 1) for i in range(n_ctx)])  3.6 us
    pallas_call x5, Pallas kernels, small_call(): pl.pallas_call(kernel, grid=(1,), in_specs=[scalar_spec() if x.dtype == j...  3.43 us
  transfers between devices with their start and end apart: 14, of which 5 were waited for; matrix products, arithmetic and copies ran while one was open for 0% of the time, Pallas kernels for 31%

profile of v1, /device:TPU:1, one launch (start us, length us, event | category | flops | bytes accessed | tf_op | source)
XLA Modules:
  0.0 72.3 jit_solution(7091394350960378946)
XLA Ops:
  0.6 15.0 %block_stats.1 = (f32[16,16,32,128]{3,2,1,0:T(8,128)}, f32[16,16,32,128]{3,2,1,0:T(8,128)}, f32[16,32,128]{2,1,0:T(8,128)}, f32[7,8,32,128]{3,2,1,0:T(8,128)}, f32[6,8,32,128]{3,2,1,0:T(8,128)}) custom-call(bf16[128,4096]{1,0:T(8,128)(2,1)} %bitcast.19, bf16[128,4096]{1,0:T(8,128)(2,1)} %bitcast.23, bf16[128,4096]{1,0:T(8,128)(2,1)} %bitcast.27, ...), custom_call_target="tpu_custom_call" | custom-call | tf_op jit(solution)/shard_map/block_stats/pallas_call | solution.py:447
  15.7 2.4 %collective-permute-done.got_ref = f32[6,256,128]{2,1,0:T(8,128)S(1)} collective-permute-done((f32[6,256,128]{2,1,0:T(8,128)}, f32[6,256,128]{2,1,0:T(8,128)S(1)}, u32[]{:S(2)}, u32[]{:S(2)}) %collective-permute-start) | collective-permute-done | bytes 786464 | tf_op jit(solution)/shard_map/ppermute | solution.py:469
  18.1 1.2 %copy-done = f32[7,8,32,128]{3,2,1,0:T(8,128)S(1)} copy-done((f32[7,8,32,128]{3,2,1,0:T(8,128)S(1)}, f32[7,8,32,128]{3,2,1,0:T(8,128)}, u32[]{:S(2)}) %copy-start) | copy-done | bytes 917528
  19.3 1.0 %chip_stats.1 = (f32[6,64,128]{2,1,0:T(8,128)S(1)}, f32[6,64,128]{2,1,0:T(8,128)S(1)}, f32[6,64,128]{2,1,0:T(8,128)S(1)}, f32[6,64,128]{2,1,0:T(8,128)S(1)}, f32[64,128]{1,0:T(8,128)S(1)}) custom-call(s32[1,8]{1,0:T(1,128)S(1)} %copy-done.9, f32[7,256,128]{2,1,0:T(8,128)S(1)} %bitcast.14, f32[6,256,128]{2,1,0:T(8,128)S(1)} %collective-permute-done.got_ref), custom_call_target="tpu_custom_call" | custom-call | tf_op jit(solution)/shard_map/chip_stats/pallas_call | solution.py:392
  20.9 2.3 %collective-permute-start.1 = (f32[6,64,128]{2,1,0:T(8,128)S(1)}, f32[6,64,128]{2,1,0:T(8,128)S(1)}, u32[]{:S(2)}, u32[]{:S(2)}) collective-permute-start(f32[6,64,128]{2,1,0:T(8,128)S(1)} %get-tuple-element.48), channel_id=1, source_target_pairs={{0,2},{1,3},{2,0},{3,1},{4,6},{5,7},{6,4},{7,5},{8,10},{9,11},{10,... | collective-permute-start | bytes 589832 | tf_op jit(solution)/shard_map/ppermute | solution.py:473
  23.2 1.2 %collective-permute-start.2 = (f32[6,64,128]{2,1,0:T(8,128)S(1)}, f32[6,64,128]{2,1,0:T(8,128)S(1)}, u32[]{:S(2)}, u32[]{:S(2)}) collective-permute-start(f32[6,64,128]{2,1,0:T(8,128)S(1)} %get-tuple-element.49), channel_id=1, source_target_pairs={{0,4},{1,5},{2,6},{3,7},{4,0},{5,1},{6,2},{7,3},{8,12},{9,13},{10,... | collective-permute-start | bytes 589832 | tf_op jit(solution)/shard_map/ppermute | solution.py:473
  24.5 11.3 %local_outputs.1 = (f32[4,128,8,128]{3,2,1,0:T(8,128)}, f32[4,128,8,128]{3,2,1,0:T(8,128)}, f32[1,128]{1,0:T(1,128)}) custom-call(bf16[128,4096]{1,0:T(8,128)(2,1)} %bitcast.20, bf16[128,4096]{1,0:T(8,128)(2,1)} %bitcast.24, bf16[128,4096]{1,0:T(8,128)(2,1)} %bitcast.28, bf16[128,4096]{1,0:T(8,128)(2,1)} %bitcast.32, ...), custom_call_target="tpu_custom_call" | custom-call | flops 10000000000 | bytes 20000000 | tf_op jit(solution)/shard_map/local_outputs/pallas_call | solution.py:485
  36.5 0.7 row_scan.1
  37.2 1.5 %collective-permute-start.5 = (f32[2,64,128]{2,1,0:T(8,128)S(1)}, f32[2,64,128]{2,1,0:T(8,128)S(1)}, u32[]{:S(2)}, u32[]{:S(2)}) collective-permute-start(f32[2,64,128]{2,1,0:T(8,128)S(1)} %get-tuple-element.53), channel_id=1, source_target_pairs={{0,2},{1,3},{2,0},{3,1},{4,6},{5,7},{6,4},{7,5},{8,10},{9,11},{10,... | collective-permute-start | bytes 196616 | tf_op jit(solution)/shard_map/ppermute | solution.py:473
  38.7 1.3 %collective-permute-start.4 = (f32[2,64,128]{2,1,0:T(8,128)S(1)}, f32[2,64,128]{2,1,0:T(8,128)S(1)}, u32[]{:S(2)}, u32[]{:S(2)}) collective-permute-start(f32[2,64,128]{2,1,0:T(8,128)S(1)} %get-tuple-element.51), channel_id=1, source_target_pairs={{0,8},{8,0},{16,24},{24,16},{1,9},{9,1},{17,25},{25,17},{2,10},{10... | collective-permute-start | bytes 196616 | tf_op jit(solution)/shard_map/ppermute | solution.py:506
  40.0 1.2 %collective-permute-start.6 = (f32[2,64,128]{2,1,0:T(8,128)S(1)}, f32[2,64,128]{2,1,0:T(8,128)S(1)}, u32[]{:S(2)}, u32[]{:S(2)}) collective-permute-start(f32[2,64,128]{2,1,0:T(8,128)S(1)} %get-tuple-element.54), channel_id=1, source_target_pairs={{0,4},{1,5},{2,6},{3,7},{4,0},{5,1},{6,2},{7,3},{8,12},{9,13},{10,... | collective-permute-start | bytes 196616 | tf_op jit(solution)/shard_map/ppermute | solution.py:473
  42.1 1.3 %collective-permute-done.6.refs_2_ = f32[2,64,128]{2,1,0:T(8,128)S(1)} collective-permute-done((f32[2,64,128]{2,1,0:T(8,128)S(1)}, f32[2,64,128]{2,1,0:T(8,128)S(1)}, u32[]{:S(2)}, u32[]{:S(2)}) %collective-permute-start.6) | collective-permute-done | bytes 65568 | tf_op jit(solution)/shard_map/ppermute | solution.py:473
  43.4 1.9 %collective-permute-done.7.refs_3_ = f32[2,64,128]{2,1,0:T(8,128)S(1)} collective-permute-done((f32[2,64,128]{2,1,0:T(8,128)S(1)}, f32[2,64,128]{2,1,0:T(8,128)S(1)}, u32[]{:S(2)}, u32[]{:S(2)}) %collective-permute-start.7) | collective-permute-done | bytes 65568 | tf_op jit(solution)/shard_map/ppermute | solution.py:473
  46.7 3.1 %collective-permute-start.8 = (f32[2,256,128]{2,1,0:T(8,128)S(1)}, f32[2,256,128]{2,1,0:T(8,128)S(1)}, u32[]{:S(2)}, u32[]{:S(2)}) collective-permute-start(f32[2,256,128]{2,1,0:T(8,128)S(1)} %get-tuple-element.57), channel_id=1, source_target_pairs={{0,1},{1,0},{2,3},{3,2},{4,5},{5,4},{6,7},{7,6},{8,9},{9,8},{10,11... | collective-permute-start | bytes 786440 | tf_op jit(solution)/shard_map/ppermute | solution.py:469
  49.8 2.3 %collective-permute-start.9 = (f32[2,64,128]{2,1,0:T(8,128)S(1)}, f32[2,64,128]{2,1,0:T(8,128)S(1)}, u32[]{:S(2)}, u32[]{:S(2)}) collective-permute-start(f32[2,64,128]{2,1,0:T(8,128)S(1)} %add.16.after_ref), channel_id=1, source_target_pairs={{0,16},{8,24},{16,0},{24,8},{1,17},{9,25},{17,1},{25,9},{2,18},{10... | collective-permute-start | bytes 196616 | tf_op jit(solution)/shard_map/ppermute | solution.py:539
  52.8 5.5 %outputs.2 = (bf16[128,4096]{1,0:T(8,128)(2,1)}, bf16[128,4096]{1,0:T(8,128)(2,1)}, bf16[128,4096]{1,0:T(8,128)(2,1)}, bf16[128,4096]{1,0:T(8,128)(2,1)}, f32[1,128]{1,0:T(1,128)}) custom-call(bf16[128,4096]{1,0:T(8,128)(2,1)} %bitcast.21, bf16[128,4096]{1,0:T(8,128)(2,1)} %bitcast.25, bf16[128,4096]{1,0:T(8,128)(2,1)} %bitcast.29, ...), custom_call_target="tpu_custom_call" | custom-call | flops 4000000000 | bytes 10000000 | tf_op jit(solution)/shard_map/outputs/pallas_call | solution.py:521
  58.3 0.9 %add_add_fusion.after_ref.refs_0_ = f32[2,64,128]{2,1,0:T(8,128)S(1)} fusion(f32[2,64,128]{2,1,0:T(8,128)} %copy-done.2, f32[2,64,128]{2,1,0:T(8,128)S(1)} %collective-permute-done.9, f32[128]{0:T(128)} %bitcast.35), kind=kLoop, calls=%fused_computation | loop fusion | flops 32768 | bytes 197120 | tf_op jit(solution)/shard_map/add | solution.py:545
  59.4 1.2 %collective-permute-start.11 = (f32[2,64,128]{2,1,0:T(8,128)S(1)}, f32[2,64,128]{2,1,0:T(8,128)S(1)}, u32[]{:S(2)}, u32[]{:S(2)}) collective-permute-start(f32[2,64,128]{2,1,0:T(8,128)S(1)} %add_add_fusion.after_ref.refs_0_), channel_id=1, source_target_pairs={{0,4},{1,5},{2,6},{3,7},{4,0},{5,1},{6,2},{7,3},{8,12},{9,13},{10,... | collective-permute-start | bytes 196616 | tf_op jit(solution)/shard_map/ppermute | solution.py:473
  60.7 1.2 %collective-permute-start.10 = (f32[2,64,128]{2,1,0:T(8,128)S(1)}, f32[2,64,128]{2,1,0:T(8,128)S(1)}, u32[]{:S(2)}, u32[]{:S(2)}) collective-permute-start(f32[2,64,128]{2,1,0:T(8,128)S(1)} %add_add_fusion.after_ref.refs_0_), channel_id=1, source_target_pairs={{0,2},{1,3},{2,0},{3,1},{4,6},{5,7},{6,4},{7,5},{8,10},{9,11},{10,... | collective-permute-start | bytes 196616 | tf_op jit(solution)/shard_map/ppermute | solution.py:473
  61.9 5.5 %outputs.3 = (bf16[128,4096]{1,0:T(8,128)(2,1)}, bf16[128,4096]{1,0:T(8,128)(2,1)}, bf16[128,4096]{1,0:T(8,128)(2,1)}, bf16[128,4096]{1,0:T(8,128)(2,1)}, f32[1,128]{1,0:T(1,128)}) custom-call(bf16[128,4096]{1,0:T(8,128)(2,1)} %bitcast.22, bf16[128,4096]{1,0:T(8,128)(2,1)} %bitcast.26, ...), custom_call_target="tpu_custom_call", output_to_operand_aliasing={{0}: (11, {}), {1}: (12, {}), {2}: (13, {}), {3}: (14, {})} | custom-call | flops 4000000000 | bytes 10000000 | tf_op jit(solution)/shard_map/outputs/pallas_call | solution.py:521
  67.5 0.8 %copy-done.4 = f32[2,64,128]{2,1,0:T(8,128)S(1)} copy-done((f32[2,64,128]{2,1,0:T(8,128)S(1)}, f32[2,64,128]{2,1,0:T(8,128)}, u32[]{:S(2)}) %copy-start.4) | copy-done | bytes 65560
  69.0 1.2 %collective-permute-start.13 = (f32[2,256,128]{2,1,0:T(8,128)S(1)}, f32[2,256,128]{2,1,0:T(8,128)S(1)}, u32[]{:S(2)}, u32[]{:S(2)}) collective-permute-start(f32[2,256,128]{2,1,0:T(8,128)S(1)} %gather_sums.1.kept_ref), channel_id=1, source_target_pairs={{0,1},{1,0},{2,3},{3,2},{4,5},{5,4},{6,7},{7,6},{8,9},{9,8},{10,11... | collective-permute-start | bytes 786440 | tf_op jit(solution)/shard_map/ppermute | solution.py:469
  70.2 1.2 %collective-permute-done.13.got_ref = f32[2,256,128]{2,1,0:T(8,128)S(1)} collective-permute-done((f32[2,256,128]{2,1,0:T(8,128)S(1)}, f32[2,256,128]{2,1,0:T(8,128)S(1)}, u32[]{:S(2)}, u32[]{:S(2)}) %collective-permute-start.13) | collective-permute-done | bytes 262176 | tf_op jit(solution)/shard_map/ppermute | solution.py:469
  71.3 1.0 %parameter_grads.1 = (f32[16,4096]{1,0:T(8,128)}, f32[16,4096]{1,0:T(8,128)}) custom-call(f32[512,128]{1,0:T(8,128)S(1)} %bitcast.16, f32[16,4096]{1,0:T(8,128)S(1)} %copy-done.5, f32[2,256,128]{2,1,0:T(8,128)S(1)} %gather_sums.1.kept_ref, f32[2,256,128]{2,1,0:T(8,128)S(1)} %collective-permute-done.13.got_ref), custom_call_target="tpu_custom_call" | custom-call | tf_op jit(solution)/shard_map/parameter_grads/pallas_call | solution.py:392
  (43 shorter events, 5.3 us)
Async XLA Ops:
  0.6 17.5 %copy-start.9 = (s32[1,8]{1,0:T(1,128)S(1)}, s32[1,8]{1,0:T(1,128)}, u32[]{:S(2)}) copy-start(s32[1,8]{1,0:T(1,128)} %doc_ref.5) | copy-start | bytes 100
  15.6 2.5 %collective-permute-start = (f32[6,256,128]{2,1,0:T(8,128)}, f32[6,256,128]{2,1,0:T(8,128)S(1)}, u32[]{:S(2)}, u32[]{:S(2)}) collective-permute-start(f32[6,256,128]{2,1,0:T(8,128)} %bitcast.36), channel_id=1, source_target_pairs={{0,1},{1,0},{2,3},{3,2},{4,5},{5,4},{6,7},{7,6},{8,9},{9,8},{10,11... | collective-permute-start | bytes 2359304 | tf_op jit(solution)/shard_map/ppermute | solution.py:469
  18.1 1.2 %copy-start = (f32[7,8,32,128]{3,2,1,0:T(8,128)S(1)}, f32[7,8,32,128]{3,2,1,0:T(8,128)}, u32[]{:S(2)}) copy-start(f32[7,8,32,128]{3,2,1,0:T(8,128)} %get-tuple-element.41) | copy-start | bytes 2752516
  20.9 14.9 %collective-permute-start.1 = (f32[6,64,128]{2,1,0:T(8,128)S(1)}, f32[6,64,128]{2,1,0:T(8,128)S(1)}, u32[]{:S(2)}, u32[]{:S(2)}) collective-permute-start(f32[6,64,128]{2,1,0:T(8,128)S(1)} %get-tuple-element.48), channel_id=1, source_target_pairs={{0,2},{1,3},{2,0},{3,1},{4,6},{5,7},{6,4},{7,5},{8,10},{9,11},{10,... | collective-permute-start | bytes 589832 | tf_op jit(solution)/shard_map/ppermute | solution.py:473
  23.2 12.5 %collective-permute-start.2 = (f32[6,64,128]{2,1,0:T(8,128)S(1)}, f32[6,64,128]{2,1,0:T(8,128)S(1)}, u32[]{:S(2)}, u32[]{:S(2)}) collective-permute-start(f32[6,64,128]{2,1,0:T(8,128)S(1)} %get-tuple-element.49), channel_id=1, source_target_pairs={{0,4},{1,5},{2,6},{3,7},{4,0},{5,1},{6,2},{7,3},{8,12},{9,13},{10,... | collective-permute-start | bytes 589832 | tf_op jit(solution)/shard_map/ppermute | solution.py:473
  24.5 11.3 %collective-permute-start.3 = (f32[6,64,128]{2,1,0:T(8,128)S(1)}, f32[6,64,128]{2,1,0:T(8,128)S(1)}, u32[]{:S(2)}, u32[]{:S(2)}) collective-permute-start(f32[6,64,128]{2,1,0:T(8,128)S(1)} %get-tuple-element.50), channel_id=1, source_target_pairs={{0,6},{1,7},{2,4},{3,5},{4,2},{5,3},{6,0},{7,1},{8,14},{9,15},{10,... | collective-permute-start | bytes 589832 | tf_op jit(solution)/shard_map/ppermute | solution.py:473
  24.5 11.3 %copy-start.8 = (f32[64,128]{1,0:T(8,128)S(1)}, f32[64,128]{1,0:T(8,128)}, u32[]{:S(2)}) copy-start(f32[64,128]{1,0:T(8,128)} %copy-done.7) | copy-start | bytes 98308
  24.5 20.8 %copy-start.1 = (f32[7,8,32,128]{3,2,1,0:T(8,128)S(1)}, f32[7,8,32,128]{3,2,1,0:T(8,128)}, u32[]{:S(2)}) copy-start(f32[7,8,32,128]{3,2,1,0:T(8,128)} %get-tuple-element.41) | copy-start | bytes 2752516
  37.2 4.9 %collective-permute-start.5 = (f32[2,64,128]{2,1,0:T(8,128)S(1)}, f32[2,64,128]{2,1,0:T(8,128)S(1)}, u32[]{:S(2)}, u32[]{:S(2)}) collective-permute-start(f32[2,64,128]{2,1,0:T(8,128)S(1)} %get-tuple-element.53), channel_id=1, source_target_pairs={{0,2},{1,3},{2,0},{3,1},{4,6},{5,7},{6,4},{7,5},{8,10},{9,11},{10,... | collective-permute-start | bytes 196616 | tf_op jit(solution)/shard_map/ppermute | solution.py:473
  38.7 3.4 %collective-permute-start.4 = (f32[2,64,128]{2,1,0:T(8,128)S(1)}, f32[2,64,128]{2,1,0:T(8,128)S(1)}, u32[]{:S(2)}, u32[]{:S(2)}) collective-permute-start(f32[2,64,128]{2,1,0:T(8,128)S(1)} %get-tuple-element.51), channel_id=1, source_target_pairs={{0,8},{8,0},{16,24},{24,16},{1,9},{9,1},{17,25},{25,17},{2,10},{10... | collective-permute-start | bytes 196616 | tf_op jit(solution)/shard_map/ppermute | solution.py:506
  40.0 3.4 %collective-permute-start.6 = (f32[2,64,128]{2,1,0:T(8,128)S(1)}, f32[2,64,128]{2,1,0:T(8,128)S(1)}, u32[]{:S(2)}, u32[]{:S(2)}) collective-permute-start(f32[2,64,128]{2,1,0:T(8,128)S(1)} %get-tuple-element.54), channel_id=1, source_target_pairs={{0,4},{1,5},{2,6},{3,7},{4,0},{5,1},{6,2},{7,3},{8,12},{9,13},{10,... | collective-permute-start | bytes 196616 | tf_op jit(solution)/shard_map/ppermute | solution.py:473
  41.2 4.1 %collective-permute-start.7 = (f32[2,64,128]{2,1,0:T(8,128)S(1)}, f32[2,64,128]{2,1,0:T(8,128)S(1)}, u32[]{:S(2)}, u32[]{:S(2)}) collective-permute-start(f32[2,64,128]{2,1,0:T(8,128)S(1)} %get-tuple-element.55), channel_id=1, source_target_pairs={{0,6},{1,7},{2,4},{3,5},{4,2},{5,3},{6,0},{7,1},{8,14},{9,15},{10,... | collective-permute-start | bytes 196616 | tf_op jit(solution)/shard_map/ppermute | solution.py:473
  42.1 10.1 %copy-start.2 = (f32[2,64,128]{2,1,0:T(8,128)}, f32[2,64,128]{2,1,0:T(8,128)S(1)}, u32[]{:S(2)}) copy-start(f32[2,64,128]{2,1,0:T(8,128)S(1)} %add.16.after_ref) | copy-start | bytes 196612
  46.0 0.7 copy-start.12
  46.7 5.5 %collective-permute-start.8 = (f32[2,256,128]{2,1,0:T(8,128)S(1)}, f32[2,256,128]{2,1,0:T(8,128)S(1)}, u32[]{:S(2)}, u32[]{:S(2)}) collective-permute-start(f32[2,256,128]{2,1,0:T(8,128)S(1)} %get-tuple-element.57), channel_id=1, source_target_pairs={{0,1},{1,0},{2,3},{3,2},{4,5},{5,4},{6,7},{7,6},{8,9},{9,8},{10,11... | collective-permute-start | bytes 786440 | tf_op jit(solution)/shard_map/ppermute | solution.py:469
  49.8 8.5 %collective-permute-start.9 = (f32[2,64,128]{2,1,0:T(8,128)S(1)}, f32[2,64,128]{2,1,0:T(8,128)S(1)}, u32[]{:S(2)}, u32[]{:S(2)}) collective-permute-start(f32[2,64,128]{2,1,0:T(8,128)S(1)} %add.16.after_ref), channel_id=1, source_target_pairs={{0,16},{8,24},{16,0},{24,8},{1,17},{9,25},{17,1},{25,9},{2,18},{10... | collective-permute-start | bytes 196616 | tf_op jit(solution)/shard_map/ppermute | solution.py:539
  59.2 2.7 %copy-start.3 = (f32[2,64,128]{2,1,0:T(8,128)}, f32[2,64,128]{2,1,0:T(8,128)S(1)}, u32[]{:S(2)}) copy-start(f32[2,64,128]{2,1,0:T(8,128)S(1)} %add_add_fusion.after_ref.refs_0_) | copy-start | bytes 196612
  59.2 8.3 %collective-permute-start.12 = (f32[2,64,128]{2,1,0:T(8,128)S(1)}, f32[2,64,128]{2,1,0:T(8,128)S(1)}, u32[]{:S(2)}, u32[]{:S(2)}) collective-permute-start(f32[2,64,128]{2,1,0:T(8,128)S(1)} %add_add_fusion.after_ref.refs_0_), channel_id=1, source_target_pairs={{0,6},{1,7},{2,4},{3,5},{4,2},{5,3},{6,0},{7,1},{8,14},{9,15},{10,... | collective-permute-start | bytes 196616 | tf_op jit(solution)/shard_map/ppermute | solution.py:473
  59.4 8.0 %collective-permute-start.11 = (f32[2,64,128]{2,1,0:T(8,128)S(1)}, f32[2,64,128]{2,1,0:T(8,128)S(1)}, u32[]{:S(2)}, u32[]{:S(2)}) collective-permute-start(f32[2,64,128]{2,1,0:T(8,128)S(1)} %add_add_fusion.after_ref.refs_0_), channel_id=1, source_target_pairs={{0,4},{1,5},{2,6},{3,7},{4,0},{5,1},{6,2},{7,3},{8,12},{9,13},{10,... | collective-permute-start | bytes 196616 | tf_op jit(solution)/shard_map/ppermute | solution.py:473
  60.7 6.8 %collective-permute-start.10 = (f32[2,64,128]{2,1,0:T(8,128)S(1)}, f32[2,64,128]{2,1,0:T(8,128)S(1)}, u32[]{:S(2)}, u32[]{:S(2)}) collective-permute-start(f32[2,64,128]{2,1,0:T(8,128)S(1)} %add_add_fusion.after_ref.refs_0_), channel_id=1, source_target_pairs={{0,2},{1,3},{2,0},{3,1},{4,6},{5,7},{6,4},{7,5},{8,10},{9,11},{10,... | collective-permute-start | bytes 196616 | tf_op jit(solution)/shard_map/ppermute | solution.py:473
  61.9 9.4 %copy-start.5 = (f32[16,4096]{1,0:T(8,128)S(1)}, f32[16,4096]{1,0:T(8,128)}, u32[]{:S(2)}) copy-start(f32[16,4096]{1,0:T(8,128)} %residue_ref.7) | copy-start | bytes 786436
  61.9 9.4 %copy-start.6 = (f32[16,32,128]{2,1,0:T(8,128)S(1)}, f32[16,32,128]{2,1,0:T(8,128)}, u32[]{:S(2)}) copy-start(f32[16,32,128]{2,1,0:T(8,128)} %get-tuple-element.38.rate_ref) | copy-start | bytes 786436
  67.5 0.8 %copy-start.4 = (f32[2,64,128]{2,1,0:T(8,128)S(1)}, f32[2,64,128]{2,1,0:T(8,128)}, u32[]{:S(2)}) copy-start(f32[2,64,128]{2,1,0:T(8,128)} %copy-done.3) | copy-start | bytes 196612
  69.0 2.4 %collective-permute-start.13 = (f32[2,256,128]{2,1,0:T(8,128)S(1)}, f32[2,256,128]{2,1,0:T(8,128)S(1)}, u32[]{:S(2)}, u32[]{:S(2)}) collective-permute-start(f32[2,256,128]{2,1,0:T(8,128)S(1)} %gather_sums.1.kept_ref), channel_id=1, source_target_pairs={{0,1},{1,0},{2,3},{3,2},{4,5},{5,4},{6,7},{7,6},{8,9},{9,8},{10,11... | collective-permute-start | bytes 786440 | tf_op jit(solution)/shard_map/ppermute | solution.py:469
  (4 other events, 2.6 us)

commit v2 on v1

--- a/solution.py
+++ b/solution.py
@@ -13,7 +13,7 @@
 SUBS = 8
 GROUP = LANES * SUBS
 CHUNK = 8
-BIG = 60
+BIG = 32
 
 
 def to_rows(left_ref, right_ref, rows_ref):
@@ -58,7 +58,7 @@
     zero = jnp.zeros((SUBS, LANES), F32)
     for m in range(modes):
         rate = mode_row(p_rows, m) / row_len
-        rate_ref[m] = rate
+        rate_ref[0, m] = rate
         lam = jnp.exp(-rate)
         square = lam * lam
         fourth = square * square
@@ -90,8 +90,8 @@
             for t in range(CHUNK - 2, -1, -1):
                 headl = head if headl is None else headl * lam + head
                 head = head * lam + d[t]
-            c_ref[chunk, m] = end
-            b_ref[chunk, m] = head
+            c_ref[0, chunk, m] = end
+            b_ref[0, chunk, m] = head
             state, lag_state = state_s[m], lag_s[m]
             res_s[m] = res_s[m] + head * state
             mixl_s[m] = mixl_s[m] + (headl * state + head * lag_state)
@@ -125,17 +125,17 @@
 
     half = modes // 2
     for m in range(half):
-        kept_ref[6, m] = jnp.where(first, rate_ref[m], rate_ref[m + half])
+        kept_ref[6, 0, m] = jnp.where(first, rate_ref[0, m], rate_ref[0, m + half])
         for i, (low, high) in enumerate(zip(stats_of(m), stats_of(m + half))):
-            kept_ref[i, m] = jnp.where(first, low, high)
-            send_ref[i, m] = jnp.where(first, high, low)
+            kept_ref[i, 0, m] = jnp.where(first, low, high)
+            send_ref[i, 0, m] = jnp.where(first, high, low)
 
 
 def local_kernel(
     k_ref, v_ref, q_ref, g_ref, rate_ref, residue_ref, c_ref, b_ref, after_ref,
     z_ref, w_ref, zeros_ref, u_rows, d_rows, r_rows, lam_s, jump_s, lead_s, state_s, back_s, tap_s,
 ):
-    modes = rate_ref.shape[0]
+    modes = rate_ref.shape[1]
     chunks = k_ref.shape[0] // CHUNK
     zeros_ref[...] = jnp.zeros((1, LANES), F32)
     to_rows(k_ref, v_ref, u_rows)
@@ -144,7 +144,7 @@
     zero = jnp.zeros((SUBS, LANES), F32)
     taps = [zero for _ in range(CHUNK)]
     for m in range(modes):
-        rate = rate_ref[m]
+        rate = rate_ref[0, m]
         lam = jnp.exp(-rate)
         square = lam * lam
         fourth = square * square
@@ -160,7 +160,8 @@
     for lag in range(CHUNK):
         tap_s[lag] = taps[lag]
 
-    def ahead(chunk, _):
+    def step(chunk, _):
+        mirror = chunks - 1 - chunk
         u = [token_row(u_rows, chunk, t) for t in range(CHUNK)]
         z = [None] * CHUNK
         for lag in range(CHUNK):
@@ -168,22 +169,7 @@
             for t in range(lag, CHUNK):
                 term = tap * u[t - lag]
                 z[t] = term if z[t] is None else z[t] + term
-        for m in range(modes):
-            lam = lam_s[m]
-            state = state_s[m]
-            term = state * lead_s[m]
-            for t in range(CHUNK):
-                z[t] = z[t] + term
-                if t + 1 < CHUNK:
-                    term = term * lam
-            state_s[m] = state * jump_s[m] + c_ref[chunk, m]
-        for t in range(CHUNK):
-            z_ref[0, chunk * CHUNK + t] = z[t]
-        return 0
-
-    def behind(index, _):
-        chunk = chunks - 1 - index
-        d = [token_row(d_rows, chunk, t) for t in range(CHUNK)]
+        d = [token_row(d_rows, mirror, t) for t in range(CHUNK)]
         w = [None] * CHUNK
         for lag in range(CHUNK):
             tap = tap_s[lag]
@@ -191,20 +177,23 @@
                 term = tap * d[t + lag]
                 w[t] = term if w[t] is None else w[t] + term
         for m in range(modes):
-            lam = lam_s[m]
-            back = back_s[m]
-            term = back * lead_s[m]
-            for t in range(CHUNK - 1, -1, -1):
-                w[t] = w[t] + term
-                if t > 0:
-                    term = term * lam
-            back_s[m] = back * jump_s[m] + b_ref[chunk, m]
+            lam, lead, jump = lam_s[m], lead_s[m], jump_s[m]
+            state, back = state_s[m], back_s[m]
+            ahead, behind = state * lead, back * lead
+            for t in range(CHUNK):
+                z[t] = z[t] + ahead
+                w[CHUNK - 1 - t] = w[CHUNK - 1 - t] + behind
+                if t + 1 < CHUNK:
+                    ahead = ahead * lam
+                    behind = behind * lam
+            state_s[m] = state * jump + c_ref[0, chunk, m]
+            back_s[m] = back * jump + b_ref[0, mirror, m]
         for t in range(CHUNK):
-            w_ref[0, chunk * CHUNK + t] = w[t]
+            z_ref[0, chunk * CHUNK + t] = z[t]
+            w_ref[0, mirror * CHUNK + t] = w[t]
         return 0
 
-    lax.fori_loop(0, chunks, ahead, 0)
-    lax.fori_loop(0, chunks, behind, 0)
+    lax.fori_loop(0, chunks, step, 0)
 
 
 def output_kernel(
@@ -212,20 +201,20 @@
 ):
     mixed_ref, qg_ref, kg_ref, vg_ref, zeros_ref = refs[earlier : earlier + 5]
     z_rows, w_rows, r_rows, lam_s, ahead_s, behind_s = refs[earlier + 5 :]
-    modes = rate_ref.shape[0]
+    modes = rate_ref.shape[1]
     half = modes // 2
     chunks = k_ref.shape[0] // CHUNK
     first = lax.axis_index("ctx") % 2 == 0
     zeros_ref[...] = jnp.zeros((1, LANES), F32)
     mode_rows(residue_ref, r_rows)
     for m in range(modes):
-        rate = rate_ref[m]
+        rate = rate_ref[0, m]
         lam = jnp.exp(-rate)
         lam_s[m] = lam
         lead = mode_row(r_rows, m) * jnp.sqrt(2.0 * rate) * lam
         mine = first if m < half else jnp.logical_not(first)
-        ahead_s[m] = lead * jnp.where(mine, kept_ref[0, m % half], got_ref[0, m % half])
-        behind_s[m] = lead * jnp.where(mine, kept_ref[1, m % half], got_ref[1, m % half])
+        ahead_s[m] = lead * jnp.where(mine, kept_ref[0, 0, m % half], got_ref[0, 0, m % half])
+        behind_s[m] = lead * jnp.where(mine, kept_ref[1, 0, m % half], got_ref[1, 0, m % half])
 
     def step(chunk, _):
         mirror = chunks - 1 - chunk
@@ -292,7 +281,8 @@
         outs[away][...] = chip_ref[:, pl.ds(start, part), :]
 
 
-def scan_kernel(block, chips, doc_ref, rate_ref, after_ref, *refs):
+def scan_kernel(block, chips, doc_ref, rate_ref, *refs):
+    refs = refs[:chips] + refs[chips + 1 :]
     ins, outs, total_ref = refs[:chips], refs[chips : 2 * chips], refs[2 * chips]
     ordered, ends = refs[2 * chips + 1], refs[2 * chips + 2]
     core, chip = chip_of()
@@ -329,7 +319,7 @@
     total_ref[1] = grad_lag
 
 
-def expand_kernel(block, chips, doc_ref, kept_ref, got_ref, after_ref, *refs):
+def expand_kernel(block, chips, doc_ref, kept_ref, got_ref, *refs):
     ins, mine_ref, send_ref, whole = refs[:chips], refs[chips], refs[chips + 1], refs[chips + 2]
     core, chip = chip_of()
     first = core == 0
@@ -350,8 +340,8 @@
     send_ref[1] = jnp.where(first, back, back_left)
 
 
-def gather_kernel(chips, zeros_ref, *refs):
-    ins, out_ref = refs[:chips], refs[chips]
+def gather_kernel(chips, *refs):
+    ins, out_ref = refs[:chips], refs[chips + 1]
     core, chip = chip_of()
     part = ins[0].shape[1]
     for away in range(chips):
@@ -365,11 +355,11 @@
     sums[:, pl.ds(pl.multiple_of(core * half, half), half), :] = kept_ref[...]
     sums[:, pl.ds(pl.multiple_of((1 - core) * half, half), half), :] = got_ref[...]
     modes, channels = residue_ref.shape
-    tall = channels // LANES
+    halves = modes // 2
     for group in range(channels // GROUP):
         for m in range(modes):
-            window = pl.ds(m * tall + group * SUBS, SUBS)
-            rate = rate_ref[window, :]
+            window = pl.ds((m // halves) * half + (group * halves + m % halves) * SUBS, SUBS)
+            rate = rate_ref[group, m]
             root = jnp.sqrt(2.0 * rate) * scale
             grad_res, grad_lag = sums[0, window, :], sums[1, window, :]
             target = pl.ds((m // 8) * 64 + m % 8, 8, stride=8)
@@ -388,17 +378,29 @@
     return pl.BlockSpec(array.shape, lambda i: (0,) * rank)
 
 
-def small_call(kernel, name, ins, outs, scratch):
+def unread():
+    return pl.BlockSpec(memory_space=pl.ANY)
+
+
+def small_call(kernel, name, ins, outs, scratch, after=()):
     return pl.pallas_call(
         kernel,
         grid=(1,),
-        in_specs=[scalar_spec() if x.dtype == jnp.int32 else whole(x) for x in ins],
+        in_specs=[scalar_spec() if x.dtype == jnp.int32 else whole(x) for x in ins] + [unread() for _ in after],
         out_specs=[whole(x) for x in outs],
         out_shape=outs,
         scratch_shapes=scratch,
         compiler_params=params(),
         name=name,
-    )(*ins)
+    )(*ins, *after)
+
+
+def hbm(x):
+    return pltpu.with_memory_space_constraint(x, pltpu.HBM)
+
+
+def vmem(x):
+    return pltpu.with_memory_space_constraint(x, pltpu.VMEM)
 
 
 def f32(*shape):
@@ -422,13 +424,12 @@
     chips = n_ctx // 2
     groups = channels // GROUP
     chunks = block // CHUNK
-    tall = channels // LANES
-    rows = modes * tall
+    rows = modes * channels // LANES
     half = rows // 2
     part = half // chips
     halves = modes // 2
 
-    k_in, v_in, q_in, g_in = (x.reshape(block, channels) for x in (k_proj, v_proj, q_proj, out_grad))
+    k_in, v_in, q_in, g_in = (hbm(x.reshape(block, channels)) for x in (k_proj, v_proj, q_proj, out_grad))
     row_scratch = pltpu.VMEM((block * SUBS, LANES), F32)
     mode_scratch = pltpu.VMEM((modes, SUBS, LANES), F32)
     flat_scratch = pltpu.VMEM((modes * SUBS, LANES), F32)
@@ -437,10 +438,10 @@
     def specs(at):
         return (
             pl.BlockSpec((block, GROUP), lambda i: (0, at(i))),
-            pl.BlockSpec((modes, SUBS, LANES), lambda i: (0, at(i), 0)),
+            pl.BlockSpec((1, modes, SUBS, LANES), lambda i: (at(i), 0, 0, 0)),
             pl.BlockSpec((modes, GROUP), lambda i: (0, at(i))),
-            pl.BlockSpec((chunks, modes, SUBS, LANES), lambda i: (0, 0, at(i), 0)),
-            lambda count: pl.BlockSpec((count, halves, SUBS, LANES), lambda i: (0, 0, at(i), 0)),
+            pl.BlockSpec((1, chunks, modes, SUBS, LANES), lambda i: (at(i), 0, 0, 0, 0)),
+            lambda count: pl.BlockSpec((count, 1, halves, SUBS, LANES), lambda i: (0, at(i), 0, 0, 0)),
         )
 
     wide, slim, natural, chunked, halved = specs(lambda i: i)
@@ -450,18 +451,17 @@
         in_specs=[wide] * 4 + [natural],
         out_specs=[chunked, chunked, slim, halved(7), halved(6)],
         out_shape=[
-            jax.ShapeDtypeStruct((chunks, modes, tall, LANES), F32),
-            jax.ShapeDtypeStruct((chunks, modes, tall, LANES), F32),
-            jax.ShapeDtypeStruct((modes, tall, LANES), F32),
-            jax.ShapeDtypeStruct((7, halves, tall, LANES), F32),
-            jax.ShapeDtypeStruct((6, halves, tall, LANES), F32),
+            pltpu.VMEM((groups, chunks, modes, SUBS, LANES), F32),
+            pltpu.VMEM((groups, chunks, modes, SUBS, LANES), F32),
+            pltpu.HBM((groups, modes, SUBS, LANES), F32),
+            pltpu.VMEM((7, groups, halves, SUBS, LANES), F32),
+            pltpu.VMEM((6, groups, halves, SUBS, LANES), F32),
         ],
         scratch_shapes=[row_scratch] * 2 + [flat_scratch] + [mode_scratch] * 11 + [tap_scratch],
         compiler_params=params(BIG),
         name="block_stats",
-    )(k_in, v_in, q_in, g_in, pole_decay)
-
-    rate_rows = rate.reshape(rows, LANES)
+    )(k_in, v_in, q_in, g_in, hbm(pole_decay))
+
     kept = kept.reshape(7, half, LANES)
     send = send.reshape(6, half, LANES)
 
@@ -487,33 +487,33 @@
         grid=(groups,),
         in_specs=[wide] * 4 + [slim, natural] + [chunked] * 2 + [pl.BlockSpec(memory_space=pl.ANY)],
         out_specs=[columns] * 2 + [pl.BlockSpec((1, LANES), lambda i: (0, 0))],
-        out_shape=[f32(groups, block, SUBS, LANES)] * 2 + [f32(1, LANES)],
+        out_shape=[pltpu.VMEM((groups, block, SUBS, LANES), F32)] * 2 + [pltpu.HBM((1, LANES), F32)],
         scratch_shapes=[row_scratch] * 2 + [flat_scratch] + [mode_scratch] * 5 + [tap_scratch],
         compiler_params=params(BIG),
         cost_estimate=pl.CostEstimate(flops=10_000_000_000, bytes_accessed=20_000_000, transcendentals=0),
         name="local_outputs",
-    )(k_in, v_in, q_in, g_in, rate, residue, ends, heads, rate_part)
+    )(k_in, v_in, q_in, g_in, hbm(rate), hbm(residue), vmem(ends), vmem(heads), rate_part)
     scanned = small_call(
         partial(scan_kernel, float(block), chips),
         "row_scan",
-        [group_doc, rate_part, zeros, *swap_chips(pieces)],
+        [group_doc, rate_part, *swap_chips(pieces)],
         [f32(2, part, LANES)] * (chips + 1),
         [pltpu.VMEM((chips, 6, part, LANES), F32), pltpu.VMEM((chips, 2, part, LANES), F32)],
+        after=[hbm(zeros)],
     )
-    total, reach, outs, done = scanned[chips], 1, [], 0
-    arrived = swap_chips(scanned[:chips])
-    if n_dp > 2:
-        total = total + lax.ppermute(total, "dp", [(i, i ^ reach) for i in range(n_dp)])
-        reach *= 2
+    total = scanned[chips]
+    for away in [lax.ppermute(total, "dp", [(i, i ^ away) for i in range(n_dp)]) for away in range(1, n_dp)]:
+        total = total + away
     mine, give = small_call(
         partial(expand_kernel, float(block), chips),
         "block_edges",
-        [group_doc, kept, got, total, *arrived],
+        [group_doc, kept, got, *swap_chips(scanned[:chips])],
         [f32(2, half, LANES)] * 2,
         [pltpu.VMEM((2, half, LANES), F32)],
     )
     theirs = swap_core(give)
-    edges = [x.reshape(2, halves, tall, LANES) for x in (mine, theirs)]
+
+    edges = [x.reshape(2, groups, halves, SUBS, LANES) for x in (mine, theirs)]
 
     def outputs(first, count, after, outs):
         wide, slim, natural, chunked, halved = specs(lambda i: i + first)
@@ -524,34 +524,28 @@
             in_specs=[wide] * 4 + [slim, natural] + [columns] * 2 + [halved(2)] * 2
             + [pl.BlockSpec(memory_space=pl.ANY)] * (1 + len(outs)),
             out_specs=[wide] * 4 + [pl.BlockSpec((1, LANES), lambda i: (0, 0))],
-            out_shape=[jax.ShapeDtypeStruct((block, channels), jnp.bfloat16)] * 4 + [f32(1, LANES)],
+            out_shape=[pltpu.HBM((block, channels), jnp.bfloat16)] * 4 + [pltpu.HBM((1, LANES), F32)],
             input_output_aliases={11 + i: i for i in range(len(outs))},
             scratch_shapes=[row_scratch] * 2 + [flat_scratch] + [mode_scratch] * 3,
             compiler_params=params(BIG),
             cost_estimate=pl.CostEstimate(
-                flops=2_000_000_000 * count, bytes_accessed=5_000_000 * count, transcendentals=0
+                flops=100_000_000 * count, bytes_accessed=500_000 * count, transcendentals=0
             ),
             name="outputs",
-        )(k_in, v_in, q_in, g_in, rate, residue, z_local, w_local, *edges, after, *outs)
+        )(k_in, v_in, q_in, g_in, hbm(rate), hbm(residue), vmem(z_local), vmem(w_local), *edges, after, *outs)
         return result[:4], result[4]
 
-    while reach < n_dp:
-        other = lax.ppermute(total, "dp", [(i, i ^ reach) for i in range(n_dp)])
-        reach *= 2
-        if reach >= n_dp and groups > 1:
-            done = groups // 2
-            outs, zeros = outputs(0, done, total, outs)
-            other = other + zeros
-        total = total + other
     sums = swap_chips([total] * chips)
-    outs, zeros = outputs(done, groups - done, total, outs)
+    outs, zeros = outputs(0, (groups + 1) // 2, total, [])
     (gathered,) = small_call(
-        partial(gather_kernel, chips), "gather_sums", [zeros, *sums], [f32(2, half, LANES)], []
+        partial(gather_kernel, chips), "gather_sums", sums, [f32(2, half, LANES)], [], after=[hbm(zeros)]
     )
+    if groups > 1:
+        outs, _ = outputs((groups + 1) // 2, groups // 2, gathered, outs)
     residue_grad, pole_grad = small_call(
         partial(final_kernel, 1.0 / math.sqrt(total_tokens)),
         "parameter_grads",
-        [rate_rows, residue, gathered, swap_core(gathered)],
+        [rate, residue, gathered, swap_core(gathered)],
         [f32(modes, channels)] * 2,
         [pltpu.VMEM((2, rows, LANES), F32)] + [flat_scratch] * 2,
     )

time: 73 us -> 60.7 us (0.83)
  local copies, waits for them, and re-layouts: 5.32 us -> 0.01 us
  waiting for transfers between devices: 7.47 us -> 3.49 us
  Pallas kernels: 40.7 us -> 37.1 us
  starting transfers between devices: 17.2 us -> 19.1 us
  other arithmetic: 0.86 us -> 0.02 us
    unnamed x28 -> x6, local copies, waits for them, and re-layouts: 5.32 us -> 0.01 us
    ppermute x9, waiting for transfers between devices: 3.2 us -> 0.33 us  [swap_chips(): lax.ppermute(xs[away], 'ctx', [(i, i ^ 2 * away) for i in range(n_ctx)])]
    pallas_call x1, Pallas kernels: 11.3 us -> 9.27 us  [body(): pl.pallas_call(local_kernel, grid=(groups,), in_specs=[wide] * 4 + [slim,...]
    ppermute x3, starting transfers between devices: 4.41 us -> 6.22 us  [swap_core(): return lax.ppermute(x, 'ctx', [(i, i ^ 1) for i in range(n_ctx)])]
    ppermute x3, waiting for transfers between devices: 3.6 us -> 2.23 us  [swap_core(): return lax.ppermute(x, 'ctx', [(i, i ^ 1) for i in range(n_ctx)])]
    add x2 -> x1, other arithmetic: 0.86 us -> 0.02 us  [body(): total = total + away]
    pallas_call x2, Pallas kernels: 11 us -> 10.2 us  [outputs(): pl.pallas_call(partial(output_kernel, len(outs)), grid=(count,), in_specs...]
    pallas_call x1, Pallas kernels: 15 us -> 14.2 us  [body(): pl.pallas_call(partial(stats_kernel, float(row_len)), grid=(groups,), in_...]
  transfers between devices with their start and end apart: 14 -> 15, of which waited for: 5 -> 3; matrix products, arithmetic and copies ran while one was open for 0% -> 0% of each run, Pallas kernels for 31% -> 33%
where the time goes in v2:
time: 60.7 us; the launch traced here: 60.4 us
  Pallas kernels  37.1 us (61%)
  starting transfers between devices  19.1 us (31%)
  waiting for transfers between devices  3.49 us (6%)
  between operations  0.73 us (1%)
    pallas_call x1, Pallas kernels, body(): pl.pallas_call(partial(stats_kernel, float(row_len)), grid=(groups,), in_...  14.2 us
    pallas_call x2, Pallas kernels, outputs(): pl.pallas_call(partial(output_kernel, len(outs)), grid=(count,), in_specs...  10.2 us
    pallas_call x1, Pallas kernels, body(): pl.pallas_call(local_kernel, grid=(groups,), in_specs=[wide] * 4 + [slim,...  9.27 us
    ppermute x9, starting transfers between devices, swap_chips(): lax.ppermute(xs[away], 'ctx', [(i, i ^ 2 * away) for i in range(n_ctx)])  9.1 us
    ppermute x3, starting transfers between devices, swap_core(): return lax.ppermute(x, 'ctx', [(i, i ^ 1) for i in range(n_ctx)])  6.22 us
    ppermute x3, starting transfers between devices, body(): lax.ppermute(total, 'dp', [(i, i ^ away) for i in range(n_dp)])  3.78 us
    pallas_call x5, Pallas kernels, small_call(): pl.pallas_call(kernel, grid=(1,), in_specs=[scalar_spec() if x.dtype == j...  3.43 us
    ppermute x3, waiting for transfers between devices, swap_core(): return lax.ppermute(x, 'ctx', [(i, i ^ 1) for i in range(n_ctx)])  2.23 us
  transfers between devices with their start and end apart: 15, of which 3 were waited for; matrix products, arithmetic and copies ran while one was open for 0% of the time, Pallas kernels for 33%

profile of v2, /device:TPU:1, one launch (start us, length us, event | category | flops | bytes accessed | tf_op | source)
XLA Modules:
  0.0 60.4 jit_solution(13745080676553717469)
XLA Ops:
  0.6 14.2 %block_stats.1 = (f32[4,16,16,8,128]{4,3,2,1,0:T(8,128)S(1)}, f32[4,16,16,8,128]{4,3,2,1,0:T(8,128)S(1)}, f32[4,16,8,128]{3,2,1,0:T(8,128)}, f32[7,4,8,8,128]{4,3,2,1,0:T(8,128)S(1)}, f32[6,4,8,8,128]{4,3,2,1,0:T(8,128)S(1)}) custom-call(bf16[128,4096]{1,0:T(8,128)(2,1)} %bitcast.19, bf16[128,4096]{1,0:T(8,128)(2,1)} %bitcast.23, ...), custom_call_target="tpu_custom_call" | custom-call | tf_op jit(solution)/shard_map/block_stats/pallas_call | solution.py:448
  14.8 0.1 collective-permute-start
  14.9 2.2 %collective-permute-done.got_ref = f32[6,256,128]{2,1,0:T(8,128)S(1)} collective-permute-done((f32[6,256,128]{2,1,0:T(8,128)S(1)}, f32[6,256,128]{2,1,0:T(8,128)S(1)}, u32[]{:S(2)}, u32[]{:S(2)}) %collective-permute-start) | collective-permute-done | bytes 786464 | tf_op jit(solution)/shard_map/ppermute | solution.py:469
  17.1 1.0 %chip_stats.1 = (f32[6,64,128]{2,1,0:T(8,128)S(1)}, f32[6,64,128]{2,1,0:T(8,128)S(1)}, f32[6,64,128]{2,1,0:T(8,128)S(1)}, f32[6,64,128]{2,1,0:T(8,128)S(1)}, f32[64,128]{1,0:T(8,128)S(1)}) custom-call(s32[1,8]{1,0:T(1,128)S(1)} %copy-done.2, f32[7,256,128]{2,1,0:T(8,128)S(1)} %bitcast.12, f32[6,256,128]{2,1,0:T(8,128)S(1)} %collective-permute-done.got_ref), custom_call_target="tpu_custom_call" | custom-call | tf_op jit(solution)/shard_map/chip_stats/pallas_call | solution.py:386
  18.1 2.4 %collective-permute-start.1 = (f32[6,64,128]{2,1,0:T(8,128)S(1)}, f32[6,64,128]{2,1,0:T(8,128)S(1)}, u32[]{:S(2)}, u32[]{:S(2)}) collective-permute-start(f32[6,64,128]{2,1,0:T(8,128)S(1)} %get-tuple-element.46), channel_id=1, source_target_pairs={{0,2},{1,3},{2,0},{3,1},{4,6},{5,7},{6,4},{7,5},{8,10},{9,11},{10,... | collective-permute-start | bytes 589832 | tf_op jit(solution)/shard_map/ppermute | solution.py:473
  20.5 1.2 %collective-permute-start.2 = (f32[6,64,128]{2,1,0:T(8,128)S(1)}, f32[6,64,128]{2,1,0:T(8,128)S(1)}, u32[]{:S(2)}, u32[]{:S(2)}) collective-permute-start(f32[6,64,128]{2,1,0:T(8,128)S(1)} %get-tuple-element.47), channel_id=1, source_target_pairs={{0,4},{1,5},{2,6},{3,7},{4,0},{5,1},{6,2},{7,3},{8,12},{9,13},{10,... | collective-permute-start | bytes 589832 | tf_op jit(solution)/shard_map/ppermute | solution.py:473
  21.7 0.0 collective-permute-start.3
  21.7 9.3 %local_outputs.1 = (f32[4,128,8,128]{3,2,1,0:T(8,128)S(1)}, f32[4,128,8,128]{3,2,1,0:T(8,128)S(1)}, f32[1,128]{1,0:T(1,128)}) custom-call(bf16[128,4096]{1,0:T(8,128)(2,1)} %bitcast.20, bf16[128,4096]{1,0:T(8,128)(2,1)} %bitcast.24, bf16[128,4096]{1,0:T(8,128)(2,1)} %bitcast.28, bf16[128,4096]{1,0:T(8,128)(2,1)} %bitcast.32, ...), custom_call_target="tpu_custom_call" | custom-call | flops 10000000000 | bytes 20000000 | tf_op jit(solution)/shard_map/local_outputs/pallas_call | solution.py:485
  31.0 0.7 %row_scan.1 = (f32[2,64,128]{2,1,0:T(8,128)S(1)}, f32[2,64,128]{2,1,0:T(8,128)S(1)}, f32[2,64,128]{2,1,0:T(8,128)S(1)}, f32[2,64,128]{2,1,0:T(8,128)S(1)}, f32[2,64,128]{2,1,0:T(8,128)S(1)}) custom-call(s32[1,8]{1,0:T(1,128)S(1)} %copy-done.2, f32[64,128]{1,0:T(8,128)S(1)} %get-tuple-element.42.after_ref.rate_ref, ...), custom_call_target="tpu_custom_call" | custom-call | tf_op jit(solution)/shard_map/row_scan/pallas_call | solution.py:386
  31.8 1.5 %collective-permute-start.4 = (f32[2,64,128]{2,1,0:T(8,128)S(1)}, f32[2,64,128]{2,1,0:T(8,128)S(1)}, u32[]{:S(2)}, u32[]{:S(2)}) collective-permute-start(f32[2,64,128]{2,1,0:T(8,128)S(1)} %get-tuple-element.51), channel_id=1, source_target_pairs={{0,2},{1,3},{2,0},{3,1},{4,6},{5,7},{6,4},{7,5},{8,10},{9,11},{10,... | collective-permute-start | bytes 196616 | tf_op jit(solution)/shard_map/ppermute | solution.py:473
  33.2 1.2 %collective-permute-start.5 = (f32[2,64,128]{2,1,0:T(8,128)S(1)}, f32[2,64,128]{2,1,0:T(8,128)S(1)}, u32[]{:S(2)}, u32[]{:S(2)}) collective-permute-start(f32[2,64,128]{2,1,0:T(8,128)S(1)} %get-tuple-element.52), channel_id=1, source_target_pairs={{0,4},{1,5},{2,6},{3,7},{4,0},{5,1},{6,2},{7,3},{8,12},{9,13},{10,... | collective-permute-start | bytes 196616 | tf_op jit(solution)/shard_map/ppermute | solution.py:473
  34.5 3.5 %collective-permute-start.10 = (f32[2,64,128]{2,1,0:T(8,128)S(1)}, f32[2,64,128]{2,1,0:T(8,128)S(1)}, u32[]{:S(2)}, u32[]{:S(2)}) collective-permute-start(f32[2,64,128]{2,1,0:T(8,128)S(1)} %get-tuple-element.56), channel_id=1, source_target_pairs={{0,24},{8,16},{16,8},{24,0},{1,25},{9,17},{17,9},{25,1},{2,26},{10... | collective-permute-start | bytes 196616 | tf_op jit(solution)/shard_map/ppermute | solution.py:505
  38.0 0.3 collective-permute-start.8
  38.3 0.3 collective-permute-done.6.refs_3_
  38.6 0.7 %block_edges.1 = (f32[2,256,128]{2,1,0:T(8,128)S(1)}, f32[2,256,128]{2,1,0:T(8,128)S(1)}) custom-call(s32[1,8]{1,0:T(1,128)S(1)} %copy-done.2, f32[7,256,128]{2,1,0:T(8,128)S(1)} %bitcast.13, f32[6,256,128]{2,1,0:T(8,128)S(1)} %collective-permute-done.got_ref, f32[2,64,128]{2,1,0:T(8,128)S(1)} %get-tuple-element.50.refs_0_, ...), custom_call_target="tpu_custom_call" | custom-call | tf_op jit(solution)/shard_map/block_edges/pallas_call | solution.py:386
  39.3 2.9 %collective-permute-start.7 = (f32[2,256,128]{2,1,0:T(8,128)S(1)}, f32[2,256,128]{2,1,0:T(8,128)S(1)}, u32[]{:S(2)}, u32[]{:S(2)}) collective-permute-start(f32[2,256,128]{2,1,0:T(8,128)S(1)} %get-tuple-element.55), channel_id=1, source_target_pairs={{0,1},{1,0},{2,3},{3,2},{4,5},{5,4},{6,7},{7,6},{8,9},{9,8},{10,11... | collective-permute-start | bytes 786440 | tf_op jit(solution)/shard_map/ppermute | solution.py:469
  42.2 0.9 %collective-permute-done.9 = f32[2,64,128]{2,1,0:T(8,128)S(1)} collective-permute-done((f32[2,64,128]{2,1,0:T(8,128)S(1)}, f32[2,64,128]{2,1,0:T(8,128)S(1)}, u32[]{:S(2)}, u32[]{:S(2)}) %collective-permute-start.9) | collective-permute-done | bytes 65568 | tf_op jit(solution)/shard_map/ppermute | solution.py:505
  43.1 2.2 %collective-permute-start.13 = (f32[2,64,128]{2,1,0:T(8,128)S(1)}, f32[2,64,128]{2,1,0:T(8,128)S(1)}, u32[]{:S(2)}, u32[]{:S(2)}) collective-permute-start(f32[2,64,128]{2,1,0:T(8,128)S(1)} %add_add_fusion.after_ref.refs_0_), channel_id=1, source_target_pairs={{0,6},{1,7},{2,4},{3,5},{4,2},{5,3},{6,0},{7,1},{8,14},{9,15},{10,... | collective-permute-start | bytes 196616 | tf_op jit(solution)/shard_map/ppermute | solution.py:473
  45.4 0.2 collective-permute-start.12
  45.6 0.3 collective-permute-start.11
  45.8 5.1 %outputs.2 = (bf16[128,4096]{1,0:T(8,128)(2,1)}, bf16[128,4096]{1,0:T(8,128)(2,1)}, bf16[128,4096]{1,0:T(8,128)(2,1)}, bf16[128,4096]{1,0:T(8,128)(2,1)}, f32[1,128]{1,0:T(1,128)}) custom-call(bf16[128,4096]{1,0:T(8,128)(2,1)} %bitcast.21, bf16[128,4096]{1,0:T(8,128)(2,1)} %bitcast.25, bf16[128,4096]{1,0:T(8,128)(2,1)} %bitcast.29, ...), custom_call_target="tpu_custom_call" | custom-call | flops 200000000 | bytes 1000000 | tf_op jit(solution)/shard_map/outputs/pallas_call | solution.py:521
  51.0 3.3 %collective-permute-start.14 = (f32[2,256,128]{2,1,0:T(8,128)S(1)}, f32[2,256,128]{2,1,0:T(8,128)S(1)}, u32[]{:S(2)}, u32[]{:S(2)}) collective-permute-start(f32[2,256,128]{2,1,0:T(8,128)S(1)} %gather_sums.1.after_ref.kept_ref), channel_id=1, source_target_pairs={{0,1},{1,0},{2,3},{3,2},{4,5},{5,4},{6,7},{7,6},{8,9},{9,8},{10,11... | collective-permute-start | bytes 786440 | tf_op jit(solution)/shard_map/ppermute | solution.py:469
  54.3 5.1 %outputs.3 = (bf16[128,4096]{1,0:T(8,128)(2,1)}, bf16[128,4096]{1,0:T(8,128)(2,1)}, bf16[128,4096]{1,0:T(8,128)(2,1)}, bf16[128,4096]{1,0:T(8,128)(2,1)}, f32[1,128]{1,0:T(1,128)}) custom-call(bf16[128,4096]{1,0:T(8,128)(2,1)} %bitcast.22, bf16[128,4096]{1,0:T(8,128)(2,1)} %bitcast.26, ...), custom_call_target="tpu_custom_call", output_to_operand_aliasing={{0}: (11, {}), {1}: (12, {}), {2}: (13, {}), {3}: (14, {})} | custom-call | flops 200000000 | bytes 1000000 | tf_op jit(solution)/shard_map/outputs/pallas_call | solution.py:521
  59.4 1.0 %parameter_grads.1 = (f32[16,4096]{1,0:T(8,128)}, f32[16,4096]{1,0:T(8,128)}) custom-call(f32[4,16,8,128]{3,2,1,0:T(8,128)S(1)} %copy-done.1, f32[16,4096]{1,0:T(8,128)S(1)} %copy-done, f32[2,256,128]{2,1,0:T(8,128)S(1)} %gather_sums.1.after_ref.kept_ref, f32[2,256,128]{2,1,0:T(8,128)S(1)} %collective-permute-done.14.got_ref), custom_call_target="tpu_custom_call" | custom-call | tf_op jit(solution)/shard_map/parameter_grads/pallas_call | solution.py:386
  (22 shorter events, 0.1 us)
Async XLA Ops:
  0.6 16.5 %copy-start.2 = (s32[1,8]{1,0:T(1,128)S(1)}, s32[1,8]{1,0:T(1,128)}, u32[]{:S(2)}) copy-start(s32[1,8]{1,0:T(1,128)} %doc_ref.5) | copy-start | bytes 100
  14.8 2.3 %collective-permute-start = (f32[6,256,128]{2,1,0:T(8,128)S(1)}, f32[6,256,128]{2,1,0:T(8,128)S(1)}, u32[]{:S(2)}, u32[]{:S(2)}) collective-permute-start(f32[6,256,128]{2,1,0:T(8,128)S(1)} %bitcast.18), channel_id=1, source_target_pairs={{0,1},{1,0},{2,3},{3,2},{4,5},{5,4},{6,7},{7,6},{8,9},{9,8},{10,11... | collective-permute-start | bytes 2359304 | tf_op jit(solution)/shard_map/ppermute | solution.py:469
  18.1 12.9 %collective-permute-start.1 = (f32[6,64,128]{2,1,0:T(8,128)S(1)}, f32[6,64,128]{2,1,0:T(8,128)S(1)}, u32[]{:S(2)}, u32[]{:S(2)}) collective-permute-start(f32[6,64,128]{2,1,0:T(8,128)S(1)} %get-tuple-element.46), channel_id=1, source_target_pairs={{0,2},{1,3},{2,0},{3,1},{4,6},{5,7},{6,4},{7,5},{8,10},{9,11},{10,... | collective-permute-start | bytes 589832 | tf_op jit(solution)/shard_map/ppermute | solution.py:473
  20.5 10.5 %collective-permute-start.2 = (f32[6,64,128]{2,1,0:T(8,128)S(1)}, f32[6,64,128]{2,1,0:T(8,128)S(1)}, u32[]{:S(2)}, u32[]{:S(2)}) collective-permute-start(f32[6,64,128]{2,1,0:T(8,128)S(1)} %get-tuple-element.47), channel_id=1, source_target_pairs={{0,4},{1,5},{2,6},{3,7},{4,0},{5,1},{6,2},{7,3},{8,12},{9,13},{10,... | collective-permute-start | bytes 589832 | tf_op jit(solution)/shard_map/ppermute | solution.py:473
  21.7 9.3 %collective-permute-start.3 = (f32[6,64,128]{2,1,0:T(8,128)S(1)}, f32[6,64,128]{2,1,0:T(8,128)S(1)}, u32[]{:S(2)}, u32[]{:S(2)}) collective-permute-start(f32[6,64,128]{2,1,0:T(8,128)S(1)} %get-tuple-element.48), channel_id=1, source_target_pairs={{0,6},{1,7},{2,4},{3,5},{4,2},{5,3},{6,0},{7,1},{8,14},{9,15},{10,... | collective-permute-start | bytes 589832 | tf_op jit(solution)/shard_map/ppermute | solution.py:473
  31.8 6.2 %collective-permute-start.4 = (f32[2,64,128]{2,1,0:T(8,128)S(1)}, f32[2,64,128]{2,1,0:T(8,128)S(1)}, u32[]{:S(2)}, u32[]{:S(2)}) collective-permute-start(f32[2,64,128]{2,1,0:T(8,128)S(1)} %get-tuple-element.51), channel_id=1, source_target_pairs={{0,2},{1,3},{2,0},{3,1},{4,6},{5,7},{6,4},{7,5},{8,10},{9,11},{10,... | collective-permute-start | bytes 196616 | tf_op jit(solution)/shard_map/ppermute | solution.py:473
  33.2 5.1 %collective-permute-start.5 = (f32[2,64,128]{2,1,0:T(8,128)S(1)}, f32[2,64,128]{2,1,0:T(8,128)S(1)}, u32[]{:S(2)}, u32[]{:S(2)}) collective-permute-start(f32[2,64,128]{2,1,0:T(8,128)S(1)} %get-tuple-element.52), channel_id=1, source_target_pairs={{0,4},{1,5},{2,6},{3,7},{4,0},{5,1},{6,2},{7,3},{8,12},{9,13},{10,... | collective-permute-start | bytes 196616 | tf_op jit(solution)/shard_map/ppermute | solution.py:473
  34.5 4.1 %collective-permute-start.6 = (f32[2,64,128]{2,1,0:T(8,128)S(1)}, f32[2,64,128]{2,1,0:T(8,128)S(1)}, u32[]{:S(2)}, u32[]{:S(2)}) collective-permute-start(f32[2,64,128]{2,1,0:T(8,128)S(1)} %get-tuple-element.53), channel_id=1, source_target_pairs={{0,6},{1,7},{2,4},{3,5},{4,2},{5,3},{6,0},{7,1},{8,14},{9,15},{10,... | collective-permute-start | bytes 196616 | tf_op jit(solution)/shard_map/ppermute | solution.py:473
  34.5 7.7 %collective-permute-start.10 = (f32[2,64,128]{2,1,0:T(8,128)S(1)}, f32[2,64,128]{2,1,0:T(8,128)S(1)}, u32[]{:S(2)}, u32[]{:S(2)}) collective-permute-start(f32[2,64,128]{2,1,0:T(8,128)S(1)} %get-tuple-element.56), channel_id=1, source_target_pairs={{0,24},{8,16},{16,8},{24,0},{1,25},{9,17},{17,9},{25,1},{2,26},{10... | collective-permute-start | bytes 196616 | tf_op jit(solution)/shard_map/ppermute | solution.py:505
  38.0 5.1 %collective-permute-start.9 = (f32[2,64,128]{2,1,0:T(8,128)S(1)}, f32[2,64,128]{2,1,0:T(8,128)S(1)}, u32[]{:S(2)}, u32[]{:S(2)}) collective-permute-start(f32[2,64,128]{2,1,0:T(8,128)S(1)} %get-tuple-element.56), channel_id=1, source_target_pairs={{0,16},{8,24},{16,0},{24,8},{1,17},{9,25},{17,1},{25,9},{2,18},{10... | collective-permute-start | bytes 196616 | tf_op jit(solution)/shard_map/ppermute | solution.py:505
  38.0 5.1 %collective-permute-start.8 = (f32[2,64,128]{2,1,0:T(8,128)S(1)}, f32[2,64,128]{2,1,0:T(8,128)S(1)}, u32[]{:S(2)}, u32[]{:S(2)}) collective-permute-start(f32[2,64,128]{2,1,0:T(8,128)S(1)} %get-tuple-element.56), channel_id=1, source_target_pairs={{0,8},{8,0},{16,24},{24,16},{1,9},{9,1},{17,25},{25,17},{2,10},{10... | collective-permute-start | bytes 196616 | tf_op jit(solution)/shard_map/ppermute | solution.py:505
  39.3 6.6 %collective-permute-start.7 = (f32[2,256,128]{2,1,0:T(8,128)S(1)}, f32[2,256,128]{2,1,0:T(8,128)S(1)}, u32[]{:S(2)}, u32[]{:S(2)}) collective-permute-start(f32[2,256,128]{2,1,0:T(8,128)S(1)} %get-tuple-element.55), channel_id=1, source_target_pairs={{0,1},{1,0},{2,3},{3,2},{4,5},{5,4},{6,7},{7,6},{8,9},{9,8},{10,11... | collective-permute-start | bytes 786440 | tf_op jit(solution)/shard_map/ppermute | solution.py:469
  43.1 7.8 %collective-permute-start.13 = (f32[2,64,128]{2,1,0:T(8,128)S(1)}, f32[2,64,128]{2,1,0:T(8,128)S(1)}, u32[]{:S(2)}, u32[]{:S(2)}) collective-permute-start(f32[2,64,128]{2,1,0:T(8,128)S(1)} %add_add_fusion.after_ref.refs_0_), channel_id=1, source_target_pairs={{0,6},{1,7},{2,4},{3,5},{4,2},{5,3},{6,0},{7,1},{8,14},{9,15},{10,... | collective-permute-start | bytes 196616 | tf_op jit(solution)/shard_map/ppermute | solution.py:473
  45.4 5.6 %collective-permute-start.12 = (f32[2,64,128]{2,1,0:T(8,128)S(1)}, f32[2,64,128]{2,1,0:T(8,128)S(1)}, u32[]{:S(2)}, u32[]{:S(2)}) collective-permute-start(f32[2,64,128]{2,1,0:T(8,128)S(1)} %add_add_fusion.after_ref.refs_0_), channel_id=1, source_target_pairs={{0,4},{1,5},{2,6},{3,7},{4,0},{5,1},{6,2},{7,3},{8,12},{9,13},{10,... | collective-permute-start | bytes 196616 | tf_op jit(solution)/shard_map/ppermute | solution.py:473
  45.6 5.3 %collective-permute-start.11 = (f32[2,64,128]{2,1,0:T(8,128)S(1)}, f32[2,64,128]{2,1,0:T(8,128)S(1)}, u32[]{:S(2)}, u32[]{:S(2)}) collective-permute-start(f32[2,64,128]{2,1,0:T(8,128)S(1)} %add_add_fusion.after_ref.refs_0_), channel_id=1, source_target_pairs={{0,2},{1,3},{2,0},{3,1},{4,6},{5,7},{6,4},{7,5},{8,10},{9,11},{10,... | collective-permute-start | bytes 196616 | tf_op jit(solution)/shard_map/ppermute | solution.py:473
  51.0 8.4 %collective-permute-start.14 = (f32[2,256,128]{2,1,0:T(8,128)S(1)}, f32[2,256,128]{2,1,0:T(8,128)S(1)}, u32[]{:S(2)}, u32[]{:S(2)}) collective-permute-start(f32[2,256,128]{2,1,0:T(8,128)S(1)} %gather_sums.1.after_ref.kept_ref), channel_id=1, source_target_pairs={{0,1},{1,0},{2,3},{3,2},{4,5},{5,4},{6,7},{7,6},{8,9},{9,8},{10,11... | collective-permute-start | bytes 786440 | tf_op jit(solution)/shard_map/ppermute | solution.py:469
  54.3 5.1 %copy-start = (f32[16,4096]{1,0:T(8,128)S(1)}, f32[16,4096]{1,0:T(8,128)}, u32[]{:S(2)}) copy-start(f32[16,4096]{1,0:T(8,128)} %residue_ref.7) | copy-start | bytes 786436
  54.3 5.1 %copy-start.1 = (f32[4,16,8,128]{3,2,1,0:T(8,128)S(1)}, f32[4,16,8,128]{3,2,1,0:T(8,128)}, u32[]{:S(2)}) copy-start(f32[4,16,8,128]{3,2,1,0:T(8,128)} %get-tuple-element.37.rate_ref) | copy-start | bytes 786436

commit v3 on v2

--- a/solution.py
+++ b/solution.py
@@ -429,7 +429,8 @@
     part = half // chips
     halves = modes // 2
 
-    k_in, v_in, q_in, g_in = (hbm(x.reshape(block, channels)) for x in (k_proj, v_proj, q_proj, out_grad))
+    tokens = [x.reshape(block, channels) for x in (k_proj, v_proj, q_proj, out_grad)]
+    k_in, v_in, q_in, g_in = (hbm(x) for x in tokens)
     row_scratch = pltpu.VMEM((block * SUBS, LANES), F32)
     mode_scratch = pltpu.VMEM((modes, SUBS, LANES), F32)
     flat_scratch = pltpu.VMEM((modes * SUBS, LANES), F32)
@@ -453,7 +454,7 @@
         out_shape=[
             pltpu.VMEM((groups, chunks, modes, SUBS, LANES), F32),
             pltpu.VMEM((groups, chunks, modes, SUBS, LANES), F32),
-            pltpu.HBM((groups, modes, SUBS, LANES), F32),
+            pltpu.VMEM((groups, modes, SUBS, LANES), F32),
             pltpu.VMEM((7, groups, halves, SUBS, LANES), F32),
             pltpu.VMEM((6, groups, halves, SUBS, LANES), F32),
         ],
@@ -487,23 +488,23 @@
         grid=(groups,),
         in_specs=[wide] * 4 + [slim, natural] + [chunked] * 2 + [pl.BlockSpec(memory_space=pl.ANY)],
         out_specs=[columns] * 2 + [pl.BlockSpec((1, LANES), lambda i: (0, 0))],
-        out_shape=[pltpu.VMEM((groups, block, SUBS, LANES), F32)] * 2 + [pltpu.HBM((1, LANES), F32)],
+        out_shape=[pltpu.VMEM((groups, block, SUBS, LANES), F32)] * 2 + [pltpu.VMEM((1, LANES), F32)],
         scratch_shapes=[row_scratch] * 2 + [flat_scratch] + [mode_scratch] * 5 + [tap_scratch],
         compiler_params=params(BIG),
         cost_estimate=pl.CostEstimate(flops=10_000_000_000, bytes_accessed=20_000_000, transcendentals=0),
         name="local_outputs",
-    )(k_in, v_in, q_in, g_in, hbm(rate), hbm(residue), vmem(ends), vmem(heads), rate_part)
+    )(k_in, v_in, q_in, g_in, vmem(rate), hbm(residue), vmem(ends), vmem(heads), rate_part)
     scanned = small_call(
         partial(scan_kernel, float(block), chips),
         "row_scan",
         [group_doc, rate_part, *swap_chips(pieces)],
         [f32(2, part, LANES)] * (chips + 1),
         [pltpu.VMEM((chips, 6, part, LANES), F32), pltpu.VMEM((chips, 2, part, LANES), F32)],
-        after=[hbm(zeros)],
+        after=[zeros],
     )
     total = scanned[chips]
-    for away in [lax.ppermute(total, "dp", [(i, i ^ away) for i in range(n_dp)]) for away in range(1, n_dp)]:
-        total = total + away
+    for other in [lax.ppermute(total, "dp", [(i, i ^ away) for i in range(n_dp)]) for away in range(1, n_dp)]:
+        total = total + other
     mine, give = small_call(
         partial(expand_kernel, float(block), chips),
         "block_edges",
@@ -514,6 +515,8 @@
     theirs = swap_core(give)
 
     edges = [x.reshape(2, groups, halves, SUBS, LANES) for x in (mine, theirs)]
+
+    held = [vmem(x) for x in (*tokens, rate, residue)]
 
     def outputs(first, count, after, outs):
         wide, slim, natural, chunked, halved = specs(lambda i: i + first)
@@ -524,7 +527,7 @@
             in_specs=[wide] * 4 + [slim, natural] + [columns] * 2 + [halved(2)] * 2
             + [pl.BlockSpec(memory_space=pl.ANY)] * (1 + len(outs)),
             out_specs=[wide] * 4 + [pl.BlockSpec((1, LANES), lambda i: (0, 0))],
-            out_shape=[pltpu.HBM((block, channels), jnp.bfloat16)] * 4 + [pltpu.HBM((1, LANES), F32)],
+            out_shape=[pltpu.HBM((block, channels), jnp.bfloat16)] * 4 + [pltpu.VMEM((1, LANES), F32)],
             input_output_aliases={11 + i: i for i in range(len(outs))},
             scratch_shapes=[row_scratch] * 2 + [flat_scratch] + [mode_scratch] * 3,
             compiler_params=params(BIG),
@@ -532,16 +535,17 @@
                 flops=100_000_000 * count, bytes_accessed=500_000 * count, transcendentals=0
             ),
             name="outputs",
-        )(k_in, v_in, q_in, g_in, hbm(rate), hbm(residue), vmem(z_local), vmem(w_local), *edges, after, *outs)
+        )(*held, vmem(z_local), vmem(w_local), *edges, after, *outs)
         return result[:4], result[4]
 
     sums = swap_chips([total] * chips)
-    outs, zeros = outputs(0, (groups + 1) // 2, total, [])
+    cut = (3 * groups + 3) // 4
+    outs, zeros = outputs(0, cut, total, [])
     (gathered,) = small_call(
-        partial(gather_kernel, chips), "gather_sums", sums, [f32(2, half, LANES)], [], after=[hbm(zeros)]
+        partial(gather_kernel, chips), "gather_sums", sums, [f32(2, half, LANES)], [], after=[zeros]
     )
-    if groups > 1:
-        outs, _ = outputs((groups + 1) // 2, groups // 2, gathered, outs)
+    if cut < groups:
+        outs, _ = outputs(cut, groups - cut, gathered, outs)
     residue_grad, pole_grad = small_call(
         partial(final_kernel, 1.0 / math.sqrt(total_tokens)),
         "parameter_grads",

time: 60.7 us -> 57.8 us (0.952)
  Pallas kernels: 37.1 us -> 34.2 us
    pallas_call x2, Pallas kernels: 10.2 us -> 8.17 us  [outputs(): pl.pallas_call(partial(output_kernel, len(outs)), grid=(count,), in_specs...]
  transfers between devices with their start and end apart: 15 -> 15, of which waited for: 3 -> 3; matrix products, arithmetic and copies ran while one was open for 0% -> 0% of each run, Pallas kernels for 33% -> 31%
where the time goes in v3:
time: 57.8 us; the launch traced here: 57.7 us
  Pallas kernels  34.2 us (59%)
  starting transfers between devices  19.2 us (33%)
  waiting for transfers between devices  3.49 us (6%)
  between operations  0.77 us (1%)
    pallas_call x1, Pallas kernels, body(): pl.pallas_call(partial(stats_kernel, float(row_len)), grid=(groups,), in_...  13.7 us
    ppermute x9, starting transfers between devices, swap_chips(): lax.ppermute(xs[away], 'ctx', [(i, i ^ 2 * away) for i in range(n_ctx)])  9.1 us
    pallas_call x1, Pallas kernels, body(): pl.pallas_call(local_kernel, grid=(groups,), in_specs=[wide] * 4 + [slim,...  8.92 us
    pallas_call x2, Pallas kernels, outputs(): pl.pallas_call(partial(output_kernel, len(outs)), grid=(count,), in_specs...  8.17 us
    ppermute x3, starting transfers between devices, swap_core(): return lax.ppermute(x, 'ctx', [(i, i ^ 1) for i in range(n_ctx)])  6.29 us
    ppermute x3, starting transfers between devices, body(): lax.ppermute(total, 'dp', [(i, i ^ away) for i in range(n_dp)])  3.78 us
    pallas_call x5, Pallas kernels, small_call(): pl.pallas_call(kernel, grid=(1,), in_specs=[scalar_spec() if x.dtype == j...  3.45 us
    ppermute x3, waiting for transfers between devices, swap_core(): return lax.ppermute(x, 'ctx', [(i, i ^ 1) for i in range(n_ctx)])  2.23 us
  transfers between devices with their start and end apart: 15, of which 3 were waited for; matrix products, arithmetic and copies ran while one was open for 0% of the time, Pallas kernels for 31%

profile of v3, /device:TPU:1, one launch (start us, length us, event | category | flops | bytes accessed | tf_op | source)
XLA Modules:
  0.0 57.7 jit_solution(10462900773385577822)
XLA Ops:
  0.6 13.7 %block_stats.1 = (f32[4,16,16,8,128]{4,3,2,1,0:T(8,128)S(1)}, f32[4,16,16,8,128]{4,3,2,1,0:T(8,128)S(1)}, f32[4,16,8,128]{3,2,1,0:T(8,128)S(1)}, f32[7,4,8,8,128...) custom-call(bf16[128,4096]{1,0:T(8,128)(2,1)} %bitcast.12, bf16[128,4096]{1,0:T(8,128)(2,1)} %bitcast.16, ...), custom_call_target="tpu_custom_call" | custom-call | tf_op jit(solution)/shard_map/block_stats/pallas_call | solution.py:449
  14.3 0.1 collective-permute-start
  14.4 2.2 %collective-permute-done.got_ref = f32[6,256,128]{2,1,0:T(8,128)S(1)} collective-permute-done((f32[6,256,128]{2,1,0:T(8,128)S(1)}, f32[6,256,128]{2,1,0:T(8,128)S(1)}, u32[]{:S(2)}, u32[]{:S(2)}) %collective-permute-start) | collective-permute-done | bytes 786464 | tf_op jit(solution)/shard_map/ppermute | solution.py:470
  16.7 1.0 %chip_stats.1 = (f32[6,64,128]{2,1,0:T(8,128)S(1)}, f32[6,64,128]{2,1,0:T(8,128)S(1)}, f32[6,64,128]{2,1,0:T(8,128)S(1)}, f32[6,64,128]{2,1,0:T(8,128)S(1)}, f32[64,128]{1,0:T(8,128)S(1)}) custom-call(s32[1,8]{1,0:T(1,128)S(1)} %copy-done.5, f32[7,256,128]{2,1,0:T(8,128)S(1)} %bitcast.28, f32[6,256,128]{2,1,0:T(8,128)S(1)} %collective-permute-done.got_ref), custom_call_target="tpu_custom_call" | custom-call | tf_op jit(solution)/shard_map/chip_stats/pallas_call | solution.py:386
  17.7 2.4 %collective-permute-start.1 = (f32[6,64,128]{2,1,0:T(8,128)S(1)}, f32[6,64,128]{2,1,0:T(8,128)S(1)}, u32[]{:S(2)}, u32[]{:S(2)}) collective-permute-start(f32[6,64,128]{2,1,0:T(8,128)S(1)} %get-tuple-element.46), channel_id=1, source_target_pairs={{0,2},{1,3},{2,0},{3,1},{4,6},{5,7},{6,4},{7,5},{8,10},{9,11},{10,... | collective-permute-start | bytes 589832 | tf_op jit(solution)/shard_map/ppermute | solution.py:474
  20.1 1.2 %collective-permute-start.2 = (f32[6,64,128]{2,1,0:T(8,128)S(1)}, f32[6,64,128]{2,1,0:T(8,128)S(1)}, u32[]{:S(2)}, u32[]{:S(2)}) collective-permute-start(f32[6,64,128]{2,1,0:T(8,128)S(1)} %get-tuple-element.47), channel_id=1, source_target_pairs={{0,4},{1,5},{2,6},{3,7},{4,0},{5,1},{6,2},{7,3},{8,12},{9,13},{10,... | collective-permute-start | bytes 589832 | tf_op jit(solution)/shard_map/ppermute | solution.py:474
  21.3 8.9 %local_outputs.1 = (f32[4,128,8,128]{3,2,1,0:T(8,128)S(1)}, f32[4,128,8,128]{3,2,1,0:T(8,128)S(1)}, f32[1,128]{1,0:T(1,128)S(1)}) custom-call(bf16[128,4096]{1,0:T(8,128)(2,1)} %bitcast.13, bf16[128,4096]{1,0:T(8,128)(2,1)} %bitcast.17, bf16[128,4096]{1,0:T(8,128)(2,1)} %bitcast.21, bf16[128,4096]{1,0:T(8,128)(2,1)} %bitcast.25, ...), custom_call_target="tpu_custom_call" | custom-call | flops 10000000000 | bytes 20000000 | tf_op jit(solution)/shard_map/local_outputs/pallas_call | solution.py:486
  30.3 0.7 %row_scan.1 = (f32[2,64,128]{2,1,0:T(8,128)S(1)}, f32[2,64,128]{2,1,0:T(8,128)S(1)}, f32[2,64,128]{2,1,0:T(8,128)S(1)}, f32[2,64,128]{2,1,0:T(8,128)S(1)}, f32[2,64,128]{2,1,0:T(8,128)S(1)}) custom-call(s32[1,8]{1,0:T(1,128)S(1)} %copy-done.5, f32[64,128]{1,0:T(8,128)S(1)} %get-tuple-element.42.after_ref.rate_ref, ...), custom_call_target="tpu_custom_call" | custom-call | tf_op jit(solution)/shard_map/row_scan/pallas_call | solution.py:386
  31.0 1.5 %collective-permute-start.4 = (f32[2,64,128]{2,1,0:T(8,128)S(1)}, f32[2,64,128]{2,1,0:T(8,128)S(1)}, u32[]{:S(2)}, u32[]{:S(2)}) collective-permute-start(f32[2,64,128]{2,1,0:T(8,128)S(1)} %get-tuple-element.51), channel_id=1, source_target_pairs={{0,2},{1,3},{2,0},{3,1},{4,6},{5,7},{6,4},{7,5},{8,10},{9,11},{10,... | collective-permute-start | bytes 196616 | tf_op jit(solution)/shard_map/ppermute | solution.py:474
  32.5 1.2 %collective-permute-start.5 = (f32[2,64,128]{2,1,0:T(8,128)S(1)}, f32[2,64,128]{2,1,0:T(8,128)S(1)}, u32[]{:S(2)}, u32[]{:S(2)}) collective-permute-start(f32[2,64,128]{2,1,0:T(8,128)S(1)} %get-tuple-element.52), channel_id=1, source_target_pairs={{0,4},{1,5},{2,6},{3,7},{4,0},{5,1},{6,2},{7,3},{8,12},{9,13},{10,... | collective-permute-start | bytes 196616 | tf_op jit(solution)/shard_map/ppermute | solution.py:474
  33.7 0.0 collective-permute-start.6
  33.8 3.5 %collective-permute-start.10 = (f32[2,64,128]{2,1,0:T(8,128)S(1)}, f32[2,64,128]{2,1,0:T(8,128)S(1)}, u32[]{:S(2)}, u32[]{:S(2)}) collective-permute-start(f32[2,64,128]{2,1,0:T(8,128)S(1)} %get-tuple-element.56), channel_id=1, source_target_pairs={{0,24},{8,16},{16,8},{24,0},{1,25},{9,17},{17,9},{25,1},{2,26},{10... | collective-permute-start | bytes 196616 | tf_op jit(solution)/shard_map/ppermute | solution.py:506
  37.3 0.3 collective-permute-start.8
  37.5 0.3 collective-permute-done.6.refs_3_
  37.9 0.7 %block_edges.1 = (f32[2,256,128]{2,1,0:T(8,128)S(1)}, f32[2,256,128]{2,1,0:T(8,128)S(1)}) custom-call(s32[1,8]{1,0:T(1,128)S(1)} %copy-done.5, f32[7,256,128]{2,1,0:T(8,128)S(1)} %bitcast.29, f32[6,256,128]{2,1,0:T(8,128)S(1)} %collective-permute-done.got_ref, f32[2,64,128]{2,1,0:T(8,128)S(1)} %get-tuple-element.50.refs_0_, ...), custom_call_target="tpu_custom_call" | custom-call | tf_op jit(solution)/shard_map/block_edges/pallas_call | solution.py:386
  38.6 2.9 %collective-permute-start.7 = (f32[2,256,128]{2,1,0:T(8,128)S(1)}, f32[2,256,128]{2,1,0:T(8,128)S(1)}, u32[]{:S(2)}, u32[]{:S(2)}) collective-permute-start(f32[2,256,128]{2,1,0:T(8,128)S(1)} %get-tuple-element.55), channel_id=1, source_target_pairs={{0,1},{1,0},{2,3},{3,2},{4,5},{5,4},{6,7},{7,6},{8,9},{9,8},{10,11... | collective-permute-start | bytes 786440 | tf_op jit(solution)/shard_map/ppermute | solution.py:470
  41.4 0.9 %collective-permute-done.9 = f32[2,64,128]{2,1,0:T(8,128)S(1)} collective-permute-done((f32[2,64,128]{2,1,0:T(8,128)S(1)}, f32[2,64,128]{2,1,0:T(8,128)S(1)}, u32[]{:S(2)}, u32[]{:S(2)}) %collective-permute-start.9) | collective-permute-done | bytes 65568 | tf_op jit(solution)/shard_map/ppermute | solution.py:506
  42.4 2.2 %collective-permute-start.13 = (f32[2,64,128]{2,1,0:T(8,128)S(1)}, f32[2,64,128]{2,1,0:T(8,128)S(1)}, u32[]{:S(2)}, u32[]{:S(2)}) collective-permute-start(f32[2,64,128]{2,1,0:T(8,128)S(1)} %add_add_fusion.after_ref.refs_0_), channel_id=1, source_target_pairs={{0,6},{1,7},{2,4},{3,5},{4,2},{5,3},{6,0},{7,1},{8,14},{9,15},{10,... | collective-permute-start | bytes 196616 | tf_op jit(solution)/shard_map/ppermute | solution.py:474
  44.6 0.2 collective-permute-start.12
  44.9 0.3 collective-permute-start.11
  45.2 5.8 %outputs.2 = (bf16[128,4096]{1,0:T(8,128)(2,1)}, bf16[128,4096]{1,0:T(8,128)(2,1)}, bf16[128,4096]{1,0:T(8,128)(2,1)}, bf16[128,4096]{1,0:T(8,128)(2,1)}, f32[1,128]{1,0:T(1,128)S(1)}) custom-call(bf16[128,4096]{1,0:T(8,128)(2,1)S(1)} %bitcast.14, bf16[128,4096]{1,0:T(8,128)(2,1)S(1)} %bitcast.18, bf16[128,4096]{1,0:T(8,128)(2,1)S(1)} %bitcast.22, ...), custom_call_target="tpu_custom_call" | custom-call | flops 300000000 | bytes 1500000 | tf_op jit(solution)/shard_map/outputs/pallas_call | solution.py:524
  51.0 3.3 %collective-permute-start.14 = (f32[2,256,128]{2,1,0:T(8,128)S(1)}, f32[2,256,128]{2,1,0:T(8,128)S(1)}, u32[]{:S(2)}, u32[]{:S(2)}) collective-permute-start(f32[2,256,128]{2,1,0:T(8,128)S(1)} %gather_sums.1.after_ref.kept_ref), channel_id=1, source_target_pairs={{0,1},{1,0},{2,3},{3,2},{4,5},{5,4},{6,7},{7,6},{8,9},{9,8},{10,11... | collective-permute-start | bytes 786440 | tf_op jit(solution)/shard_map/ppermute | solution.py:470
  54.3 2.4 %outputs.3 = (bf16[128,4096]{1,0:T(8,128)(2,1)}, bf16[128,4096]{1,0:T(8,128)(2,1)}, bf16[128,4096]{1,0:T(8,128)(2,1)}, bf16[128,4096]{1,0:T(8,128)(2,1)}, f32[1,128]{1,0:T(1,128)}) custom-call(bf16[128,4096]{1,0:T(8,128)(2,1)S(1)} %bitcast.15, ...), custom_call_target="tpu_custom_call", output_to_operand_aliasing={{0}: (11, {}), {1}: (12, {}), {2}: (13, {}), {3}: (14, {})} | custom-call | flops 100000000 | bytes 500000 | tf_op jit(solution)/shard_map/outputs/pallas_call | solution.py:524
  56.7 1.0 %parameter_grads.1 = (f32[16,4096]{1,0:T(8,128)}, f32[16,4096]{1,0:T(8,128)}) custom-call(f32[4,16,8,128]{3,2,1,0:T(8,128)S(1)} %get-tuple-element.37.rate_ref, f32[16,4096]{1,0:T(8,128)S(1)} %copy-done.4, f32[2,256,128]{2,1,0:T(8,128)S(1)} %gather_sums.1.after_ref.kept_ref, f32[2,256,128]{2,1,0:T(8,128)S(1)} %collective-permute-done.14.got_ref), custom_call_target="tpu_custom_call" | custom-call | tf_op jit(solution)/shard_map/parameter_grads/pallas_call | solution.py:386
  (28 shorter events, 0.1 us)
Async XLA Ops:
  0.6 16.0 %copy-start.5 = (s32[1,8]{1,0:T(1,128)S(1)}, s32[1,8]{1,0:T(1,128)}, u32[]{:S(2)}) copy-start(s32[1,8]{1,0:T(1,128)} %doc_ref.5) | copy-start | bytes 100
  14.3 2.4 %collective-permute-start = (f32[6,256,128]{2,1,0:T(8,128)S(1)}, f32[6,256,128]{2,1,0:T(8,128)S(1)}, u32[]{:S(2)}, u32[]{:S(2)}) collective-permute-start(f32[6,256,128]{2,1,0:T(8,128)S(1)} %bitcast.34), channel_id=1, source_target_pairs={{0,1},{1,0},{2,3},{3,2},{4,5},{5,4},{6,7},{7,6},{8,9},{9,8},{10,11... | collective-permute-start | bytes 2359304 | tf_op jit(solution)/shard_map/ppermute | solution.py:470
  17.7 12.6 %collective-permute-start.1 = (f32[6,64,128]{2,1,0:T(8,128)S(1)}, f32[6,64,128]{2,1,0:T(8,128)S(1)}, u32[]{:S(2)}, u32[]{:S(2)}) collective-permute-start(f32[6,64,128]{2,1,0:T(8,128)S(1)} %get-tuple-element.46), channel_id=1, source_target_pairs={{0,2},{1,3},{2,0},{3,1},{4,6},{5,7},{6,4},{7,5},{8,10},{9,11},{10,... | collective-permute-start | bytes 589832 | tf_op jit(solution)/shard_map/ppermute | solution.py:474
  20.1 10.2 %collective-permute-start.2 = (f32[6,64,128]{2,1,0:T(8,128)S(1)}, f32[6,64,128]{2,1,0:T(8,128)S(1)}, u32[]{:S(2)}, u32[]{:S(2)}) collective-permute-start(f32[6,64,128]{2,1,0:T(8,128)S(1)} %get-tuple-element.47), channel_id=1, source_target_pairs={{0,4},{1,5},{2,6},{3,7},{4,0},{5,1},{6,2},{7,3},{8,12},{9,13},{10,... | collective-permute-start | bytes 589832 | tf_op jit(solution)/shard_map/ppermute | solution.py:474
  21.3 9.0 %collective-permute-start.3 = (f32[6,64,128]{2,1,0:T(8,128)S(1)}, f32[6,64,128]{2,1,0:T(8,128)S(1)}, u32[]{:S(2)}, u32[]{:S(2)}) collective-permute-start(f32[6,64,128]{2,1,0:T(8,128)S(1)} %get-tuple-element.48), channel_id=1, source_target_pairs={{0,6},{1,7},{2,4},{3,5},{4,2},{5,3},{6,0},{7,1},{8,14},{9,15},{10,... | collective-permute-start | bytes 589832 | tf_op jit(solution)/shard_map/ppermute | solution.py:474
  21.3 23.8 %copy-start = (bf16[1,128,4096]{2,1,0:T(8,128)(2,1)S(1)}, bf16[1,128,4096]{2,1,0:T(8,128)(2,1)}, u32[]{:S(2)}) copy-start(bf16[1,128,4096]{2,1,0:T(8,128)(2,1)} %param.8) | copy-start | bytes 3145732
  21.3 23.8 %copy-start.1 = (bf16[1,128,4096]{2,1,0:T(8,128)(2,1)S(1)}, bf16[1,128,4096]{2,1,0:T(8,128)(2,1)}, u32[]{:S(2)}) copy-start(bf16[1,128,4096]{2,1,0:T(8,128)(2,1)} %param.9) | copy-start | bytes 3145732
  21.3 23.8 %copy-start.2 = (bf16[1,128,4096]{2,1,0:T(8,128)(2,1)S(1)}, bf16[1,128,4096]{2,1,0:T(8,128)(2,1)}, u32[]{:S(2)}) copy-start(bf16[1,128,4096]{2,1,0:T(8,128)(2,1)} %param.7) | copy-start | bytes 3145732
  21.3 23.8 %copy-start.3 = (bf16[1,128,4096]{2,1,0:T(8,128)(2,1)S(1)}, bf16[1,128,4096]{2,1,0:T(8,128)(2,1)}, u32[]{:S(2)}) copy-start(bf16[1,128,4096]{2,1,0:T(8,128)(2,1)} %param.10) | copy-start | bytes 3145732
  21.3 23.8 %copy-start.4 = (f32[16,4096]{1,0:T(8,128)S(1)}, f32[16,4096]{1,0:T(8,128)}, u32[]{:S(2)}) copy-start(f32[16,4096]{1,0:T(8,128)} %residue_ref.7) | copy-start | bytes 786436
  31.0 6.2 %collective-permute-start.4 = (f32[2,64,128]{2,1,0:T(8,128)S(1)}, f32[2,64,128]{2,1,0:T(8,128)S(1)}, u32[]{:S(2)}, u32[]{:S(2)}) collective-permute-start(f32[2,64,128]{2,1,0:T(8,128)S(1)} %get-tuple-element.51), channel_id=1, source_target_pairs={{0,2},{1,3},{2,0},{3,1},{4,6},{5,7},{6,4},{7,5},{8,10},{9,11},{10,... | collective-permute-start | bytes 196616 | tf_op jit(solution)/shard_map/ppermute | solution.py:474
  32.5 5.1 %collective-permute-start.5 = (f32[2,64,128]{2,1,0:T(8,128)S(1)}, f32[2,64,128]{2,1,0:T(8,128)S(1)}, u32[]{:S(2)}, u32[]{:S(2)}) collective-permute-start(f32[2,64,128]{2,1,0:T(8,128)S(1)} %get-tuple-element.52), channel_id=1, source_target_pairs={{0,4},{1,5},{2,6},{3,7},{4,0},{5,1},{6,2},{7,3},{8,12},{9,13},{10,... | collective-permute-start | bytes 196616 | tf_op jit(solution)/shard_map/ppermute | solution.py:474
  33.7 4.1 %collective-permute-start.6 = (f32[2,64,128]{2,1,0:T(8,128)S(1)}, f32[2,64,128]{2,1,0:T(8,128)S(1)}, u32[]{:S(2)}, u32[]{:S(2)}) collective-permute-start(f32[2,64,128]{2,1,0:T(8,128)S(1)} %get-tuple-element.53), channel_id=1, source_target_pairs={{0,6},{1,7},{2,4},{3,5},{4,2},{5,3},{6,0},{7,1},{8,14},{9,15},{10,... | collective-permute-start | bytes 196616 | tf_op jit(solution)/shard_map/ppermute | solution.py:474
  33.8 7.7 %collective-permute-start.10 = (f32[2,64,128]{2,1,0:T(8,128)S(1)}, f32[2,64,128]{2,1,0:T(8,128)S(1)}, u32[]{:S(2)}, u32[]{:S(2)}) collective-permute-start(f32[2,64,128]{2,1,0:T(8,128)S(1)} %get-tuple-element.56), channel_id=1, source_target_pairs={{0,24},{8,16},{16,8},{24,0},{1,25},{9,17},{17,9},{25,1},{2,26},{10... | collective-permute-start | bytes 196616 | tf_op jit(solution)/shard_map/ppermute | solution.py:506
  37.3 5.1 %collective-permute-start.9 = (f32[2,64,128]{2,1,0:T(8,128)S(1)}, f32[2,64,128]{2,1,0:T(8,128)S(1)}, u32[]{:S(2)}, u32[]{:S(2)}) collective-permute-start(f32[2,64,128]{2,1,0:T(8,128)S(1)} %get-tuple-element.56), channel_id=1, source_target_pairs={{0,16},{8,24},{16,0},{24,8},{1,17},{9,25},{17,1},{25,9},{2,18},{10... | collective-permute-start | bytes 196616 | tf_op jit(solution)/shard_map/ppermute | solution.py:506
  37.3 5.1 %collective-permute-start.8 = (f32[2,64,128]{2,1,0:T(8,128)S(1)}, f32[2,64,128]{2,1,0:T(8,128)S(1)}, u32[]{:S(2)}, u32[]{:S(2)}) collective-permute-start(f32[2,64,128]{2,1,0:T(8,128)S(1)} %get-tuple-element.56), channel_id=1, source_target_pairs={{0,8},{8,0},{16,24},{24,16},{1,9},{9,1},{17,25},{25,17},{2,10},{10... | collective-permute-start | bytes 196616 | tf_op jit(solution)/shard_map/ppermute | solution.py:506
  38.6 6.6 %collective-permute-start.7 = (f32[2,256,128]{2,1,0:T(8,128)S(1)}, f32[2,256,128]{2,1,0:T(8,128)S(1)}, u32[]{:S(2)}, u32[]{:S(2)}) collective-permute-start(f32[2,256,128]{2,1,0:T(8,128)S(1)} %get-tuple-element.55), channel_id=1, source_target_pairs={{0,1},{1,0},{2,3},{3,2},{4,5},{5,4},{6,7},{7,6},{8,9},{9,8},{10,11... | collective-permute-start | bytes 786440 | tf_op jit(solution)/shard_map/ppermute | solution.py:470
  42.4 8.5 %collective-permute-start.13 = (f32[2,64,128]{2,1,0:T(8,128)S(1)}, f32[2,64,128]{2,1,0:T(8,128)S(1)}, u32[]{:S(2)}, u32[]{:S(2)}) collective-permute-start(f32[2,64,128]{2,1,0:T(8,128)S(1)} %add_add_fusion.after_ref.refs_0_), channel_id=1, source_target_pairs={{0,6},{1,7},{2,4},{3,5},{4,2},{5,3},{6,0},{7,1},{8,14},{9,15},{10,... | collective-permute-start | bytes 196616 | tf_op jit(solution)/shard_map/ppermute | solution.py:474
  44.6 6.3 %collective-permute-start.12 = (f32[2,64,128]{2,1,0:T(8,128)S(1)}, f32[2,64,128]{2,1,0:T(8,128)S(1)}, u32[]{:S(2)}, u32[]{:S(2)}) collective-permute-start(f32[2,64,128]{2,1,0:T(8,128)S(1)} %add_add_fusion.after_ref.refs_0_), channel_id=1, source_target_pairs={{0,4},{1,5},{2,6},{3,7},{4,0},{5,1},{6,2},{7,3},{8,12},{9,13},{10,... | collective-permute-start | bytes 196616 | tf_op jit(solution)/shard_map/ppermute | solution.py:474
  44.9 6.1 %collective-permute-start.11 = (f32[2,64,128]{2,1,0:T(8,128)S(1)}, f32[2,64,128]{2,1,0:T(8,128)S(1)}, u32[]{:S(2)}, u32[]{:S(2)}) collective-permute-start(f32[2,64,128]{2,1,0:T(8,128)S(1)} %add_add_fusion.after_ref.refs_0_), channel_id=1, source_target_pairs={{0,2},{1,3},{2,0},{3,1},{4,6},{5,7},{6,4},{7,5},{8,10},{9,11},{10,... | collective-permute-start | bytes 196616 | tf_op jit(solution)/shard_map/ppermute | solution.py:474
  51.0 5.7 %collective-permute-start.14 = (f32[2,256,128]{2,1,0:T(8,128)S(1)}, f32[2,256,128]{2,1,0:T(8,128)S(1)}, u32[]{:S(2)}, u32[]{:S(2)}) collective-permute-start(f32[2,256,128]{2,1,0:T(8,128)S(1)} %gather_sums.1.after_ref.kept_ref), channel_id=1, source_target_pairs={{0,1},{1,0},{2,3},{3,2},{4,5},{5,4},{6,7},{7,6},{8,9},{9,8},{10,11... | collective-permute-start | bytes 786440 | tf_op jit(solution)/shard_map/ppermute | solution.py:470

commit v4 on v3

--- a/solution.py
+++ b/solution.py
@@ -62,9 +62,11 @@
         lam = jnp.exp(-rate)
         square = lam * lam
         fourth = square * square
-        lam_s[m] = lam
+        cube = square * lam
+        for j, power in enumerate((lam, square, cube, fourth, fourth * lam, fourth * square, fourth * cube)):
+            lam_s[m, j] = power
         jump_s[m] = fourth * fourth
-        slope_s[m] = CHUNK * (fourth * (square * lam))
+        slope_s[m] = CHUNK * (fourth * fourth)
         for ref in (state_s, lag_s, res_s, mixl_s, head_s, headl_s, headm_s):
             ref[m] = zero
         pow_s[m] = zero + 1.0
@@ -81,15 +83,15 @@
             corr_s[lag] = total
         offset = (chunk * CHUNK).astype(F32)
         for m in range(modes):
-            lam = lam_s[m]
-            end, endl = u[0], None
-            for t in range(1, CHUNK):
-                endl = end if endl is None else endl * lam + end
-                end = end * lam + u[t]
-            head, headl = d[CHUNK - 1], None
-            for t in range(CHUNK - 2, -1, -1):
-                headl = head if headl is None else headl * lam + head
-                head = head * lam + d[t]
+            power = [lam_s[m, j] for j in range(CHUNK - 1)]
+            end, head = power[-1] * u[0], power[-1] * d[-1]
+            endl, headl = end, head
+            for j in range(CHUNK - 2, 0, -1):
+                end = end + power[j - 1] * u[CHUNK - 1 - j]
+                endl = endl + end
+                head = head + power[j - 1] * d[j]
+                headl = headl + head
+            end, head = end + u[-1], head + d[0]
             c_ref[0, chunk, m] = end
             b_ref[0, chunk, m] = head
             state, lag_state = state_s[m], lag_s[m]
@@ -98,17 +100,17 @@
             jump = jump_s[m]
             lag_s[m] = lag_state * jump + (state * slope_s[m] + endl)
             state_s[m] = state * jump + end
-            power = pow_s[m]
-            far = power * head
+            decay = pow_s[m]
+            far = decay * head
             head_s[m] = head_s[m] + far
-            headl_s[m] = headl_s[m] + power * headl
+            headl_s[m] = headl_s[m] + decay * headl
             headm_s[m] = headm_s[m] + offset * far
-            pow_s[m] = power * jump
+            pow_s[m] = decay * jump
         return 0
 
     lax.fori_loop(0, chunks, step, 0)
     def stats_of(m):
-        lam = lam_s[m]
+        lam = lam_s[m, 0]
         near, nearl = corr_s[CHUNK - 1], None
         for lag in range(CHUNK - 2, -1, -1):
             nearl = near if nearl is None else nearl * lam + near
@@ -116,11 +118,11 @@
         res = res_s[m]
         return (
             state_s[m],
-            lam * lag_s[m],
+            lag_s[m],
             head_s[m],
-            lam * headl_s[m] + headm_s[m],
+            headl_s[m] + headm_s[m],
             near + lam * res,
-            lam * (nearl + (res + lam * mixl_s[m])),
+            lam * (nearl + (res + mixl_s[m])),
         )
 
     half = modes // 2
@@ -458,7 +460,8 @@
             pltpu.VMEM((7, groups, halves, SUBS, LANES), F32),
             pltpu.VMEM((6, groups, halves, SUBS, LANES), F32),
         ],
-        scratch_shapes=[row_scratch] * 2 + [flat_scratch] + [mode_scratch] * 11 + [tap_scratch],
+        scratch_shapes=[row_scratch] * 2 + [flat_scratch, pltpu.VMEM((modes, CHUNK - 1, SUBS, LANES), F32)]
+        + [mode_scratch] * 10 + [tap_scratch],
         compiler_params=params(BIG),
         name="block_stats",
     )(k_in, v_in, q_in, g_in, hbm(pole_decay))

time: 57.8 us -> 56.3 us (0.974)
  Pallas kernels: 34.2 us -> 32.7 us
    pallas_call x1, Pallas kernels: 13.7 us -> 12.2 us  [body(): pl.pallas_call(partial(stats_kernel, float(row_len)), grid=(groups,), in_...]
  transfers between devices with their start and end apart: 15 -> 15, of which waited for: 3 -> 3; matrix products, arithmetic and copies ran while one was open for 0% -> 0% of each run, Pallas kernels for 31% -> 32%
where the time goes in v4:
time: 56.3 us; the launch traced here: 56.2 us
  Pallas kernels  32.7 us (58%)
  starting transfers between devices  19.2 us (34%)
  waiting for transfers between devices  3.49 us (6%)
  between operations  0.77 us (1%)
    pallas_call x1, Pallas kernels, body(): pl.pallas_call(partial(stats_kernel, float(row_len)), grid=(groups,), in_...  12.2 us
    ppermute x9, starting transfers between devices, swap_chips(): lax.ppermute(xs[away], 'ctx', [(i, i ^ 2 * away) for i in range(n_ctx)])  9.1 us
    pallas_call x1, Pallas kernels, body(): pl.pallas_call(local_kernel, grid=(groups,), in_specs=[wide] * 4 + [slim,...  8.92 us
    pallas_call x2, Pallas kernels, outputs(): pl.pallas_call(partial(output_kernel, len(outs)), grid=(count,), in_specs...  8.17 us
    ppermute x3, starting transfers between devices, swap_core(): return lax.ppermute(x, 'ctx', [(i, i ^ 1) for i in range(n_ctx)])  6.29 us
    ppermute x3, starting transfers between devices, body(): lax.ppermute(total, 'dp', [(i, i ^ away) for i in range(n_dp)])  3.78 us
    pallas_call x5, Pallas kernels, small_call(): pl.pallas_call(kernel, grid=(1,), in_specs=[scalar_spec() if x.dtype == j...  3.45 us
    ppermute x3, waiting for transfers between devices, swap_core(): return lax.ppermute(x, 'ctx', [(i, i ^ 1) for i in range(n_ctx)])  2.23 us
  transfers between devices with their start and end apart: 15, of which 3 were waited for; matrix products, arithmetic and copies ran while one was open for 0% of the time, Pallas kernels for 32%

profile of v4, /device:TPU:1, one launch (start us, length us, event | category | flops | bytes accessed | tf_op | source)
XLA Modules:
  0.0 56.2 jit_solution(15311010474331180711)
XLA Ops:
  0.6 12.2 %block_stats.1 = (f32[4,16,16,8,128]{4,3,2,1,0:T(8,128)S(1)}, f32[4,16,16,8,128]{4,3,2,1,0:T(8,128)S(1)}, f32[4,16,8,128]{3,2,1,0:T(8,128)S(1)}, f32[7,4,8,8,128...) custom-call(bf16[128,4096]{1,0:T(8,128)(2,1)} %bitcast.12, bf16[128,4096]{1,0:T(8,128)(2,1)} %bitcast.16, ...), custom_call_target="tpu_custom_call" | custom-call | tf_op jit(solution)/shard_map/block_stats/pallas_call | solution.py:451
  12.8 0.1 collective-permute-start
  12.9 2.2 %collective-permute-done.got_ref = f32[6,256,128]{2,1,0:T(8,128)S(1)} collective-permute-done((f32[6,256,128]{2,1,0:T(8,128)S(1)}, f32[6,256,128]{2,1,0:T(8,128)S(1)}, u32[]{:S(2)}, u32[]{:S(2)}) %collective-permute-start) | collective-permute-done | bytes 786464 | tf_op jit(solution)/shard_map/ppermute | solution.py:473
  15.2 1.0 %chip_stats.1 = (f32[6,64,128]{2,1,0:T(8,128)S(1)}, f32[6,64,128]{2,1,0:T(8,128)S(1)}, f32[6,64,128]{2,1,0:T(8,128)S(1)}, f32[6,64,128]{2,1,0:T(8,128)S(1)}, f32[64,128]{1,0:T(8,128)S(1)}) custom-call(s32[1,8]{1,0:T(1,128)S(1)} %copy-done.5, f32[7,256,128]{2,1,0:T(8,128)S(1)} %bitcast.28, f32[6,256,128]{2,1,0:T(8,128)S(1)} %collective-permute-done.got_ref), custom_call_target="tpu_custom_call" | custom-call | tf_op jit(solution)/shard_map/chip_stats/pallas_call | solution.py:388
  16.1 2.4 %collective-permute-start.1 = (f32[6,64,128]{2,1,0:T(8,128)S(1)}, f32[6,64,128]{2,1,0:T(8,128)S(1)}, u32[]{:S(2)}, u32[]{:S(2)}) collective-permute-start(f32[6,64,128]{2,1,0:T(8,128)S(1)} %get-tuple-element.46), channel_id=1, source_target_pairs={{0,2},{1,3},{2,0},{3,1},{4,6},{5,7},{6,4},{7,5},{8,10},{9,11},{10,... | collective-permute-start | bytes 589832 | tf_op jit(solution)/shard_map/ppermute | solution.py:477
  18.5 1.2 %collective-permute-start.2 = (f32[6,64,128]{2,1,0:T(8,128)S(1)}, f32[6,64,128]{2,1,0:T(8,128)S(1)}, u32[]{:S(2)}, u32[]{:S(2)}) collective-permute-start(f32[6,64,128]{2,1,0:T(8,128)S(1)} %get-tuple-element.47), channel_id=1, source_target_pairs={{0,4},{1,5},{2,6},{3,7},{4,0},{5,1},{6,2},{7,3},{8,12},{9,13},{10,... | collective-permute-start | bytes 589832 | tf_op jit(solution)/shard_map/ppermute | solution.py:477
  19.8 8.9 %local_outputs.1 = (f32[4,128,8,128]{3,2,1,0:T(8,128)S(1)}, f32[4,128,8,128]{3,2,1,0:T(8,128)S(1)}, f32[1,128]{1,0:T(1,128)S(1)}) custom-call(bf16[128,4096]{1,0:T(8,128)(2,1)} %bitcast.13, bf16[128,4096]{1,0:T(8,128)(2,1)} %bitcast.17, bf16[128,4096]{1,0:T(8,128)(2,1)} %bitcast.21, bf16[128,4096]{1,0:T(8,128)(2,1)} %bitcast.25, ...), custom_call_target="tpu_custom_call" | custom-call | flops 10000000000 | bytes 20000000 | tf_op jit(solution)/shard_map/local_outputs/pallas_call | solution.py:489
  28.8 0.7 %row_scan.1 = (f32[2,64,128]{2,1,0:T(8,128)S(1)}, f32[2,64,128]{2,1,0:T(8,128)S(1)}, f32[2,64,128]{2,1,0:T(8,128)S(1)}, f32[2,64,128]{2,1,0:T(8,128)S(1)}, f32[2,64,128]{2,1,0:T(8,128)S(1)}) custom-call(s32[1,8]{1,0:T(1,128)S(1)} %copy-done.5, f32[64,128]{1,0:T(8,128)S(1)} %get-tuple-element.42.after_ref.rate_ref, ...), custom_call_target="tpu_custom_call" | custom-call | tf_op jit(solution)/shard_map/row_scan/pallas_call | solution.py:388
  29.5 1.5 %collective-permute-start.4 = (f32[2,64,128]{2,1,0:T(8,128)S(1)}, f32[2,64,128]{2,1,0:T(8,128)S(1)}, u32[]{:S(2)}, u32[]{:S(2)}) collective-permute-start(f32[2,64,128]{2,1,0:T(8,128)S(1)} %get-tuple-element.51), channel_id=1, source_target_pairs={{0,2},{1,3},{2,0},{3,1},{4,6},{5,7},{6,4},{7,5},{8,10},{9,11},{10,... | collective-permute-start | bytes 196616 | tf_op jit(solution)/shard_map/ppermute | solution.py:477
  31.0 1.2 %collective-permute-start.5 = (f32[2,64,128]{2,1,0:T(8,128)S(1)}, f32[2,64,128]{2,1,0:T(8,128)S(1)}, u32[]{:S(2)}, u32[]{:S(2)}) collective-permute-start(f32[2,64,128]{2,1,0:T(8,128)S(1)} %get-tuple-element.52), channel_id=1, source_target_pairs={{0,4},{1,5},{2,6},{3,7},{4,0},{5,1},{6,2},{7,3},{8,12},{9,13},{10,... | collective-permute-start | bytes 196616 | tf_op jit(solution)/shard_map/ppermute | solution.py:477
  32.2 0.0 collective-permute-start.6
  32.2 3.5 %collective-permute-start.10 = (f32[2,64,128]{2,1,0:T(8,128)S(1)}, f32[2,64,128]{2,1,0:T(8,128)S(1)}, u32[]{:S(2)}, u32[]{:S(2)}) collective-permute-start(f32[2,64,128]{2,1,0:T(8,128)S(1)} %get-tuple-element.56), channel_id=1, source_target_pairs={{0,24},{8,16},{16,8},{24,0},{1,25},{9,17},{17,9},{25,1},{2,26},{10... | collective-permute-start | bytes 196616 | tf_op jit(solution)/shard_map/ppermute | solution.py:509
  35.7 0.3 collective-permute-start.8
  36.0 0.3 collective-permute-done.6.refs_3_
  36.3 0.7 %block_edges.1 = (f32[2,256,128]{2,1,0:T(8,128)S(1)}, f32[2,256,128]{2,1,0:T(8,128)S(1)}) custom-call(s32[1,8]{1,0:T(1,128)S(1)} %copy-done.5, f32[7,256,128]{2,1,0:T(8,128)S(1)} %bitcast.29, f32[6,256,128]{2,1,0:T(8,128)S(1)} %collective-permute-done.got_ref, f32[2,64,128]{2,1,0:T(8,128)S(1)} %get-tuple-element.50.refs_0_, ...), custom_call_target="tpu_custom_call" | custom-call | tf_op jit(solution)/shard_map/block_edges/pallas_call | solution.py:388
  37.0 2.9 %collective-permute-start.7 = (f32[2,256,128]{2,1,0:T(8,128)S(1)}, f32[2,256,128]{2,1,0:T(8,128)S(1)}, u32[]{:S(2)}, u32[]{:S(2)}) collective-permute-start(f32[2,256,128]{2,1,0:T(8,128)S(1)} %get-tuple-element.55), channel_id=1, source_target_pairs={{0,1},{1,0},{2,3},{3,2},{4,5},{5,4},{6,7},{7,6},{8,9},{9,8},{10,11... | collective-permute-start | bytes 786440 | tf_op jit(solution)/shard_map/ppermute | solution.py:473
  39.9 0.9 %collective-permute-done.9 = f32[2,64,128]{2,1,0:T(8,128)S(1)} collective-permute-done((f32[2,64,128]{2,1,0:T(8,128)S(1)}, f32[2,64,128]{2,1,0:T(8,128)S(1)}, u32[]{:S(2)}, u32[]{:S(2)}) %collective-permute-start.9) | collective-permute-done | bytes 65568 | tf_op jit(solution)/shard_map/ppermute | solution.py:509
  40.9 2.2 %collective-permute-start.13 = (f32[2,64,128]{2,1,0:T(8,128)S(1)}, f32[2,64,128]{2,1,0:T(8,128)S(1)}, u32[]{:S(2)}, u32[]{:S(2)}) collective-permute-start(f32[2,64,128]{2,1,0:T(8,128)S(1)} %add_add_fusion.after_ref.refs_0_), channel_id=1, source_target_pairs={{0,6},{1,7},{2,4},{3,5},{4,2},{5,3},{6,0},{7,1},{8,14},{9,15},{10,... | collective-permute-start | bytes 196616 | tf_op jit(solution)/shard_map/ppermute | solution.py:477
  43.1 0.2 collective-permute-start.12
  43.3 0.3 collective-permute-start.11
  43.6 5.8 %outputs.2 = (bf16[128,4096]{1,0:T(8,128)(2,1)}, bf16[128,4096]{1,0:T(8,128)(2,1)}, bf16[128,4096]{1,0:T(8,128)(2,1)}, bf16[128,4096]{1,0:T(8,128)(2,1)}, f32[1,128]{1,0:T(1,128)S(1)}) custom-call(bf16[128,4096]{1,0:T(8,128)(2,1)S(1)} %bitcast.14, bf16[128,4096]{1,0:T(8,128)(2,1)S(1)} %bitcast.18, bf16[128,4096]{1,0:T(8,128)(2,1)S(1)} %bitcast.22, ...), custom_call_target="tpu_custom_call" | custom-call | flops 300000000 | bytes 1500000 | tf_op jit(solution)/shard_map/outputs/pallas_call | solution.py:527
  49.5 3.3 %collective-permute-start.14 = (f32[2,256,128]{2,1,0:T(8,128)S(1)}, f32[2,256,128]{2,1,0:T(8,128)S(1)}, u32[]{:S(2)}, u32[]{:S(2)}) collective-permute-start(f32[2,256,128]{2,1,0:T(8,128)S(1)} %gather_sums.1.after_ref.kept_ref), channel_id=1, source_target_pairs={{0,1},{1,0},{2,3},{3,2},{4,5},{5,4},{6,7},{7,6},{8,9},{9,8},{10,11... | collective-permute-start | bytes 786440 | tf_op jit(solution)/shard_map/ppermute | solution.py:473
  52.7 2.4 %outputs.3 = (bf16[128,4096]{1,0:T(8,128)(2,1)}, bf16[128,4096]{1,0:T(8,128)(2,1)}, bf16[128,4096]{1,0:T(8,128)(2,1)}, bf16[128,4096]{1,0:T(8,128)(2,1)}, f32[1,128]{1,0:T(1,128)}) custom-call(bf16[128,4096]{1,0:T(8,128)(2,1)S(1)} %bitcast.15, ...), custom_call_target="tpu_custom_call", output_to_operand_aliasing={{0}: (11, {}), {1}: (12, {}), {2}: (13, {}), {3}: (14, {})} | custom-call | flops 100000000 | bytes 500000 | tf_op jit(solution)/shard_map/outputs/pallas_call | solution.py:527
  55.2 1.0 %parameter_grads.1 = (f32[16,4096]{1,0:T(8,128)}, f32[16,4096]{1,0:T(8,128)}) custom-call(f32[4,16,8,128]{3,2,1,0:T(8,128)S(1)} %get-tuple-element.37.rate_ref, f32[16,4096]{1,0:T(8,128)S(1)} %copy-done.4, f32[2,256,128]{2,1,0:T(8,128)S(1)} %gather_sums.1.after_ref.kept_ref, f32[2,256,128]{2,1,0:T(8,128)S(1)} %collective-permute-done.14.got_ref), custom_call_target="tpu_custom_call" | custom-call | tf_op jit(solution)/shard_map/parameter_grads/pallas_call | solution.py:388
  (28 shorter events, 0.1 us)
Async XLA Ops:
  0.6 14.5 %copy-start.5 = (s32[1,8]{1,0:T(1,128)S(1)}, s32[1,8]{1,0:T(1,128)}, u32[]{:S(2)}) copy-start(s32[1,8]{1,0:T(1,128)} %doc_ref.5) | copy-start | bytes 100
  12.8 2.4 %collective-permute-start = (f32[6,256,128]{2,1,0:T(8,128)S(1)}, f32[6,256,128]{2,1,0:T(8,128)S(1)}, u32[]{:S(2)}, u32[]{:S(2)}) collective-permute-start(f32[6,256,128]{2,1,0:T(8,128)S(1)} %bitcast.34), channel_id=1, source_target_pairs={{0,1},{1,0},{2,3},{3,2},{4,5},{5,4},{6,7},{7,6},{8,9},{9,8},{10,11... | collective-permute-start | bytes 2359304 | tf_op jit(solution)/shard_map/ppermute | solution.py:473
  16.1 12.6 %collective-permute-start.1 = (f32[6,64,128]{2,1,0:T(8,128)S(1)}, f32[6,64,128]{2,1,0:T(8,128)S(1)}, u32[]{:S(2)}, u32[]{:S(2)}) collective-permute-start(f32[6,64,128]{2,1,0:T(8,128)S(1)} %get-tuple-element.46), channel_id=1, source_target_pairs={{0,2},{1,3},{2,0},{3,1},{4,6},{5,7},{6,4},{7,5},{8,10},{9,11},{10,... | collective-permute-start | bytes 589832 | tf_op jit(solution)/shard_map/ppermute | solution.py:477
  18.5 10.2 %collective-permute-start.2 = (f32[6,64,128]{2,1,0:T(8,128)S(1)}, f32[6,64,128]{2,1,0:T(8,128)S(1)}, u32[]{:S(2)}, u32[]{:S(2)}) collective-permute-start(f32[6,64,128]{2,1,0:T(8,128)S(1)} %get-tuple-element.47), channel_id=1, source_target_pairs={{0,4},{1,5},{2,6},{3,7},{4,0},{5,1},{6,2},{7,3},{8,12},{9,13},{10,... | collective-permute-start | bytes 589832 | tf_op jit(solution)/shard_map/ppermute | solution.py:477
  19.8 9.0 %collective-permute-start.3 = (f32[6,64,128]{2,1,0:T(8,128)S(1)}, f32[6,64,128]{2,1,0:T(8,128)S(1)}, u32[]{:S(2)}, u32[]{:S(2)}) collective-permute-start(f32[6,64,128]{2,1,0:T(8,128)S(1)} %get-tuple-element.48), channel_id=1, source_target_pairs={{0,6},{1,7},{2,4},{3,5},{4,2},{5,3},{6,0},{7,1},{8,14},{9,15},{10,... | collective-permute-start | bytes 589832 | tf_op jit(solution)/shard_map/ppermute | solution.py:477
  19.8 23.8 %copy-start = (bf16[1,128,4096]{2,1,0:T(8,128)(2,1)S(1)}, bf16[1,128,4096]{2,1,0:T(8,128)(2,1)}, u32[]{:S(2)}) copy-start(bf16[1,128,4096]{2,1,0:T(8,128)(2,1)} %param.8) | copy-start | bytes 3145732
  19.8 23.8 %copy-start.1 = (bf16[1,128,4096]{2,1,0:T(8,128)(2,1)S(1)}, bf16[1,128,4096]{2,1,0:T(8,128)(2,1)}, u32[]{:S(2)}) copy-start(bf16[1,128,4096]{2,1,0:T(8,128)(2,1)} %param.9) | copy-start | bytes 3145732
  19.8 23.8 %copy-start.2 = (bf16[1,128,4096]{2,1,0:T(8,128)(2,1)S(1)}, bf16[1,128,4096]{2,1,0:T(8,128)(2,1)}, u32[]{:S(2)}) copy-start(bf16[1,128,4096]{2,1,0:T(8,128)(2,1)} %param.7) | copy-start | bytes 3145732
  19.8 23.8 %copy-start.3 = (bf16[1,128,4096]{2,1,0:T(8,128)(2,1)S(1)}, bf16[1,128,4096]{2,1,0:T(8,128)(2,1)}, u32[]{:S(2)}) copy-start(bf16[1,128,4096]{2,1,0:T(8,128)(2,1)} %param.10) | copy-start | bytes 3145732
  19.8 23.8 %copy-start.4 = (f32[16,4096]{1,0:T(8,128)S(1)}, f32[16,4096]{1,0:T(8,128)}, u32[]{:S(2)}) copy-start(f32[16,4096]{1,0:T(8,128)} %residue_ref.7) | copy-start | bytes 786436
  29.5 6.2 %collective-permute-start.4 = (f32[2,64,128]{2,1,0:T(8,128)S(1)}, f32[2,64,128]{2,1,0:T(8,128)S(1)}, u32[]{:S(2)}, u32[]{:S(2)}) collective-permute-start(f32[2,64,128]{2,1,0:T(8,128)S(1)} %get-tuple-element.51), channel_id=1, source_target_pairs={{0,2},{1,3},{2,0},{3,1},{4,6},{5,7},{6,4},{7,5},{8,10},{9,11},{10,... | collective-permute-start | bytes 196616 | tf_op jit(solution)/shard_map/ppermute | solution.py:477
  31.0 5.1 %collective-permute-start.5 = (f32[2,64,128]{2,1,0:T(8,128)S(1)}, f32[2,64,128]{2,1,0:T(8,128)S(1)}, u32[]{:S(2)}, u32[]{:S(2)}) collective-permute-start(f32[2,64,128]{2,1,0:T(8,128)S(1)} %get-tuple-element.52), channel_id=1, source_target_pairs={{0,4},{1,5},{2,6},{3,7},{4,0},{5,1},{6,2},{7,3},{8,12},{9,13},{10,... | collective-permute-start | bytes 196616 | tf_op jit(solution)/shard_map/ppermute | solution.py:477
  32.2 4.1 %collective-permute-start.6 = (f32[2,64,128]{2,1,0:T(8,128)S(1)}, f32[2,64,128]{2,1,0:T(8,128)S(1)}, u32[]{:S(2)}, u32[]{:S(2)}) collective-permute-start(f32[2,64,128]{2,1,0:T(8,128)S(1)} %get-tuple-element.53), channel_id=1, source_target_pairs={{0,6},{1,7},{2,4},{3,5},{4,2},{5,3},{6,0},{7,1},{8,14},{9,15},{10,... | collective-permute-start | bytes 196616 | tf_op jit(solution)/shard_map/ppermute | solution.py:477
  32.2 7.7 %collective-permute-start.10 = (f32[2,64,128]{2,1,0:T(8,128)S(1)}, f32[2,64,128]{2,1,0:T(8,128)S(1)}, u32[]{:S(2)}, u32[]{:S(2)}) collective-permute-start(f32[2,64,128]{2,1,0:T(8,128)S(1)} %get-tuple-element.56), channel_id=1, source_target_pairs={{0,24},{8,16},{16,8},{24,0},{1,25},{9,17},{17,9},{25,1},{2,26},{10... | collective-permute-start | bytes 196616 | tf_op jit(solution)/shard_map/ppermute | solution.py:509
  35.7 5.1 %collective-permute-start.9 = (f32[2,64,128]{2,1,0:T(8,128)S(1)}, f32[2,64,128]{2,1,0:T(8,128)S(1)}, u32[]{:S(2)}, u32[]{:S(2)}) collective-permute-start(f32[2,64,128]{2,1,0:T(8,128)S(1)} %get-tuple-element.56), channel_id=1, source_target_pairs={{0,16},{8,24},{16,0},{24,8},{1,17},{9,25},{17,1},{25,9},{2,18},{10... | collective-permute-start | bytes 196616 | tf_op jit(solution)/shard_map/ppermute | solution.py:509
  35.7 5.1 %collective-permute-start.8 = (f32[2,64,128]{2,1,0:T(8,128)S(1)}, f32[2,64,128]{2,1,0:T(8,128)S(1)}, u32[]{:S(2)}, u32[]{:S(2)}) collective-permute-start(f32[2,64,128]{2,1,0:T(8,128)S(1)} %get-tuple-element.56), channel_id=1, source_target_pairs={{0,8},{8,0},{16,24},{24,16},{1,9},{9,1},{17,25},{25,17},{2,10},{10... | collective-permute-start | bytes 196616 | tf_op jit(solution)/shard_map/ppermute | solution.py:509
  37.0 6.6 %collective-permute-start.7 = (f32[2,256,128]{2,1,0:T(8,128)S(1)}, f32[2,256,128]{2,1,0:T(8,128)S(1)}, u32[]{:S(2)}, u32[]{:S(2)}) collective-permute-start(f32[2,256,128]{2,1,0:T(8,128)S(1)} %get-tuple-element.55), channel_id=1, source_target_pairs={{0,1},{1,0},{2,3},{3,2},{4,5},{5,4},{6,7},{7,6},{8,9},{9,8},{10,11... | collective-permute-start | bytes 786440 | tf_op jit(solution)/shard_map/ppermute | solution.py:473
  40.9 8.5 %collective-permute-start.13 = (f32[2,64,128]{2,1,0:T(8,128)S(1)}, f32[2,64,128]{2,1,0:T(8,128)S(1)}, u32[]{:S(2)}, u32[]{:S(2)}) collective-permute-start(f32[2,64,128]{2,1,0:T(8,128)S(1)} %add_add_fusion.after_ref.refs_0_), channel_id=1, source_target_pairs={{0,6},{1,7},{2,4},{3,5},{4,2},{5,3},{6,0},{7,1},{8,14},{9,15},{10,... | collective-permute-start | bytes 196616 | tf_op jit(solution)/shard_map/ppermute | solution.py:477
  43.1 6.3 %collective-permute-start.12 = (f32[2,64,128]{2,1,0:T(8,128)S(1)}, f32[2,64,128]{2,1,0:T(8,128)S(1)}, u32[]{:S(2)}, u32[]{:S(2)}) collective-permute-start(f32[2,64,128]{2,1,0:T(8,128)S(1)} %add_add_fusion.after_ref.refs_0_), channel_id=1, source_target_pairs={{0,4},{1,5},{2,6},{3,7},{4,0},{5,1},{6,2},{7,3},{8,12},{9,13},{10,... | collective-permute-start | bytes 196616 | tf_op jit(solution)/shard_map/ppermute | solution.py:477
  43.3 6.1 %collective-permute-start.11 = (f32[2,64,128]{2,1,0:T(8,128)S(1)}, f32[2,64,128]{2,1,0:T(8,128)S(1)}, u32[]{:S(2)}, u32[]{:S(2)}) collective-permute-start(f32[2,64,128]{2,1,0:T(8,128)S(1)} %add_add_fusion.after_ref.refs_0_), channel_id=1, source_target_pairs={{0,2},{1,3},{2,0},{3,1},{4,6},{5,7},{6,4},{7,5},{8,10},{9,11},{10,... | collective-permute-start | bytes 196616 | tf_op jit(solution)/shard_map/ppermute | solution.py:477
  49.5 5.7 %collective-permute-start.14 = (f32[2,256,128]{2,1,0:T(8,128)S(1)}, f32[2,256,128]{2,1,0:T(8,128)S(1)}, u32[]{:S(2)}, u32[]{:S(2)}) collective-permute-start(f32[2,256,128]{2,1,0:T(8,128)S(1)} %gather_sums.1.after_ref.kept_ref), channel_id=1, source_target_pairs={{0,1},{1,0},{2,3},{3,2},{4,5},{5,4},{6,7},{7,6},{8,9},{9,8},{10,11... | collective-permute-start | bytes 786440 | tf_op jit(solution)/shard_map/ppermute | solution.py:473

commit v5 on v4

--- a/solution.py
+++ b/solution.py
@@ -198,31 +198,21 @@
     lax.fori_loop(0, chunks, step, 0)
 
 
-def output_kernel(
-    earlier, k_ref, v_ref, q_ref, g_ref, rate_ref, residue_ref, zl_ref, wl_ref, kept_ref, got_ref, after_ref, *refs
-):
-    mixed_ref, qg_ref, kg_ref, vg_ref, zeros_ref = refs[earlier : earlier + 5]
-    z_rows, w_rows, r_rows, lam_s, ahead_s, behind_s = refs[earlier + 5 :]
-    modes = rate_ref.shape[1]
-    half = modes // 2
-    chunks = k_ref.shape[0] // CHUNK
-    first = lax.axis_index("ctx") % 2 == 0
-    zeros_ref[...] = jnp.zeros((1, LANES), F32)
-    mode_rows(residue_ref, r_rows)
-    for m in range(modes):
-        rate = rate_ref[0, m]
+def add_carry(group, chunks, core, rates, residues, edge, z_in, w_in, store, lam_s, ahead_s, behind_s):
+    halves = lam_s.shape[0]
+    for m in range(halves):
+        rate = rates(core * halves + m)
         lam = jnp.exp(-rate)
         lam_s[m] = lam
-        lead = mode_row(r_rows, m) * jnp.sqrt(2.0 * rate) * lam
-        mine = first if m < half else jnp.logical_not(first)
-        ahead_s[m] = lead * jnp.where(mine, kept_ref[0, 0, m % half], got_ref[0, 0, m % half])
-        behind_s[m] = lead * jnp.where(mine, kept_ref[1, 0, m % half], got_ref[1, 0, m % half])
+        lead = residues(core, m) * jnp.sqrt(2.0 * rate) * lam
+        ahead_s[m] = lead * edge(0, m)
+        behind_s[m] = lead * edge(1, m)
 
     def step(chunk, _):
         mirror = chunks - 1 - chunk
-        z = [zl_ref[0, chunk * CHUNK + t] for t in range(CHUNK)]
-        w = [wl_ref[0, mirror * CHUNK + t] for t in range(CHUNK)]
-        for m in range(modes):
+        z = [z_in[group, chunk * CHUNK + t] for t in range(CHUNK)]
+        w = [w_in[group, mirror * CHUNK + t] for t in range(CHUNK)]
+        for m in range(halves):
             lam = lam_s[m]
             ahead, behind = ahead_s[m], behind_s[m]
             for t in range(CHUNK):
@@ -232,12 +222,31 @@
                 behind = behind * lam
             ahead_s[m] = ahead
             behind_s[m] = behind
+        store(chunk, mirror, z, w)
+        return 0
+
+    lax.fori_loop(0, chunks, step, 0)
+
+
+def output_kernel(
+    earlier, k_ref, v_ref, q_ref, g_ref, rate_ref, residue_ref, zl_ref, wl_ref, got_ref, after_ref, *refs
+):
+    mixed_ref, qg_ref, kg_ref, vg_ref, zeros_ref = refs[earlier : earlier + 5]
+    z_rows, w_rows, r_rows, lam_s, ahead_s, behind_s = refs[earlier + 5 :]
+    chunks = k_ref.shape[0] // CHUNK
+    zeros_ref[...] = jnp.zeros((1, LANES), F32)
+    mode_rows(residue_ref, r_rows)
+
+    def store(chunk, mirror, z, w):
         for t in range(CHUNK):
             z_rows[pl.ds(chunk * 64 + t, 8, stride=8), :] = z[t]
             w_rows[pl.ds(mirror * 64 + t, 8, stride=8), :] = w[t]
-        return 0
-
-    lax.fori_loop(0, chunks, step, 0)
+
+    add_carry(
+        0, chunks, 1 - lax.axis_index("ctx") % 2, lambda mode: rate_ref[0, mode],
+        lambda core, m: r_rows[pl.ds(core * 64 + m, 8, stride=8), :],
+        lambda side, m: got_ref[side, 0, m], zl_ref, wl_ref, store, lam_s, ahead_s, behind_s,
+    )
     for pair in range(chunks // 2):
         window = pl.ds(pair * 16, 16)
         for tile in range(SUBS):
@@ -321,8 +330,10 @@
     total_ref[1] = grad_lag
 
 
-def expand_kernel(block, chips, doc_ref, kept_ref, got_ref, *refs):
-    ins, mine_ref, send_ref, whole = refs[:chips], refs[chips], refs[chips + 1], refs[chips + 2]
+def expand_kernel(block, chips, doc_ref, kept_ref, got_ref, rate_ref, residue_ref, z_in, w_in, *refs):
+    ins, (send_ref, z_out, w_out), (whole, mine, r_rows, lam_s, ahead_s, behind_s) = (
+        refs[:chips], refs[chips : chips + 3], refs[chips + 3 :],
+    )
     core, chip = chip_of()
     first = core == 0
     joined = joined_in(doc_ref, chip)
@@ -336,10 +347,33 @@
     state, back = whole[0], whole[1]
     state_right = joined * end_left + hop * state
     back_left = joined * head_right + hop * back
-    mine_ref[0] = jnp.where(first, state, state_right)
-    mine_ref[1] = jnp.where(first, back_left, back)
+    mine[0] = jnp.where(first, state, state_right)
+    mine[1] = jnp.where(first, back_left, back)
     send_ref[0] = jnp.where(first, state_right, state)
     send_ref[1] = jnp.where(first, back, back_left)
+    groups, tokens = z_in.shape[0], z_in.shape[1]
+    halves = lam_s.shape[0]
+
+    def one_group(group, _):
+        modes = pl.ds(pl.multiple_of(core * halves, halves), halves)
+        for tile in range(SUBS):
+            lanes = pl.ds(pl.multiple_of(group * GROUP + tile * LANES, LANES), LANES)
+            r_rows[pl.ds(tile * 8, 8), :] = residue_ref[modes, lanes]
+
+        def store(chunk, mirror, z, w):
+            for t in range(CHUNK):
+                z_out[group, chunk * CHUNK + t] = z[t]
+                w_out[group, mirror * CHUNK + t] = w[t]
+
+        add_carry(
+            group, tokens // CHUNK, core, lambda mode: rate_ref[group, mode],
+            lambda core, m: r_rows[pl.ds(m, 8, stride=8), :],
+            lambda side, m: mine[side, pl.ds(pl.multiple_of((group * halves + m) * SUBS, SUBS), SUBS), :],
+            z_in, w_in, store, lam_s, ahead_s, behind_s,
+        )
+        return 0
+
+    lax.fori_loop(0, groups, one_group, 0)
 
 
 def gather_kernel(chips, *refs):
@@ -508,18 +542,21 @@
     total = scanned[chips]
     for other in [lax.ppermute(total, "dp", [(i, i ^ away) for i in range(n_dp)]) for away in range(1, n_dp)]:
         total = total + other
-    mine, give = small_call(
+    held = [vmem(x) for x in (*tokens, rate, residue)]
+    half_scratch = pltpu.VMEM((halves, SUBS, LANES), F32)
+    in_vmem = pl.BlockSpec(memory_space=pltpu.VMEM)
+    give, z_local, w_local = pl.pallas_call(
         partial(expand_kernel, float(block), chips),
-        "block_edges",
-        [group_doc, kept, got, *swap_chips(scanned[:chips])],
-        [f32(2, half, LANES)] * 2,
-        [pltpu.VMEM((2, half, LANES), F32)],
-    )
-    theirs = swap_core(give)
-
-    edges = [x.reshape(2, groups, halves, SUBS, LANES) for x in (mine, theirs)]
-
-    held = [vmem(x) for x in (*tokens, rate, residue)]
+        in_specs=[scalar_spec()] + [in_vmem] * (6 + chips),
+        out_specs=[in_vmem] * 3,
+        out_shape=[f32(2, half, LANES)] + [f32(groups, block, SUBS, LANES)] * 2,
+        input_output_aliases={5: 1, 6: 2},
+        scratch_shapes=[pltpu.VMEM((2, half, LANES), F32)] * 2
+        + [pltpu.VMEM((GROUP // LANES * halves, LANES), F32)] + [half_scratch] * 3,
+        compiler_params=params(),
+        name="block_edges",
+    )(group_doc, kept, got, rate, residue, z_local, w_local, *swap_chips(scanned[:chips]))
+    theirs = swap_core(give).reshape(2, groups, halves, SUBS, LANES)
 
     def outputs(first, count, after, outs):
         wide, slim, natural, chunked, halved = specs(lambda i: i + first)
@@ -527,18 +564,18 @@
         result = pl.pallas_call(
             partial(output_kernel, len(outs)),
             grid=(count,),
-            in_specs=[wide] * 4 + [slim, natural] + [columns] * 2 + [halved(2)] * 2
+            in_specs=[wide] * 4 + [slim, natural] + [columns] * 2 + [halved(2)]
             + [pl.BlockSpec(memory_space=pl.ANY)] * (1 + len(outs)),
             out_specs=[wide] * 4 + [pl.BlockSpec((1, LANES), lambda i: (0, 0))],
             out_shape=[pltpu.HBM((block, channels), jnp.bfloat16)] * 4 + [pltpu.VMEM((1, LANES), F32)],
-            input_output_aliases={11 + i: i for i in range(len(outs))},
-            scratch_shapes=[row_scratch] * 2 + [flat_scratch] + [mode_scratch] * 3,
+            input_output_aliases={10 + i: i for i in range(len(outs))},
+            scratch_shapes=[row_scratch] * 2 + [flat_scratch] + [half_scratch] * 3,
             compiler_params=params(BIG),
             cost_estimate=pl.CostEstimate(
                 flops=100_000_000 * count, bytes_accessed=500_000 * count, transcendentals=0
             ),
             name="outputs",
-        )(*held, vmem(z_local), vmem(w_local), *edges, after, *outs)
+        )(*held, vmem(z_local), vmem(w_local), theirs, after, *outs)
         return result[:4], result[4]
 
     sums = swap_chips([total] * chips)

time: 56.3 us -> 54 us (0.959)
  starting transfers between devices: 19.2 us -> 17.4 us
  waiting for transfers between devices: 3.49 us -> 2.6 us
    pallas_call x0 -> x1, Pallas kernels: none -> 3.38 us  [body(): pl.pallas_call(partial(expand_kernel, float(block), chips), in_specs=[sca...]
    pallas_call x2, Pallas kernels: 8.17 us -> 5.91 us  [outputs(): pl.pallas_call(partial(output_kernel, len(outs)), grid=(count,), in_specs...]
    ppermute x3, starting transfers between devices: 6.29 us -> 4.53 us  [swap_core(): return lax.ppermute(x, 'ctx', [(i, i ^ 1) for i in range(n_ctx)])]
    ppermute x3, waiting for transfers between devices: 0.93 us -> 0.01 us  [body(): lax.ppermute(total, 'dp', [(i, i ^ away) for i in range(n_dp)])]
    pallas_call x5 -> x4, Pallas kernels: 3.45 us -> 2.74 us  [small_call(): pl.pallas_call(kernel, grid=(1,), in_specs=[scalar_spec() if x.dtype == j...]
  transfers between devices with their start and end apart: 15 -> 15, of which waited for: 3 -> 2; matrix products, arithmetic and copies ran while one was open for 0% -> 0% of each run, Pallas kernels for 32% -> 34%
where the time goes in v5:
time: 54 us; the launch traced here: 53.8 us
  Pallas kernels  33 us (61%)
  starting transfers between devices  17.4 us (32%)
  waiting for transfers between devices  2.6 us (5%)
  between operations  0.77 us (1%)
    pallas_call x1, Pallas kernels, body(): pl.pallas_call(partial(stats_kernel, float(row_len)), grid=(groups,), in_...  12.2 us
    ppermute x9, starting transfers between devices, swap_chips(): lax.ppermute(xs[away], 'ctx', [(i, i ^ 2 * away) for i in range(n_ctx)])  9.09 us
    pallas_call x1, Pallas kernels, body(): pl.pallas_call(local_kernel, grid=(groups,), in_specs=[wide] * 4 + [slim,...  8.8 us
    pallas_call x2, Pallas kernels, outputs(): pl.pallas_call(partial(output_kernel, len(outs)), grid=(count,), in_specs...  5.91 us
    ppermute x3, starting transfers between devices, swap_core(): return lax.ppermute(x, 'ctx', [(i, i ^ 1) for i in range(n_ctx)])  4.53 us
    ppermute x3, starting transfers between devices, body(): lax.ppermute(total, 'dp', [(i, i ^ away) for i in range(n_dp)])  3.77 us
    pallas_call x1, Pallas kernels, body(): pl.pallas_call(partial(expand_kernel, float(block), chips), in_specs=[sca...  3.38 us
    pallas_call x4, Pallas kernels, small_call(): pl.pallas_call(kernel, grid=(1,), in_specs=[scalar_spec() if x.dtype == j...  2.74 us
  transfers between devices with their start and end apart: 15, of which 2 were waited for; matrix products, arithmetic and copies ran while one was open for 0% of the time, Pallas kernels for 34%

profile of v5, /device:TPU:1, one launch (start us, length us, event | category | flops | bytes accessed | tf_op | source)
XLA Modules:
  0.0 53.8 jit_solution(11589764367973663911)
XLA Ops:
  0.6 12.2 %block_stats.1 = (f32[4,16,16,8,128]{4,3,2,1,0:T(8,128)S(1)}, f32[4,16,16,8,128]{4,3,2,1,0:T(8,128)S(1)}, f32[4,16,8,128]{3,2,1,0:T(8,128)S(1)}, f32[7,4,8,8,128...) custom-call(bf16[128,4096]{1,0:T(8,128)(2,1)} %bitcast.11, bf16[128,4096]{1,0:T(8,128)(2,1)} %bitcast.15, ...), custom_call_target="tpu_custom_call" | custom-call | tf_op jit(solution)/shard_map/block_stats/pallas_call | solution.py:485
  12.8 0.1 collective-permute-start
  12.9 2.2 %collective-permute-done.got_ref = f32[6,256,128]{2,1,0:T(8,128)S(1)} collective-permute-done((f32[6,256,128]{2,1,0:T(8,128)S(1)}, f32[6,256,128]{2,1,0:T(8,128)S(1)}, u32[]{:S(2)}, u32[]{:S(2)}) %collective-permute-start) | collective-permute-done | bytes 786464 | tf_op jit(solution)/shard_map/ppermute | solution.py:507
  15.2 1.0 %chip_stats.1 = (f32[6,64,128]{2,1,0:T(8,128)S(1)}, f32[6,64,128]{2,1,0:T(8,128)S(1)}, f32[6,64,128]{2,1,0:T(8,128)S(1)}, f32[6,64,128]{2,1,0:T(8,128)S(1)}, f32[64,128]{1,0:T(8,128)S(1)}) custom-call(s32[1,8]{1,0:T(1,128)S(1)} %copy-done.5, f32[7,256,128]{2,1,0:T(8,128)S(1)} %bitcast.27, f32[6,256,128]{2,1,0:T(8,128)S(1)} %collective-permute-done.got_ref), custom_call_target="tpu_custom_call" | custom-call | tf_op jit(solution)/shard_map/chip_stats/pallas_call | solution.py:422
  16.1 2.4 %collective-permute-start.1 = (f32[6,64,128]{2,1,0:T(8,128)S(1)}, f32[6,64,128]{2,1,0:T(8,128)S(1)}, u32[]{:S(2)}, u32[]{:S(2)}) collective-permute-start(f32[6,64,128]{2,1,0:T(8,128)S(1)} %get-tuple-element.47), channel_id=1, source_target_pairs={{0,2},{1,3},{2,0},{3,1},{4,6},{5,7},{6,4},{7,5},{8,10},{9,11},{10,... | collective-permute-start | bytes 589832 | tf_op jit(solution)/shard_map/ppermute | solution.py:511
  18.5 1.2 %collective-permute-start.2 = (f32[6,64,128]{2,1,0:T(8,128)S(1)}, f32[6,64,128]{2,1,0:T(8,128)S(1)}, u32[]{:S(2)}, u32[]{:S(2)}) collective-permute-start(f32[6,64,128]{2,1,0:T(8,128)S(1)} %get-tuple-element.48), channel_id=1, source_target_pairs={{0,4},{1,5},{2,6},{3,7},{4,0},{5,1},{6,2},{7,3},{8,12},{9,13},{10,... | collective-permute-start | bytes 589832 | tf_op jit(solution)/shard_map/ppermute | solution.py:511
  19.8 8.8 %local_outputs.1 = (f32[4,128,8,128]{3,2,1,0:T(8,128)S(1)}, f32[4,128,8,128]{3,2,1,0:T(8,128)S(1)}, f32[1,128]{1,0:T(1,128)S(1)}) custom-call(bf16[128,4096]{1,0:T(8,128)(2,1)} %bitcast.12, bf16[128,4096]{1,0:T(8,128)(2,1)} %bitcast.16, bf16[128,4096]{1,0:T(8,128)(2,1)} %bitcast.20, bf16[128,4096]{1,0:T(8,128)(2,1)} %bitcast.24, ...), custom_call_target="tpu_custom_call" | custom-call | flops 10000000000 | bytes 20000000 | tf_op jit(solution)/shard_map/local_outputs/pallas_call | solution.py:523
  28.6 0.0 collective-permute-done.3.refs_3_
  28.7 0.7 %row_scan.1 = (f32[2,64,128]{2,1,0:T(8,128)S(1)}, f32[2,64,128]{2,1,0:T(8,128)S(1)}, f32[2,64,128]{2,1,0:T(8,128)S(1)}, f32[2,64,128]{2,1,0:T(8,128)S(1)}, f32[2,64,128]{2,1,0:T(8,128)S(1)}) custom-call(s32[1,8]{1,0:T(1,128)S(1)} %copy-done.5, f32[64,128]{1,0:T(8,128)S(1)} %get-tuple-element.43.after_ref.rate_ref, ...), custom_call_target="tpu_custom_call" | custom-call | tf_op jit(solution)/shard_map/row_scan/pallas_call | solution.py:422
  29.4 1.4 %collective-permute-start.4 = (f32[2,64,128]{2,1,0:T(8,128)S(1)}, f32[2,64,128]{2,1,0:T(8,128)S(1)}, u32[]{:S(2)}, u32[]{:S(2)}) collective-permute-start(f32[2,64,128]{2,1,0:T(8,128)S(1)} %get-tuple-element.52), channel_id=1, source_target_pairs={{0,2},{1,3},{2,0},{3,1},{4,6},{5,7},{6,4},{7,5},{8,10},{9,11},{10,... | collective-permute-start | bytes 196616 | tf_op jit(solution)/shard_map/ppermute | solution.py:511
  30.8 1.2 %collective-permute-start.5 = (f32[2,64,128]{2,1,0:T(8,128)S(1)}, f32[2,64,128]{2,1,0:T(8,128)S(1)}, u32[]{:S(2)}, u32[]{:S(2)}) collective-permute-start(f32[2,64,128]{2,1,0:T(8,128)S(1)} %get-tuple-element.53), channel_id=1, source_target_pairs={{0,4},{1,5},{2,6},{3,7},{4,0},{5,1},{6,2},{7,3},{8,12},{9,13},{10,... | collective-permute-start | bytes 196616 | tf_op jit(solution)/shard_map/ppermute | solution.py:511
  32.1 0.0 collective-permute-start.6
  32.1 3.5 %collective-permute-start.10 = (f32[2,64,128]{2,1,0:T(8,128)S(1)}, f32[2,64,128]{2,1,0:T(8,128)S(1)}, u32[]{:S(2)}, u32[]{:S(2)}) collective-permute-start(f32[2,64,128]{2,1,0:T(8,128)S(1)} %get-tuple-element.58), channel_id=1, source_target_pairs={{0,24},{8,16},{16,8},{24,0},{1,25},{9,17},{17,9},{25,1},{2,26},{10... | collective-permute-start | bytes 196616 | tf_op jit(solution)/shard_map/ppermute | solution.py:543
  35.6 0.3 collective-permute-start.8
  35.9 0.3 collective-permute-done.6.refs_3_
  36.2 3.4 %block_edges.1 = (f32[2,256,128]{2,1,0:T(8,128)S(1)}, f32[4,128,8,128]{3,2,1,0:T(8,128)S(1)}, f32[4,128,8,128]{3,2,1,0:T(8,128)S(1)}) custom-call(s32[1,8]{1,0:T(1,128)S(1)} %copy-done.5, f32[7,256,128]{2,1,0:T(8,128)S(1)} %bitcast.28, f32[6,256,128]{2,1,0:T(8,128)S(1)} %collective-permute-done.got_ref, ...), custom_call_target="tpu_custom_call", output_to_operand_aliasing={{1}: (5, {}), {2}: (6, {})} | custom-call | tf_op jit(solution)/shard_map/block_edges/pallas_call | solution.py:548
  39.6 2.9 %collective-permute-start.7 = (f32[2,256,128]{2,1,0:T(8,128)S(1)}, f32[2,256,128]{2,1,0:T(8,128)S(1)}, u32[]{:S(2)}, u32[]{:S(2)}) collective-permute-start(f32[2,256,128]{2,1,0:T(8,128)S(1)} %get-tuple-element.57), channel_id=1, source_target_pairs={{0,1},{1,0},{2,3},{3,2},{4,5},{5,4},{6,7},{7,6},{8,9},{9,8},{10,11... | collective-permute-start | bytes 786440 | tf_op jit(solution)/shard_map/ppermute | solution.py:507
  42.5 2.0 %collective-permute-start.13 = (f32[2,64,128]{2,1,0:T(8,128)S(1)}, f32[2,64,128]{2,1,0:T(8,128)S(1)}, u32[]{:S(2)}, u32[]{:S(2)}) collective-permute-start(f32[2,64,128]{2,1,0:T(8,128)S(1)} %add_add_fusion.after_ref.refs_0_), channel_id=1, source_target_pairs={{0,6},{1,7},{2,4},{3,5},{4,2},{5,3},{6,0},{7,1},{8,14},{9,15},{10,... | collective-permute-start | bytes 196616 | tf_op jit(solution)/shard_map/ppermute | solution.py:511
  44.5 0.2 collective-permute-start.12
  44.7 0.5 collective-permute-start.11
  45.3 4.1 %outputs.2 = (bf16[128,4096]{1,0:T(8,128)(2,1)}, bf16[128,4096]{1,0:T(8,128)(2,1)}, bf16[128,4096]{1,0:T(8,128)(2,1)}, bf16[128,4096]{1,0:T(8,128)(2,1)}, f32[1,128]{1,0:T(1,128)S(1)}) custom-call(bf16[128,4096]{1,0:T(8,128)(2,1)S(1)} %bitcast.13, bf16[128,4096]{1,0:T(8,128)(2,1)S(1)} %bitcast.17, bf16[128,4096]{1,0:T(8,128)(2,1)S(1)} %bitcast.21, ...), custom_call_target="tpu_custom_call" | custom-call | flops 300000000 | bytes 1500000 | tf_op jit(solution)/shard_map/outputs/pallas_call | solution.py:564
  49.4 1.5 %collective-permute-start.14 = (f32[2,256,128]{2,1,0:T(8,128)S(1)}, f32[2,256,128]{2,1,0:T(8,128)S(1)}, u32[]{:S(2)}, u32[]{:S(2)}) collective-permute-start(f32[2,256,128]{2,1,0:T(8,128)S(1)} %gather_sums.1.after_ref.kept_ref), channel_id=1, source_target_pairs={{0,1},{1,0},{2,3},{3,2},{4,5},{5,4},{6,7},{7,6},{8,9},{9,8},{10,11... | collective-permute-start | bytes 786440 | tf_op jit(solution)/shard_map/ppermute | solution.py:507
  50.9 1.9 %outputs.3 = (bf16[128,4096]{1,0:T(8,128)(2,1)}, bf16[128,4096]{1,0:T(8,128)(2,1)}, bf16[128,4096]{1,0:T(8,128)(2,1)}, bf16[128,4096]{1,0:T(8,128)(2,1)}, f32[1,128]{1,0:T(1,128)}) custom-call(bf16[128,4096]{1,0:T(8,128)(2,1)S(1)} %bitcast.14, ...), custom_call_target="tpu_custom_call", output_to_operand_aliasing={{0}: (10, {}), {1}: (11, {}), {2}: (12, {}), {3}: (13, {})} | custom-call | flops 100000000 | bytes 500000 | tf_op jit(solution)/shard_map/outputs/pallas_call | solution.py:564
  52.8 1.0 %parameter_grads.1 = (f32[16,4096]{1,0:T(8,128)}, f32[16,4096]{1,0:T(8,128)}) custom-call(f32[4,16,8,128]{3,2,1,0:T(8,128)S(1)} %get-tuple-element.38.rate_ref, f32[16,4096]{1,0:T(8,128)S(1)} %copy-done.4, f32[2,256,128]{2,1,0:T(8,128)S(1)} %gather_sums.1.after_ref.kept_ref, f32[2,256,128]{2,1,0:T(8,128)S(1)} %collective-permute-done.14.got_ref), custom_call_target="tpu_custom_call" | custom-call | tf_op jit(solution)/shard_map/parameter_grads/pallas_call | solution.py:422
  (28 shorter events, 0.1 us)
Async XLA Ops:
  0.6 14.5 %copy-start.5 = (s32[1,8]{1,0:T(1,128)S(1)}, s32[1,8]{1,0:T(1,128)}, u32[]{:S(2)}) copy-start(s32[1,8]{1,0:T(1,128)} %doc_ref.5) | copy-start | bytes 100
  12.8 2.4 %collective-permute-start = (f32[6,256,128]{2,1,0:T(8,128)S(1)}, f32[6,256,128]{2,1,0:T(8,128)S(1)}, u32[]{:S(2)}, u32[]{:S(2)}) collective-permute-start(f32[6,256,128]{2,1,0:T(8,128)S(1)} %bitcast.31), channel_id=1, source_target_pairs={{0,1},{1,0},{2,3},{3,2},{4,5},{5,4},{6,7},{7,6},{8,9},{9,8},{10,11... | collective-permute-start | bytes 2359304 | tf_op jit(solution)/shard_map/ppermute | solution.py:507
  16.1 12.5 %collective-permute-start.1 = (f32[6,64,128]{2,1,0:T(8,128)S(1)}, f32[6,64,128]{2,1,0:T(8,128)S(1)}, u32[]{:S(2)}, u32[]{:S(2)}) collective-permute-start(f32[6,64,128]{2,1,0:T(8,128)S(1)} %get-tuple-element.47), channel_id=1, source_target_pairs={{0,2},{1,3},{2,0},{3,1},{4,6},{5,7},{6,4},{7,5},{8,10},{9,11},{10,... | collective-permute-start | bytes 589832 | tf_op jit(solution)/shard_map/ppermute | solution.py:511
  18.5 10.1 %collective-permute-start.2 = (f32[6,64,128]{2,1,0:T(8,128)S(1)}, f32[6,64,128]{2,1,0:T(8,128)S(1)}, u32[]{:S(2)}, u32[]{:S(2)}) collective-permute-start(f32[6,64,128]{2,1,0:T(8,128)S(1)} %get-tuple-element.48), channel_id=1, source_target_pairs={{0,4},{1,5},{2,6},{3,7},{4,0},{5,1},{6,2},{7,3},{8,12},{9,13},{10,... | collective-permute-start | bytes 589832 | tf_op jit(solution)/shard_map/ppermute | solution.py:511
  19.8 8.9 %collective-permute-start.3 = (f32[6,64,128]{2,1,0:T(8,128)S(1)}, f32[6,64,128]{2,1,0:T(8,128)S(1)}, u32[]{:S(2)}, u32[]{:S(2)}) collective-permute-start(f32[6,64,128]{2,1,0:T(8,128)S(1)} %get-tuple-element.49), channel_id=1, source_target_pairs={{0,6},{1,7},{2,4},{3,5},{4,2},{5,3},{6,0},{7,1},{8,14},{9,15},{10,... | collective-permute-start | bytes 589832 | tf_op jit(solution)/shard_map/ppermute | solution.py:511
  19.8 16.4 %copy-start.4 = (f32[16,4096]{1,0:T(8,128)S(1)}, f32[16,4096]{1,0:T(8,128)}, u32[]{:S(2)}) copy-start(f32[16,4096]{1,0:T(8,128)} %residue_ref.9) | copy-start | bytes 786436
  29.4 6.2 %collective-permute-start.4 = (f32[2,64,128]{2,1,0:T(8,128)S(1)}, f32[2,64,128]{2,1,0:T(8,128)S(1)}, u32[]{:S(2)}, u32[]{:S(2)}) collective-permute-start(f32[2,64,128]{2,1,0:T(8,128)S(1)} %get-tuple-element.52), channel_id=1, source_target_pairs={{0,2},{1,3},{2,0},{3,1},{4,6},{5,7},{6,4},{7,5},{8,10},{9,11},{10,... | collective-permute-start | bytes 196616 | tf_op jit(solution)/shard_map/ppermute | solution.py:511
  30.8 5.1 %collective-permute-start.5 = (f32[2,64,128]{2,1,0:T(8,128)S(1)}, f32[2,64,128]{2,1,0:T(8,128)S(1)}, u32[]{:S(2)}, u32[]{:S(2)}) collective-permute-start(f32[2,64,128]{2,1,0:T(8,128)S(1)} %get-tuple-element.53), channel_id=1, source_target_pairs={{0,4},{1,5},{2,6},{3,7},{4,0},{5,1},{6,2},{7,3},{8,12},{9,13},{10,... | collective-permute-start | bytes 196616 | tf_op jit(solution)/shard_map/ppermute | solution.py:511
  32.1 4.1 %collective-permute-start.6 = (f32[2,64,128]{2,1,0:T(8,128)S(1)}, f32[2,64,128]{2,1,0:T(8,128)S(1)}, u32[]{:S(2)}, u32[]{:S(2)}) collective-permute-start(f32[2,64,128]{2,1,0:T(8,128)S(1)} %get-tuple-element.54), channel_id=1, source_target_pairs={{0,6},{1,7},{2,4},{3,5},{4,2},{5,3},{6,0},{7,1},{8,14},{9,15},{10,... | collective-permute-start | bytes 196616 | tf_op jit(solution)/shard_map/ppermute | solution.py:511
  32.1 10.4 %collective-permute-start.10 = (f32[2,64,128]{2,1,0:T(8,128)S(1)}, f32[2,64,128]{2,1,0:T(8,128)S(1)}, u32[]{:S(2)}, u32[]{:S(2)}) collective-permute-start(f32[2,64,128]{2,1,0:T(8,128)S(1)} %get-tuple-element.58), channel_id=1, source_target_pairs={{0,24},{8,16},{16,8},{24,0},{1,25},{9,17},{17,9},{25,1},{2,26},{10... | collective-permute-start | bytes 196616 | tf_op jit(solution)/shard_map/ppermute | solution.py:543
  35.6 6.9 %collective-permute-start.9 = (f32[2,64,128]{2,1,0:T(8,128)S(1)}, f32[2,64,128]{2,1,0:T(8,128)S(1)}, u32[]{:S(2)}, u32[]{:S(2)}) collective-permute-start(f32[2,64,128]{2,1,0:T(8,128)S(1)} %get-tuple-element.58), channel_id=1, source_target_pairs={{0,16},{8,24},{16,0},{24,8},{1,17},{9,25},{17,1},{25,9},{2,18},{10... | collective-permute-start | bytes 196616 | tf_op jit(solution)/shard_map/ppermute | solution.py:543
  35.6 6.9 %collective-permute-start.8 = (f32[2,64,128]{2,1,0:T(8,128)S(1)}, f32[2,64,128]{2,1,0:T(8,128)S(1)}, u32[]{:S(2)}, u32[]{:S(2)}) collective-permute-start(f32[2,64,128]{2,1,0:T(8,128)S(1)} %get-tuple-element.58), channel_id=1, source_target_pairs={{0,8},{8,0},{16,24},{24,16},{1,9},{9,1},{17,25},{25,17},{2,10},{10... | collective-permute-start | bytes 196616 | tf_op jit(solution)/shard_map/ppermute | solution.py:543
  36.2 9.0 %copy-start = (bf16[1,128,4096]{2,1,0:T(8,128)(2,1)S(1)}, bf16[1,128,4096]{2,1,0:T(8,128)(2,1)}, u32[]{:S(2)}) copy-start(bf16[1,128,4096]{2,1,0:T(8,128)(2,1)} %param.8) | copy-start | bytes 3145732
  36.2 9.0 %copy-start.1 = (bf16[1,128,4096]{2,1,0:T(8,128)(2,1)S(1)}, bf16[1,128,4096]{2,1,0:T(8,128)(2,1)}, u32[]{:S(2)}) copy-start(bf16[1,128,4096]{2,1,0:T(8,128)(2,1)} %param.9) | copy-start | bytes 3145732
  36.2 9.0 %copy-start.2 = (bf16[1,128,4096]{2,1,0:T(8,128)(2,1)S(1)}, bf16[1,128,4096]{2,1,0:T(8,128)(2,1)}, u32[]{:S(2)}) copy-start(bf16[1,128,4096]{2,1,0:T(8,128)(2,1)} %param.7) | copy-start | bytes 3145732
  36.2 9.1 %copy-start.3 = (bf16[1,128,4096]{2,1,0:T(8,128)(2,1)S(1)}, bf16[1,128,4096]{2,1,0:T(8,128)(2,1)}, u32[]{:S(2)}) copy-start(bf16[1,128,4096]{2,1,0:T(8,128)(2,1)} %param.10) | copy-start | bytes 3145732
  39.6 5.6 %collective-permute-start.7 = (f32[2,256,128]{2,1,0:T(8,128)S(1)}, f32[2,256,128]{2,1,0:T(8,128)S(1)}, u32[]{:S(2)}, u32[]{:S(2)}) collective-permute-start(f32[2,256,128]{2,1,0:T(8,128)S(1)} %get-tuple-element.57), channel_id=1, source_target_pairs={{0,1},{1,0},{2,3},{3,2},{4,5},{5,4},{6,7},{7,6},{8,9},{9,8},{10,11... | collective-permute-start | bytes 786440 | tf_op jit(solution)/shard_map/ppermute | solution.py:507
  42.5 6.8 %collective-permute-start.13 = (f32[2,64,128]{2,1,0:T(8,128)S(1)}, f32[2,64,128]{2,1,0:T(8,128)S(1)}, u32[]{:S(2)}, u32[]{:S(2)}) collective-permute-start(f32[2,64,128]{2,1,0:T(8,128)S(1)} %add_add_fusion.after_ref.refs_0_), channel_id=1, source_target_pairs={{0,6},{1,7},{2,4},{3,5},{4,2},{5,3},{6,0},{7,1},{8,14},{9,15},{10,... | collective-permute-start | bytes 196616 | tf_op jit(solution)/shard_map/ppermute | solution.py:511
  44.5 4.8 %collective-permute-start.12 = (f32[2,64,128]{2,1,0:T(8,128)S(1)}, f32[2,64,128]{2,1,0:T(8,128)S(1)}, u32[]{:S(2)}, u32[]{:S(2)}) collective-permute-start(f32[2,64,128]{2,1,0:T(8,128)S(1)} %add_add_fusion.after_ref.refs_0_), channel_id=1, source_target_pairs={{0,4},{1,5},{2,6},{3,7},{4,0},{5,1},{6,2},{7,3},{8,12},{9,13},{10,... | collective-permute-start | bytes 196616 | tf_op jit(solution)/shard_map/ppermute | solution.py:511
  44.7 4.6 %collective-permute-start.11 = (f32[2,64,128]{2,1,0:T(8,128)S(1)}, f32[2,64,128]{2,1,0:T(8,128)S(1)}, u32[]{:S(2)}, u32[]{:S(2)}) collective-permute-start(f32[2,64,128]{2,1,0:T(8,128)S(1)} %add_add_fusion.after_ref.refs_0_), channel_id=1, source_target_pairs={{0,2},{1,3},{2,0},{3,1},{4,6},{5,7},{6,4},{7,5},{8,10},{9,11},{10,... | collective-permute-start | bytes 196616 | tf_op jit(solution)/shard_map/ppermute | solution.py:511
  49.4 3.4 %collective-permute-start.14 = (f32[2,256,128]{2,1,0:T(8,128)S(1)}, f32[2,256,128]{2,1,0:T(8,128)S(1)}, u32[]{:S(2)}, u32[]{:S(2)}) collective-permute-start(f32[2,256,128]{2,1,0:T(8,128)S(1)} %gather_sums.1.after_ref.kept_ref), channel_id=1, source_target_pairs={{0,1},{1,0},{2,3},{3,2},{4,5},{5,4},{6,7},{7,6},{8,9},{9,8},{10,11... | collective-permute-start | bytes 786440 | tf_op jit(solution)/shard_map/ppermute | solution.py:507

commit v6 on v5

--- a/solution.py
+++ b/solution.py
@@ -269,27 +269,27 @@
 
 
 def merge_kernel(block, chips, doc_ref, kept_ref, got_ref, *refs):
-    outs, part_ref, chip_ref = refs[:chips], refs[chips], refs[chips + 1]
+    outs, part_ref = refs[:chips], refs[chips]
     core, chip = chip_of()
     first = core == 0
     half = kept_ref.shape[1]
     part = half // chips
     joined = joined_in(doc_ref, chip)
-    rate = kept_ref[6]
     part_ref[...] = kept_ref[6, pl.ds(pl.multiple_of(chip * part, part), part), :]
-    hop = joined * jnp.exp(-block * rate)
-    link = joined * jnp.exp(-rate)
-    left = [jnp.where(first, kept_ref[i], got_ref[i]) for i in range(6)]
-    right = [jnp.where(first, got_ref[i], kept_ref[i]) for i in range(6)]
-    chip_ref[0] = right[0] + hop * left[0]
-    chip_ref[1] = right[1] + hop * (left[1] + block * left[0])
-    chip_ref[2] = left[2] + hop * right[2]
-    chip_ref[3] = left[3] + hop * (right[3] + block * right[2])
-    chip_ref[4] = left[4] + right[4] + link * (right[2] * left[0])
-    chip_ref[5] = left[5] + right[5] + link * ((right[3] + right[2]) * left[0] + right[2] * left[1])
     for away in range(chips):
-        start = pl.multiple_of((chip ^ away) * part, part)
-        outs[away][...] = chip_ref[:, pl.ds(start, part), :]
+        rows = pl.ds(pl.multiple_of((chip ^ away) * part, part), part)
+        out = outs[away]
+        rate = kept_ref[6, rows, :]
+        hop = joined * jnp.exp(-block * rate)
+        link = joined * jnp.exp(-rate)
+        left = [jnp.where(first, kept_ref[i, rows, :], got_ref[i, rows, :]) for i in range(6)]
+        right = [jnp.where(first, got_ref[i, rows, :], kept_ref[i, rows, :]) for i in range(6)]
+        out[0] = right[0] + hop * left[0]
+        out[1] = right[1] + hop * (left[1] + block * left[0])
+        out[2] = left[2] + hop * right[2]
+        out[3] = left[3] + hop * (right[3] + block * right[2])
+        out[4] = left[4] + right[4] + link * (right[2] * left[0])
+        out[5] = left[5] + right[5] + link * ((right[3] + right[2]) * left[0] + right[2] * left[1])
 
 
 def scan_kernel(block, chips, doc_ref, rate_ref, *refs):
@@ -517,7 +517,7 @@
         "chip_stats",
         [group_doc, kept, got],
         [f32(6, part, LANES)] * chips + [f32(part, LANES)],
-        [pltpu.VMEM((6, half, LANES), F32)],
+        [],
     )
     columns = pl.BlockSpec((1, block, SUBS, LANES), lambda i: (i, 0, 0, 0))
     z_local, w_local, zeros = pl.pallas_call(

time: 54 us -> 53.7 us (level)
  no operation moved by 1% of the time
where the time goes in v6:
time: 53.7 us; the launch traced here: 53.6 us
  Pallas kernels  32.8 us (61%)
  starting transfers between devices  17.4 us (32%)
  waiting for transfers between devices  2.6 us (5%)
  between operations  0.77 us (1%)
    pallas_call x1, Pallas kernels, body(): pl.pallas_call(partial(stats_kernel, float(row_len)), grid=(groups,), in_...  12.2 us
    ppermute x9, starting transfers between devices, swap_chips(): lax.ppermute(xs[away], 'ctx', [(i, i ^ 2 * away) for i in range(n_ctx)])  9.09 us
    pallas_call x1, Pallas kernels, body(): pl.pallas_call(local_kernel, grid=(groups,), in_specs=[wide] * 4 + [slim,...  8.8 us
    pallas_call x2, Pallas kernels, outputs(): pl.pallas_call(partial(output_kernel, len(outs)), grid=(count,), in_specs...  5.91 us
    ppermute x3, starting transfers between devices, swap_core(): return lax.ppermute(x, 'ctx', [(i, i ^ 1) for i in range(n_ctx)])  4.53 us
    ppermute x3, starting transfers between devices, body(): lax.ppermute(total, 'dp', [(i, i ^ away) for i in range(n_dp)])  3.77 us
    pallas_call x1, Pallas kernels, body(): pl.pallas_call(partial(expand_kernel, float(block), chips), in_specs=[sca...  3.38 us
    pallas_call x4, Pallas kernels, small_call(): pl.pallas_call(kernel, grid=(1,), in_specs=[scalar_spec() if x.dtype == j...  2.52 us
  transfers between devices with their start and end apart: 15, of which 2 were waited for; matrix products, arithmetic and copies ran while one was open for 0% of the time, Pallas kernels for 34%

profile of v6, /device:TPU:1, one launch (start us, length us, event | category | flops | bytes accessed | tf_op | source)
XLA Modules:
  0.0 53.6 jit_solution(8795626209766668160)
XLA Ops:
  0.6 12.2 %block_stats.1 = (f32[4,16,16,8,128]{4,3,2,1,0:T(8,128)S(1)}, f32[4,16,16,8,128]{4,3,2,1,0:T(8,128)S(1)}, f32[4,16,8,128]{3,2,1,0:T(8,128)S(1)}, f32[7,4,8,8,128...) custom-call(bf16[128,4096]{1,0:T(8,128)(2,1)} %bitcast.11, bf16[128,4096]{1,0:T(8,128)(2,1)} %bitcast.15, ...), custom_call_target="tpu_custom_call" | custom-call | tf_op jit(solution)/shard_map/block_stats/pallas_call | solution.py:485
  12.8 0.1 collective-permute-start
  12.9 2.2 %collective-permute-done.got_ref = f32[6,256,128]{2,1,0:T(8,128)S(1)} collective-permute-done((f32[6,256,128]{2,1,0:T(8,128)S(1)}, f32[6,256,128]{2,1,0:T(8,128)S(1)}, u32[]{:S(2)}, u32[]{:S(2)}) %collective-permute-start) | collective-permute-done | bytes 786464 | tf_op jit(solution)/shard_map/ppermute | solution.py:507
  15.2 0.7 %chip_stats.1 = (f32[6,64,128]{2,1,0:T(8,128)S(1)}, f32[6,64,128]{2,1,0:T(8,128)S(1)}, f32[6,64,128]{2,1,0:T(8,128)S(1)}, f32[6,64,128]{2,1,0:T(8,128)S(1)}, f32[64,128]{1,0:T(8,128)S(1)}) custom-call(s32[1,8]{1,0:T(1,128)S(1)} %copy-done.5, f32[7,256,128]{2,1,0:T(8,128)S(1)} %bitcast.27, f32[6,256,128]{2,1,0:T(8,128)S(1)} %collective-permute-done.got_ref), custom_call_target="tpu_custom_call" | custom-call | tf_op jit(solution)/shard_map/chip_stats/pallas_call | solution.py:422
  15.9 2.4 %collective-permute-start.1 = (f32[6,64,128]{2,1,0:T(8,128)S(1)}, f32[6,64,128]{2,1,0:T(8,128)S(1)}, u32[]{:S(2)}, u32[]{:S(2)}) collective-permute-start(f32[6,64,128]{2,1,0:T(8,128)S(1)} %get-tuple-element.47), channel_id=1, source_target_pairs={{0,2},{1,3},{2,0},{3,1},{4,6},{5,7},{6,4},{7,5},{8,10},{9,11},{10,... | collective-permute-start | bytes 589832 | tf_op jit(solution)/shard_map/ppermute | solution.py:511
  18.3 1.2 %collective-permute-start.2 = (f32[6,64,128]{2,1,0:T(8,128)S(1)}, f32[6,64,128]{2,1,0:T(8,128)S(1)}, u32[]{:S(2)}, u32[]{:S(2)}) collective-permute-start(f32[6,64,128]{2,1,0:T(8,128)S(1)} %get-tuple-element.48), channel_id=1, source_target_pairs={{0,4},{1,5},{2,6},{3,7},{4,0},{5,1},{6,2},{7,3},{8,12},{9,13},{10,... | collective-permute-start | bytes 589832 | tf_op jit(solution)/shard_map/ppermute | solution.py:511
  19.6 8.8 %local_outputs.1 = (f32[4,128,8,128]{3,2,1,0:T(8,128)S(1)}, f32[4,128,8,128]{3,2,1,0:T(8,128)S(1)}, f32[1,128]{1,0:T(1,128)S(1)}) custom-call(bf16[128,4096]{1,0:T(8,128)(2,1)} %bitcast.12, bf16[128,4096]{1,0:T(8,128)(2,1)} %bitcast.16, bf16[128,4096]{1,0:T(8,128)(2,1)} %bitcast.20, bf16[128,4096]{1,0:T(8,128)(2,1)} %bitcast.24, ...), custom_call_target="tpu_custom_call" | custom-call | flops 10000000000 | bytes 20000000 | tf_op jit(solution)/shard_map/local_outputs/pallas_call | solution.py:523
  28.4 0.0 collective-permute-done.3.refs_3_
  28.4 0.7 %row_scan.1 = (f32[2,64,128]{2,1,0:T(8,128)S(1)}, f32[2,64,128]{2,1,0:T(8,128)S(1)}, f32[2,64,128]{2,1,0:T(8,128)S(1)}, f32[2,64,128]{2,1,0:T(8,128)S(1)}, f32[2,64,128]{2,1,0:T(8,128)S(1)}) custom-call(s32[1,8]{1,0:T(1,128)S(1)} %copy-done.5, f32[64,128]{1,0:T(8,128)S(1)} %get-tuple-element.43.after_ref.rate_ref, ...), custom_call_target="tpu_custom_call" | custom-call | tf_op jit(solution)/shard_map/row_scan/pallas_call | solution.py:422
  29.2 1.4 %collective-permute-start.4 = (f32[2,64,128]{2,1,0:T(8,128)S(1)}, f32[2,64,128]{2,1,0:T(8,128)S(1)}, u32[]{:S(2)}, u32[]{:S(2)}) collective-permute-start(f32[2,64,128]{2,1,0:T(8,128)S(1)} %get-tuple-element.52), channel_id=1, source_target_pairs={{0,2},{1,3},{2,0},{3,1},{4,6},{5,7},{6,4},{7,5},{8,10},{9,11},{10,... | collective-permute-start | bytes 196616 | tf_op jit(solution)/shard_map/ppermute | solution.py:511
  30.6 1.2 %collective-permute-start.5 = (f32[2,64,128]{2,1,0:T(8,128)S(1)}, f32[2,64,128]{2,1,0:T(8,128)S(1)}, u32[]{:S(2)}, u32[]{:S(2)}) collective-permute-start(f32[2,64,128]{2,1,0:T(8,128)S(1)} %get-tuple-element.53), channel_id=1, source_target_pairs={{0,4},{1,5},{2,6},{3,7},{4,0},{5,1},{6,2},{7,3},{8,12},{9,13},{10,... | collective-permute-start | bytes 196616 | tf_op jit(solution)/shard_map/ppermute | solution.py:511
  31.9 0.0 collective-permute-start.6
  31.9 3.5 %collective-permute-start.10 = (f32[2,64,128]{2,1,0:T(8,128)S(1)}, f32[2,64,128]{2,1,0:T(8,128)S(1)}, u32[]{:S(2)}, u32[]{:S(2)}) collective-permute-start(f32[2,64,128]{2,1,0:T(8,128)S(1)} %get-tuple-element.58), channel_id=1, source_target_pairs={{0,24},{8,16},{16,8},{24,0},{1,25},{9,17},{17,9},{25,1},{2,26},{10... | collective-permute-start | bytes 196616 | tf_op jit(solution)/shard_map/ppermute | solution.py:543
  35.4 0.3 collective-permute-start.8
  35.7 0.3 collective-permute-done.6.refs_3_
  36.0 3.4 %block_edges.1 = (f32[2,256,128]{2,1,0:T(8,128)S(1)}, f32[4,128,8,128]{3,2,1,0:T(8,128)S(1)}, f32[4,128,8,128]{3,2,1,0:T(8,128)S(1)}) custom-call(s32[1,8]{1,0:T(1,128)S(1)} %copy-done.5, f32[7,256,128]{2,1,0:T(8,128)S(1)} %bitcast.28, f32[6,256,128]{2,1,0:T(8,128)S(1)} %collective-permute-done.got_ref, ...), custom_call_target="tpu_custom_call", output_to_operand_aliasing={{1}: (5, {}), {2}: (6, {})} | custom-call | tf_op jit(solution)/shard_map/block_edges/pallas_call | solution.py:548
  39.4 2.9 %collective-permute-start.7 = (f32[2,256,128]{2,1,0:T(8,128)S(1)}, f32[2,256,128]{2,1,0:T(8,128)S(1)}, u32[]{:S(2)}, u32[]{:S(2)}) collective-permute-start(f32[2,256,128]{2,1,0:T(8,128)S(1)} %get-tuple-element.57), channel_id=1, source_target_pairs={{0,1},{1,0},{2,3},{3,2},{4,5},{5,4},{6,7},{7,6},{8,9},{9,8},{10,11... | collective-permute-start | bytes 786440 | tf_op jit(solution)/shard_map/ppermute | solution.py:507
  42.3 2.0 %collective-permute-start.13 = (f32[2,64,128]{2,1,0:T(8,128)S(1)}, f32[2,64,128]{2,1,0:T(8,128)S(1)}, u32[]{:S(2)}, u32[]{:S(2)}) collective-permute-start(f32[2,64,128]{2,1,0:T(8,128)S(1)} %add_add_fusion.after_ref.refs_0_), channel_id=1, source_target_pairs={{0,6},{1,7},{2,4},{3,5},{4,2},{5,3},{6,0},{7,1},{8,14},{9,15},{10,... | collective-permute-start | bytes 196616 | tf_op jit(solution)/shard_map/ppermute | solution.py:511
  44.3 0.2 collective-permute-start.12
  44.5 0.5 collective-permute-start.11
  45.1 4.1 %outputs.2 = (bf16[128,4096]{1,0:T(8,128)(2,1)}, bf16[128,4096]{1,0:T(8,128)(2,1)}, bf16[128,4096]{1,0:T(8,128)(2,1)}, bf16[128,4096]{1,0:T(8,128)(2,1)}, f32[1,128]{1,0:T(1,128)S(1)}) custom-call(bf16[128,4096]{1,0:T(8,128)(2,1)S(1)} %bitcast.13, bf16[128,4096]{1,0:T(8,128)(2,1)S(1)} %bitcast.17, bf16[128,4096]{1,0:T(8,128)(2,1)S(1)} %bitcast.21, ...), custom_call_target="tpu_custom_call" | custom-call | flops 300000000 | bytes 1500000 | tf_op jit(solution)/shard_map/outputs/pallas_call | solution.py:564
  49.2 1.5 %collective-permute-start.14 = (f32[2,256,128]{2,1,0:T(8,128)S(1)}, f32[2,256,128]{2,1,0:T(8,128)S(1)}, u32[]{:S(2)}, u32[]{:S(2)}) collective-permute-start(f32[2,256,128]{2,1,0:T(8,128)S(1)} %gather_sums.1.after_ref.kept_ref), channel_id=1, source_target_pairs={{0,1},{1,0},{2,3},{3,2},{4,5},{5,4},{6,7},{7,6},{8,9},{9,8},{10,11... | collective-permute-start | bytes 786440 | tf_op jit(solution)/shard_map/ppermute | solution.py:507
  50.7 1.9 %outputs.3 = (bf16[128,4096]{1,0:T(8,128)(2,1)}, bf16[128,4096]{1,0:T(8,128)(2,1)}, bf16[128,4096]{1,0:T(8,128)(2,1)}, bf16[128,4096]{1,0:T(8,128)(2,1)}, f32[1,128]{1,0:T(1,128)}) custom-call(bf16[128,4096]{1,0:T(8,128)(2,1)S(1)} %bitcast.14, ...), custom_call_target="tpu_custom_call", output_to_operand_aliasing={{0}: (10, {}), {1}: (11, {}), {2}: (12, {}), {3}: (13, {})} | custom-call | flops 100000000 | bytes 500000 | tf_op jit(solution)/shard_map/outputs/pallas_call | solution.py:564
  52.6 1.0 %parameter_grads.1 = (f32[16,4096]{1,0:T(8,128)}, f32[16,4096]{1,0:T(8,128)}) custom-call(f32[4,16,8,128]{3,2,1,0:T(8,128)S(1)} %get-tuple-element.38.rate_ref, f32[16,4096]{1,0:T(8,128)S(1)} %copy-done.4, f32[2,256,128]{2,1,0:T(8,128)S(1)} %gather_sums.1.after_ref.kept_ref, f32[2,256,128]{2,1,0:T(8,128)S(1)} %collective-permute-done.14.got_ref), custom_call_target="tpu_custom_call" | custom-call | tf_op jit(solution)/shard_map/parameter_grads/pallas_call | solution.py:422
  (28 shorter events, 0.1 us)
Async XLA Ops:
  0.6 14.5 %copy-start.5 = (s32[1,8]{1,0:T(1,128)S(1)}, s32[1,8]{1,0:T(1,128)}, u32[]{:S(2)}) copy-start(s32[1,8]{1,0:T(1,128)} %doc_ref.5) | copy-start | bytes 100
  12.8 2.4 %collective-permute-start = (f32[6,256,128]{2,1,0:T(8,128)S(1)}, f32[6,256,128]{2,1,0:T(8,128)S(1)}, u32[]{:S(2)}, u32[]{:S(2)}) collective-permute-start(f32[6,256,128]{2,1,0:T(8,128)S(1)} %bitcast.31), channel_id=1, source_target_pairs={{0,1},{1,0},{2,3},{3,2},{4,5},{5,4},{6,7},{7,6},{8,9},{9,8},{10,11... | collective-permute-start | bytes 2359304 | tf_op jit(solution)/shard_map/ppermute | solution.py:507
  15.9 12.5 %collective-permute-start.1 = (f32[6,64,128]{2,1,0:T(8,128)S(1)}, f32[6,64,128]{2,1,0:T(8,128)S(1)}, u32[]{:S(2)}, u32[]{:S(2)}) collective-permute-start(f32[6,64,128]{2,1,0:T(8,128)S(1)} %get-tuple-element.47), channel_id=1, source_target_pairs={{0,2},{1,3},{2,0},{3,1},{4,6},{5,7},{6,4},{7,5},{8,10},{9,11},{10,... | collective-permute-start | bytes 589832 | tf_op jit(solution)/shard_map/ppermute | solution.py:511
  18.3 10.1 %collective-permute-start.2 = (f32[6,64,128]{2,1,0:T(8,128)S(1)}, f32[6,64,128]{2,1,0:T(8,128)S(1)}, u32[]{:S(2)}, u32[]{:S(2)}) collective-permute-start(f32[6,64,128]{2,1,0:T(8,128)S(1)} %get-tuple-element.48), channel_id=1, source_target_pairs={{0,4},{1,5},{2,6},{3,7},{4,0},{5,1},{6,2},{7,3},{8,12},{9,13},{10,... | collective-permute-start | bytes 589832 | tf_op jit(solution)/shard_map/ppermute | solution.py:511
  19.6 8.9 %collective-permute-start.3 = (f32[6,64,128]{2,1,0:T(8,128)S(1)}, f32[6,64,128]{2,1,0:T(8,128)S(1)}, u32[]{:S(2)}, u32[]{:S(2)}) collective-permute-start(f32[6,64,128]{2,1,0:T(8,128)S(1)} %get-tuple-element.49), channel_id=1, source_target_pairs={{0,6},{1,7},{2,4},{3,5},{4,2},{5,3},{6,0},{7,1},{8,14},{9,15},{10,... | collective-permute-start | bytes 589832 | tf_op jit(solution)/shard_map/ppermute | solution.py:511
  19.6 16.4 %copy-start.4 = (f32[16,4096]{1,0:T(8,128)S(1)}, f32[16,4096]{1,0:T(8,128)}, u32[]{:S(2)}) copy-start(f32[16,4096]{1,0:T(8,128)} %residue_ref.9) | copy-start | bytes 786436
  29.2 6.2 %collective-permute-start.4 = (f32[2,64,128]{2,1,0:T(8,128)S(1)}, f32[2,64,128]{2,1,0:T(8,128)S(1)}, u32[]{:S(2)}, u32[]{:S(2)}) collective-permute-start(f32[2,64,128]{2,1,0:T(8,128)S(1)} %get-tuple-element.52), channel_id=1, source_target_pairs={{0,2},{1,3},{2,0},{3,1},{4,6},{5,7},{6,4},{7,5},{8,10},{9,11},{10,... | collective-permute-start | bytes 196616 | tf_op jit(solution)/shard_map/ppermute | solution.py:511
  30.6 5.1 %collective-permute-start.5 = (f32[2,64,128]{2,1,0:T(8,128)S(1)}, f32[2,64,128]{2,1,0:T(8,128)S(1)}, u32[]{:S(2)}, u32[]{:S(2)}) collective-permute-start(f32[2,64,128]{2,1,0:T(8,128)S(1)} %get-tuple-element.53), channel_id=1, source_target_pairs={{0,4},{1,5},{2,6},{3,7},{4,0},{5,1},{6,2},{7,3},{8,12},{9,13},{10,... | collective-permute-start | bytes 196616 | tf_op jit(solution)/shard_map/ppermute | solution.py:511
  31.9 4.1 %collective-permute-start.6 = (f32[2,64,128]{2,1,0:T(8,128)S(1)}, f32[2,64,128]{2,1,0:T(8,128)S(1)}, u32[]{:S(2)}, u32[]{:S(2)}) collective-permute-start(f32[2,64,128]{2,1,0:T(8,128)S(1)} %get-tuple-element.54), channel_id=1, source_target_pairs={{0,6},{1,7},{2,4},{3,5},{4,2},{5,3},{6,0},{7,1},{8,14},{9,15},{10,... | collective-permute-start | bytes 196616 | tf_op jit(solution)/shard_map/ppermute | solution.py:511
  31.9 10.4 %collective-permute-start.10 = (f32[2,64,128]{2,1,0:T(8,128)S(1)}, f32[2,64,128]{2,1,0:T(8,128)S(1)}, u32[]{:S(2)}, u32[]{:S(2)}) collective-permute-start(f32[2,64,128]{2,1,0:T(8,128)S(1)} %get-tuple-element.58), channel_id=1, source_target_pairs={{0,24},{8,16},{16,8},{24,0},{1,25},{9,17},{17,9},{25,1},{2,26},{10... | collective-permute-start | bytes 196616 | tf_op jit(solution)/shard_map/ppermute | solution.py:543
  35.4 6.9 %collective-permute-start.9 = (f32[2,64,128]{2,1,0:T(8,128)S(1)}, f32[2,64,128]{2,1,0:T(8,128)S(1)}, u32[]{:S(2)}, u32[]{:S(2)}) collective-permute-start(f32[2,64,128]{2,1,0:T(8,128)S(1)} %get-tuple-element.58), channel_id=1, source_target_pairs={{0,16},{8,24},{16,0},{24,8},{1,17},{9,25},{17,1},{25,9},{2,18},{10... | collective-permute-start | bytes 196616 | tf_op jit(solution)/shard_map/ppermute | solution.py:543
  35.4 6.9 %collective-permute-start.8 = (f32[2,64,128]{2,1,0:T(8,128)S(1)}, f32[2,64,128]{2,1,0:T(8,128)S(1)}, u32[]{:S(2)}, u32[]{:S(2)}) collective-permute-start(f32[2,64,128]{2,1,0:T(8,128)S(1)} %get-tuple-element.58), channel_id=1, source_target_pairs={{0,8},{8,0},{16,24},{24,16},{1,9},{9,1},{17,25},{25,17},{2,10},{10... | collective-permute-start | bytes 196616 | tf_op jit(solution)/shard_map/ppermute | solution.py:543
  36.0 9.0 %copy-start = (bf16[1,128,4096]{2,1,0:T(8,128)(2,1)S(1)}, bf16[1,128,4096]{2,1,0:T(8,128)(2,1)}, u32[]{:S(2)}) copy-start(bf16[1,128,4096]{2,1,0:T(8,128)(2,1)} %param.8) | copy-start | bytes 3145732
  36.0 9.0 %copy-start.1 = (bf16[1,128,4096]{2,1,0:T(8,128)(2,1)S(1)}, bf16[1,128,4096]{2,1,0:T(8,128)(2,1)}, u32[]{:S(2)}) copy-start(bf16[1,128,4096]{2,1,0:T(8,128)(2,1)} %param.9) | copy-start | bytes 3145732
  36.0 9.0 %copy-start.2 = (bf16[1,128,4096]{2,1,0:T(8,128)(2,1)S(1)}, bf16[1,128,4096]{2,1,0:T(8,128)(2,1)}, u32[]{:S(2)}) copy-start(bf16[1,128,4096]{2,1,0:T(8,128)(2,1)} %param.7) | copy-start | bytes 3145732
  36.0 9.1 %copy-start.3 = (bf16[1,128,4096]{2,1,0:T(8,128)(2,1)S(1)}, bf16[1,128,4096]{2,1,0:T(8,128)(2,1)}, u32[]{:S(2)}) copy-start(bf16[1,128,4096]{2,1,0:T(8,128)(2,1)} %param.10) | copy-start | bytes 3145732
  39.4 5.6 %collective-permute-start.7 = (f32[2,256,128]{2,1,0:T(8,128)S(1)}, f32[2,256,128]{2,1,0:T(8,128)S(1)}, u32[]{:S(2)}, u32[]{:S(2)}) collective-permute-start(f32[2,256,128]{2,1,0:T(8,128)S(1)} %get-tuple-element.57), channel_id=1, source_target_pairs={{0,1},{1,0},{2,3},{3,2},{4,5},{5,4},{6,7},{7,6},{8,9},{9,8},{10,11... | collective-permute-start | bytes 786440 | tf_op jit(solution)/shard_map/ppermute | solution.py:507
  42.3 6.8 %collective-permute-start.13 = (f32[2,64,128]{2,1,0:T(8,128)S(1)}, f32[2,64,128]{2,1,0:T(8,128)S(1)}, u32[]{:S(2)}, u32[]{:S(2)}) collective-permute-start(f32[2,64,128]{2,1,0:T(8,128)S(1)} %add_add_fusion.after_ref.refs_0_), channel_id=1, source_target_pairs={{0,6},{1,7},{2,4},{3,5},{4,2},{5,3},{6,0},{7,1},{8,14},{9,15},{10,... | collective-permute-start | bytes 196616 | tf_op jit(solution)/shard_map/ppermute | solution.py:511
  44.3 4.8 %collective-permute-start.12 = (f32[2,64,128]{2,1,0:T(8,128)S(1)}, f32[2,64,128]{2,1,0:T(8,128)S(1)}, u32[]{:S(2)}, u32[]{:S(2)}) collective-permute-start(f32[2,64,128]{2,1,0:T(8,128)S(1)} %add_add_fusion.after_ref.refs_0_), channel_id=1, source_target_pairs={{0,4},{1,5},{2,6},{3,7},{4,0},{5,1},{6,2},{7,3},{8,12},{9,13},{10,... | collective-permute-start | bytes 196616 | tf_op jit(solution)/shard_map/ppermute | solution.py:511
  44.5 4.6 %collective-permute-start.11 = (f32[2,64,128]{2,1,0:T(8,128)S(1)}, f32[2,64,128]{2,1,0:T(8,128)S(1)}, u32[]{:S(2)}, u32[]{:S(2)}) collective-permute-start(f32[2,64,128]{2,1,0:T(8,128)S(1)} %add_add_fusion.after_ref.refs_0_), channel_id=1, source_target_pairs={{0,2},{1,3},{2,0},{3,1},{4,6},{5,7},{6,4},{7,5},{8,10},{9,11},{10,... | collective-permute-start | bytes 196616 | tf_op jit(solution)/shard_map/ppermute | solution.py:511
  49.2 3.4 %collective-permute-start.14 = (f32[2,256,128]{2,1,0:T(8,128)S(1)}, f32[2,256,128]{2,1,0:T(8,128)S(1)}, u32[]{:S(2)}, u32[]{:S(2)}) collective-permute-start(f32[2,256,128]{2,1,0:T(8,128)S(1)} %gather_sums.1.after_ref.kept_ref), channel_id=1, source_target_pairs={{0,1},{1,0},{2,3},{3,2},{4,5},{5,4},{6,7},{7,6},{8,9},{9,8},{10,11... | collective-permute-start | bytes 786440 | tf_op jit(solution)/shard_map/ppermute | solution.py:507
